TPU v7x, 32 devices: a whole 2x2x4 slice. The times are simulated.
32 devices in a mesh: seq: 16 (over z, x, core), row: 2 (over y).
Axes of the slice: x: 2, y: 2, z: 4, core: 2. Of those that a mesh axis runs over, the one named last changes fastest.
Arguments:
- inputs: bfloat16 [2, 2048, 768], P('row', 'seq'), may hold values from -6 to 6
- cotangent: bfloat16 [2, 2048, 768], P('row', 'seq'), may hold values from -6 to 6
- clip_lengths: int32 [2, 6], P('row'), may hold values from 1 to 2043, as said below
- query_weight: bfloat16 [768, 768], replicated, may hold values from -0.21875 to 0.21875
- query_bias: bfloat16 [768], replicated, may hold values from -3 to 3
- key_weight: bfloat16 [768, 768], replicated, may hold values from -0.21875 to 0.21875
- value_weight: bfloat16 [768, 768], replicated, may hold values from -0.21875 to 0.21875
- value_bias: bfloat16 [768], replicated, may hold values from -0.059814453 to 0.059814453
- out_weight: bfloat16 [768, 768], replicated, may hold values from -6 to 6
- out_bias: bfloat16 [768], replicated, may hold values from -2 to 2
- first_gain: bfloat16 [768], replicated, may hold values from 0.25 to 1.75
- first_shift: bfloat16 [768], replicated, may hold values from -2 to 2
- up_weight: bfloat16 [768, 3072], replicated, may hold values from -0.21875 to 0.21875
- up_bias: bfloat16 [3072], replicated, may hold values from -3 to 3
- down_weight: bfloat16 [3072, 768], replicated, may hold values from -0.109375 to 0.109375
- down_bias: bfloat16 [768], replicated, may hold values from -2 to 2
- second_gain: bfloat16 [768], replicated, may hold values from 0.25 to 1.75
- second_shift: bfloat16 [768], replicated, may hold values from -2 to 2
Outputs:
- outputs: bfloat16 [2, 2048, 768], P('row', 'seq')
- input_grad: float32 [2, 2048, 768], P('row', 'seq')
- grad_query_weight: float32 [768, 768], P('seq')
- grad_query_bias: float32 [768], P('seq')
- grad_key_weight: float32 [768, 768], P('seq')
- grad_value_weight: float32 [768, 768], P('seq')
- grad_value_bias: float32 [768], P('seq')
- grad_out_weight: float32 [768, 768], P('seq')
- grad_out_bias: float32 [768], P('seq')
- grad_first_gain: float32 [768], P('seq')
- grad_first_shift: float32 [768], P('seq')
- grad_up_weight: float32 [768, 3072], P('seq')
- grad_up_bias: float32 [3072], P('seq')
- grad_down_weight: float32 [3072, 768], P('seq')
- grad_down_bias: float32 [768], P('seq')
- grad_second_gain: float32 [768], P('seq')
- grad_second_shift: float32 [768], P('seq')
Inputs may be any that keep to these rules, and one draw needn't show every extreme that they name: `clip_lengths`: each row's clip lengths sum to at most 2048; frames after that sum are padding; in every draw one row is filled to all 2048 frames.
All inputs are finite; a program needn't handle non-finite values.
Results may differ from a plain program's by a relative error of at most 0.028.
Values may be sent and summed in bfloat16 or wider, within the bound.
A program may use at most 128 MiB of HBM per device.

v0:
```python
import jax
import jax.numpy as jnp
from jax import lax
from jax.sharding import PartitionSpec as P

H = 12


EPSILON = 1e-05
NEGATIVE = -1e30


def passed_along(value, axis, steps):
    count = lax.axis_size(axis)
    pairs = [(source, (source + steps) % count) for source in range(count)]
    return lax.ppermute(value, axis, pairs)


def segment_ids(lengths, positions):
    clip_ends = jnp.cumsum(lengths, axis=1)
    counted = jnp.sum((positions[None, :, None] >= clip_ends[:, None, :]).astype(jnp.int32), axis=2)
    return jnp.where(positions[None, :] < clip_ends[:, -1:], counted, -1)


def norm_parts(summed):
    centre = summed - jnp.mean(summed, axis=-1, keepdims=True)
    variance = jnp.mean(centre * centre, axis=-1, keepdims=True)
    scale_inv = lax.rsqrt(variance + EPSILON)
    return (centre * scale_inv, scale_inv)


def norm_back(upstream, normal, scale_inv):
    return scale_inv * (
        upstream
        - jnp.mean(upstream, axis=-1, keepdims=True)
        - normal * jnp.mean(upstream * normal, axis=-1, keepdims=True)
    )


def gelu_slope(hidden):
    cumulative = 0.5 * (1.0 + lax.erf(hidden * 0.7071067811865476))
    density = jnp.exp(-0.5 * hidden * hidden) * 0.3989422804014327
    return cumulative + hidden * density


def block_size(key_count, frames):
    block_keys = min(frames, key_count)
    while block_keys * 2 <= 512 and key_count % (block_keys * 2) == 0:
        block_keys = block_keys * 2
    return block_keys


def split_keys(piece):
    rows_here, key_count, double = piece.shape
    half_width = double // 2
    key_heads = piece[..., :half_width].reshape(rows_here, key_count, H, half_width // H)
    value_heads = piece[..., half_width:].reshape(rows_here, key_count, H, half_width // H)
    return (key_heads, value_heads)


def allowed_mask(query_ids, key_ids):
    return ((query_ids[:, :, None] == key_ids[:, None, :]) & (key_ids[:, None, :] >= 0))[:, None]


def forward_piece(carry, piece, start, queries, query_ids, lengths):
    row_top, totals, summed = carry
    key_heads, value_heads = split_keys(piece)
    key_ids = segment_ids(lengths, start + jnp.arange(piece.shape[1], dtype=jnp.int32))
    scores = (
        jnp.einsum("rqhd,rkhd->rhqk", queries, key_heads, preferred_element_type=jnp.float32)
        * 0.125
    )
    allowed = allowed_mask(query_ids, key_ids)
    new_top = jnp.maximum(row_top, jnp.max(jnp.where(allowed, scores, NEGATIVE), axis=-1))
    weights = jnp.exp(jnp.where(allowed, scores - new_top[..., None], -jnp.inf))
    factor = jnp.exp(row_top - new_top)
    totals = totals * factor + jnp.sum(weights, axis=-1)
    summed = summed * jnp.swapaxes(factor, 1, 2)[..., None] + jnp.einsum(
        "rhqk,rkhd->rqhd",
        weights.astype(jnp.bfloat16),
        value_heads,
        preferred_element_type=jnp.float32,
    )
    return (new_top, totals, summed)


def forward_fold(carry, piece, start, queries, query_ids, lengths, frames):
    key_count = piece.shape[1]
    block_keys = block_size(key_count, frames)
    return forward_piece(carry, piece, start, queries, query_ids, lengths)


def backward_piece(piece, start, queries, grad_heads, query_ids, lengths, row_lse, delta):
    key_heads, value_heads = split_keys(piece)
    rows_here, key_count, double = piece.shape
    key_ids = segment_ids(lengths, start + jnp.arange(key_count, dtype=jnp.int32))
    scores = (
        jnp.einsum("rqhd,rkhd->rhqk", queries, key_heads, preferred_element_type=jnp.float32)
        * 0.125
    )
    allowed = allowed_mask(query_ids, key_ids)
    probs = jnp.exp(jnp.where(allowed, scores - row_lse[..., None], -jnp.inf))
    grad_probs = jnp.einsum(
        "rqhd,rkhd->rhqk", grad_heads, value_heads, preferred_element_type=jnp.float32
    )
    grad_scores = (probs * (grad_probs - delta[..., None])).astype(jnp.bfloat16)
    grad_query = (
        jnp.einsum("rhqk,rkhd->rqhd", grad_scores, key_heads, preferred_element_type=jnp.float32)
        * 0.125
    )
    grad_key = (
        jnp.einsum("rhqk,rqhd->rkhd", grad_scores, queries, preferred_element_type=jnp.float32)
        * 0.125
    )
    grad_value = jnp.einsum(
        "rhqk,rqhd->rkhd",
        probs.astype(jnp.bfloat16),
        grad_heads,
        preferred_element_type=jnp.float32,
    )
    joined = jnp.concatenate(
        [
            grad_key.reshape(rows_here, key_count, double // 2),
            grad_value.reshape(rows_here, key_count, double // 2),
        ],
        axis=-1,
    )
    return (grad_query, joined)


def on_device(
    inputs,
    cotangent,
    clip_lengths,
    query_weight,
    query_bias,
    key_weight,
    value_weight,
    value_bias,
    out_weight,
    out_bias,
    first_gain,
    first_shift,
    up_weight,
    up_bias,
    down_weight,
    down_bias,
    second_gain,
    second_shift,
):
    rows_here, frames, model_width = inputs.shape
    head_width = model_width // H
    place = lax.axis_index("seq")
    devices = lax.axis_size("seq")
    own_ids = segment_ids(clip_lengths, place * frames + jnp.arange(frames, dtype=jnp.int32))
    queries = (
        jnp.dot(inputs, query_weight, preferred_element_type=jnp.float32) + query_bias
    ).astype(jnp.bfloat16)
    keys_low = jnp.dot(inputs, key_weight, preferred_element_type=jnp.float32).astype(jnp.bfloat16)
    values_low = (
        jnp.dot(inputs, value_weight, preferred_element_type=jnp.float32) + value_bias
    ).astype(jnp.bfloat16)
    query_heads = queries.reshape(rows_here, frames, H, head_width)
    own_block = jnp.concatenate([keys_low, values_low], axis=-1)
    start_carry = (
        jnp.full((rows_here, H, frames), NEGATIVE, jnp.float32),
        jnp.zeros((rows_here, H, frames), jnp.float32),
        jnp.zeros((rows_here, frames, H, head_width), jnp.float32),
    )

    def fold_forward(carry, piece, start):
        return forward_fold(carry, piece, start, query_heads, own_ids, clip_lengths, frames)

    carry = fold_forward(start_carry, own_block, place * frames)

    def forward_turn(turn, state):
        carry_now, block_now = state
        block_now = passed_along(block_now, "seq", 1)
        source = jnp.mod(place - turn, devices)
        return (fold_forward(carry_now, block_now, source * frames), block_now)

    carry, unused = lax.fori_loop(1, devices, forward_turn, (carry, own_block))
    row_top, totals, summed = carry
    safe_totals = jnp.where(totals > 0.5, totals, 1.0)
    row_lse = row_top + jnp.log(safe_totals)
    attended = summed / jnp.swapaxes(safe_totals, 1, 2)[..., None]
    mixed = attended.reshape(rows_here, frames, model_width).astype(jnp.bfloat16)
    branch = jnp.dot(mixed, out_weight, preferred_element_type=jnp.float32) + out_bias
    first_normal, first_scale = norm_parts(inputs.astype(jnp.float32) + branch)
    normed = first_normal * first_gain + first_shift
    normed_low = normed.astype(jnp.bfloat16)
    hidden = jnp.dot(normed_low, up_weight, preferred_element_type=jnp.float32) + up_bias
    activated = jax.nn.gelu(hidden, approximate=False).astype(jnp.bfloat16)
    feed_out = jnp.dot(activated, down_weight, preferred_element_type=jnp.float32) + down_bias
    second_normal, second_scale = norm_parts(normed + feed_out)
    outputs = (second_normal * second_gain + second_shift).astype(jnp.bfloat16)
    upstream = cotangent.astype(jnp.float32)
    grad_second_gain = jnp.sum(upstream * second_normal, axis=(0, 1))
    grad_second_shift = jnp.sum(upstream, axis=(0, 1))
    grad_residual = norm_back(upstream * second_gain, second_normal, second_scale)
    grad_feed = grad_residual.astype(jnp.bfloat16)
    grad_down_weight = jnp.einsum(
        "rfk,rfd->kd", activated, grad_feed, preferred_element_type=jnp.float32
    )
    grad_down_bias = jnp.sum(grad_feed.astype(jnp.float32), axis=(0, 1))
    grad_hidden = (
        jnp.einsum("rfd,kd->rfk", grad_feed, down_weight, preferred_element_type=jnp.float32)
        * gelu_slope(hidden)
    ).astype(jnp.bfloat16)
    grad_up_weight = jnp.einsum(
        "rfd,rfk->dk", normed_low, grad_hidden, preferred_element_type=jnp.float32
    )
    grad_up_bias = jnp.sum(grad_hidden.astype(jnp.float32), axis=(0, 1))
    grad_normed = grad_residual + jnp.einsum(
        "rfk,dk->rfd", grad_hidden, up_weight, preferred_element_type=jnp.float32
    )
    grad_first_gain = jnp.sum(grad_normed * first_normal, axis=(0, 1))
    grad_first_shift = jnp.sum(grad_normed, axis=(0, 1))
    grad_branch = norm_back(grad_normed * first_gain, first_normal, first_scale)
    grad_branch_low = grad_branch.astype(jnp.bfloat16)
    grad_out_weight = jnp.einsum(
        "rfd,rfe->de", mixed, grad_branch_low, preferred_element_type=jnp.float32
    )
    grad_out_bias = jnp.sum(grad_branch_low.astype(jnp.float32), axis=(0, 1))
    grad_mixed = jnp.einsum(
        "rfe,de->rfd", grad_branch_low, out_weight, preferred_element_type=jnp.float32
    ).astype(jnp.bfloat16)
    grad_heads = grad_mixed.reshape(rows_here, frames, H, head_width)
    delta = jnp.swapaxes(jnp.sum(grad_heads.astype(jnp.float32) * attended, axis=-1), 1, 2)

    def fold_backward(piece, start):
        return backward_piece(
            piece, start, query_heads, grad_heads, own_ids, clip_lengths, row_lse, delta
        )

    grad_query, grad_block = fold_backward(own_block, place * frames)

    def backward_turn(turn, state):
        grad_query_now, block_now, carried = state
        block_now = passed_along(block_now, "seq", -1)
        carried = passed_along(carried.astype(jnp.bfloat16), "seq", -1).astype(carried.dtype)
        source = jnp.mod(place + turn, devices)
        part_query, part_block = fold_backward(block_now, source * frames)
        return (grad_query_now + part_query, block_now, carried + part_block)

    grad_query, unused, carried = lax.fori_loop(
        1, devices, backward_turn, (grad_query, own_block, grad_block)
    )
    grad_keys = passed_along(carried.astype(jnp.bfloat16), "seq", -1).astype(carried.dtype)
    grad_query_low = grad_query.reshape(rows_here, frames, model_width).astype(jnp.bfloat16)
    grad_keys_low = grad_keys.astype(jnp.bfloat16)
    grad_key_low = grad_keys_low[..., :model_width]
    grad_value_low = grad_keys_low[..., model_width:]
    grad_query_weight = jnp.einsum(
        "rfd,rfe->de", inputs, grad_query_low, preferred_element_type=jnp.float32
    )
    grad_query_bias = jnp.sum(grad_query_low.astype(jnp.float32), axis=(0, 1))
    grad_key_weight = jnp.einsum(
        "rfd,rfe->de", inputs, grad_key_low, preferred_element_type=jnp.float32
    )
    grad_value_weight = jnp.einsum(
        "rfd,rfe->de", inputs, grad_value_low, preferred_element_type=jnp.float32
    )
    grad_value_bias = jnp.sum(grad_value_low.astype(jnp.float32), axis=(0, 1))
    input_grad = (
        grad_branch
        + jnp.einsum(
            "rfe,de->rfd", grad_query_low, query_weight, preferred_element_type=jnp.float32
        )
        + jnp.einsum("rfe,de->rfd", grad_key_low, key_weight, preferred_element_type=jnp.float32)
        + jnp.einsum(
            "rfe,de->rfd", grad_value_low, value_weight, preferred_element_type=jnp.float32
        )
    )
    shared = (
        lax.psum_scatter(
            grad_query_weight.astype(jnp.bfloat16), "seq", scatter_dimension=0, tiled=True
        ).astype(jnp.float32),
        lax.psum_scatter(
            grad_query_bias.astype(jnp.bfloat16), "seq", scatter_dimension=0, tiled=True
        ).astype(jnp.float32),
        lax.psum_scatter(
            grad_key_weight.astype(jnp.bfloat16), "seq", scatter_dimension=0, tiled=True
        ).astype(jnp.float32),
        lax.psum_scatter(
            grad_value_weight.astype(jnp.bfloat16), "seq", scatter_dimension=0, tiled=True
        ).astype(jnp.float32),
        lax.psum_scatter(
            grad_value_bias.astype(jnp.bfloat16), "seq", scatter_dimension=0, tiled=True
        ).astype(jnp.float32),
        lax.psum_scatter(
            grad_out_weight.astype(jnp.bfloat16), "seq", scatter_dimension=0, tiled=True
        ).astype(jnp.float32),
        lax.psum_scatter(
            grad_out_bias.astype(jnp.bfloat16), "seq", scatter_dimension=0, tiled=True
        ).astype(jnp.float32),
        lax.psum_scatter(
            grad_first_gain.astype(jnp.bfloat16), "seq", scatter_dimension=0, tiled=True
        ).astype(jnp.float32),
        lax.psum_scatter(
            grad_first_shift.astype(jnp.bfloat16), "seq", scatter_dimension=0, tiled=True
        ).astype(jnp.float32),
        lax.psum_scatter(
            grad_up_weight.astype(jnp.bfloat16), "seq", scatter_dimension=0, tiled=True
        ).astype(jnp.float32),
        lax.psum_scatter(
            grad_up_bias.astype(jnp.bfloat16), "seq", scatter_dimension=0, tiled=True
        ).astype(jnp.float32),
        lax.psum_scatter(
            grad_down_weight.astype(jnp.bfloat16), "seq", scatter_dimension=0, tiled=True
        ).astype(jnp.float32),
        lax.psum_scatter(
            grad_down_bias.astype(jnp.bfloat16), "seq", scatter_dimension=0, tiled=True
        ).astype(jnp.float32),
        lax.psum_scatter(
            grad_second_gain.astype(jnp.bfloat16), "seq", scatter_dimension=0, tiled=True
        ).astype(jnp.float32),
        lax.psum_scatter(
            grad_second_shift.astype(jnp.bfloat16), "seq", scatter_dimension=0, tiled=True
        ).astype(jnp.float32),
    )
    shared = (
        lax.psum(shared[0].astype(jnp.bfloat16), "row").astype(jnp.float32),
        lax.psum(shared[1].astype(jnp.bfloat16), "row").astype(jnp.float32),
        lax.psum(shared[2].astype(jnp.bfloat16), "row").astype(jnp.float32),
        lax.psum(shared[3].astype(jnp.bfloat16), "row").astype(jnp.float32),
        lax.psum(shared[4].astype(jnp.bfloat16), "row").astype(jnp.float32),
        lax.psum(shared[5].astype(jnp.bfloat16), "row").astype(jnp.float32),
        lax.psum(shared[6].astype(jnp.bfloat16), "row").astype(jnp.float32),
        lax.psum(shared[7].astype(jnp.bfloat16), "row").astype(jnp.float32),
        lax.psum(shared[8].astype(jnp.bfloat16), "row").astype(jnp.float32),
        lax.psum(shared[9].astype(jnp.bfloat16), "row").astype(jnp.float32),
        lax.psum(shared[10].astype(jnp.bfloat16), "row").astype(jnp.float32),
        lax.psum(shared[11].astype(jnp.bfloat16), "row").astype(jnp.float32),
        lax.psum(shared[12].astype(jnp.bfloat16), "row").astype(jnp.float32),
        lax.psum(shared[13].astype(jnp.bfloat16), "row").astype(jnp.float32),
        lax.psum(shared[14].astype(jnp.bfloat16), "row").astype(jnp.float32),
    )
    (
        grad_query_weight,
        grad_query_bias,
        grad_key_weight,
        grad_value_weight,
        grad_value_bias,
        grad_out_weight,
        grad_out_bias,
        grad_first_gain,
        grad_first_shift,
        grad_up_weight,
        grad_up_bias,
        grad_down_weight,
        grad_down_bias,
        grad_second_gain,
        grad_second_shift,
    ) = shared
    return (
        outputs,
        input_grad,
        grad_query_weight,
        grad_query_bias,
        grad_key_weight,
        grad_value_weight,
        grad_value_bias,
        grad_out_weight,
        grad_out_bias,
        grad_first_gain,
        grad_first_shift,
        grad_up_weight,
        grad_up_bias,
        grad_down_weight,
        grad_down_bias,
        grad_second_gain,
        grad_second_shift,
    )


def solution(mesh):
    placed = (
        P("row", "seq", None),
        P("row", "seq", None),
        P("row", None),
        P(),
        P(),
        P(),
        P(),
        P(),
        P(),
        P(),
        P(),
        P(),
        P(),
        P(),
        P(),
        P(),
        P(),
        P(),
    )
    return jax.shard_map(
        on_device,
        mesh=mesh,
        in_specs=placed,
        out_specs=(
            P("row", "seq", None),
            P("row", "seq", None),
            P("seq", None),
            P("seq"),
            P("seq", None),
            P("seq", None),
            P("seq"),
            P("seq", None),
            P("seq"),
            P("seq"),
            P("seq"),
            P("seq", None),
            P("seq"),
            P("seq", None),
            P("seq"),
            P("seq"),
            P("seq"),
        ),
        check_vma=False,
    )
```

profile of v0, /device:TPU:0, one launch (start us, length us, event | category | flops | bytes accessed | tf_op | source)
XLA Modules:
  0.0 981.2 jit_solution(8619054017350623124)
XLA Ops:
  24.4 177.1 %while.40 = (s32[]{:T(128)}, f32[1,12,128]{2,1,0:T(8,128)S(1)}, f32[1,12,128]{2,1,0:T(8,128)S(1)}, f32[1,128,12,64]{1,3,2,0:T(8,128)S(1)}, bf16[1,128,1536]{1,2,...) while((s32[]{:T(128)}, f32[1,12,128]{2,1,0:T(8,128)S(1)}, ...), condition=%wide.region_8.9_spmd, body=%wide.region_4.8_spmd.sunk | while | flops 52337936 | bytes 7049310 | solution.py:182
  26.5 9.2 collective-permute-done
  38.7 8.7 collective-permute-done
  50.5 8.7 collective-permute-done
  62.2 8.7 collective-permute-done
  73.9 8.7 collective-permute-done
  85.7 8.7 collective-permute-done
  97.4 8.7 collective-permute-done
  109.1 8.7 collective-permute-done
  120.8 8.7 collective-permute-done
  132.6 8.7 collective-permute-done
  144.3 8.7 collective-permute-done
  156.0 8.7 collective-permute-done
  167.7 8.7 collective-permute-done
  179.5 8.7 collective-permute-done
  191.2 8.7 collective-permute-done
  226.1 260.5 %while.41 = (s32[]{:T(128)}, f32[1,128,12,64]{1,3,2,0:T(8,128)S(1)}, bf16[1,128,1536]{1,2,0:T(8,128)(2,1)}, bf16[1,128,1536]{1,2,0:T(8,128)(2,1)}, s32[1,128]{1,...) while((s32[]{:T(128)}, ...), condition=%wide.region_20.21_spmd, body=%wide.region_18.20_spmd.sunk | while | flops 128322320 | bytes 12853426 | solution.py:246
  515.8 33.6 %reduce-scatter.19.cloned.1.call-done = bf16[48,768]{1,0:T(8,128)(2,1)} async-done(((bf16[768,768]{1,0:T(8,128)(2,1)}), bf16[48,768]{1,0:T(8,128)(2,1)}) %reduce-scatter.19.cloned.1.call-update) | async-done | bytes 73744
  551.0 58.9 %reduce-scatter.23.cloned.1.call-done = bf16[48,768]{1,0:T(8,128)(2,1)} async-done(((bf16[768,768]{1,0:T(8,128)(2,1)}), bf16[48,768]{1,0:T(8,128)(2,1)}) %reduce-scatter.23.cloned.1.call-update) | async-done | bytes 73744
  611.6 58.9 %reduce-scatter.21.cloned.1.call-done = bf16[48,768]{1,0:T(8,128)(2,1)} async-done(((bf16[768,768]{1,0:T(8,128)(2,1)}), bf16[48,768]{1,0:T(8,128)(2,1)}) %reduce-scatter.21.cloned.1.call-update) | async-done | bytes 73744
  672.3 58.8 %reduce-scatter.13.cloned.1.call-done = bf16[48,768]{1,0:T(8,128)(2,1)} async-done(((bf16[768,768]{1,0:T(8,128)(2,1)}), bf16[48,768]{1,0:T(8,128)(2,1)}) %reduce-scatter.13.cloned.1.call-update) | async-done | bytes 73744 | tf_op jit(solution)/shard_map/reduce_scatter | solution.py:291
  731.1 78.3 %reduce-scatter.15.cloned.1.call-done = bf16[48,3072]{1,0:T(8,128)(2,1)} async-done(((bf16[768,3072]{1,0:T(8,128)(2,1)}), bf16[48,3072]{1,0:T(8,128)(2,1)}) %reduce-scatter.15.cloned.1.call-update) | async-done | bytes 294928 | tf_op jit(solution)/shard_map/reduce_scatter | solution.py:303
  809.4 78.8 %reduce-scatter.17.cloned.1.call-done = bf16[192,768]{1,0:T(8,128)(2,1)} async-done(((bf16[3072,768]{1,0:T(8,128)(2,1)}), bf16[192,768]{1,0:T(8,128)(2,1)}) %reduce-scatter.17.cloned.1.call-update) | async-done | bytes 294928 | tf_op jit(solution)/shard_map/reduce_scatter | solution.py:309
  893.4 58.1 %all-reduce.9 = (bf16[768]{0:T(1024)(128)(2,1)S(1)}, bf16[768]{0:T(1024)(128)(2,1)S(1)}, bf16[768]{0:T(1024)(128)(2,1)S(1)}, bf16[768]{0:T(1024)(128)(2,1)S(1)},...) all-reduce(bf16[768]{0:T(1024)(128)(2,1)S(1)} %copy-done.47, ...), channel_id=3, replica_groups=mesh['seq'=16,'row'=2] {'seq'}, use_global_device_ids=true, to_apply=%region_24.25.clone | all-reduce | flops 9216 | bytes 36864
  (723 shorter events, 406.8 us)
Async XLA Ops:
  7.2 542.1 %reduce-scatter.19.cloned.1.call-start = ((), (), s32[]{:S(2)}) async-start(), calls=%async_computation.9 | async-start | bytes 1253376
  24.6 11.1 %collective-permute-start = (bf16[1,128,1536]{1,2,0:T(8,128)(2,1)}, bf16[1,128,1536]{1,2,0:T(8,128)(2,1)S(1)}, u32[]{:S(2)}, u32[]{:S(2)}) collective-permute-start(bf16[1,128,1536]{1,2,0:T(8,128)(2,1)} %get-tuple-element.939), channel_id=1, source_target_pairs={{0,2},{2,4},{4,6},{6,8},{8,10},{10,12},{12,14},{14,16},{16,18},{18... | collective-permute-start | bytes 1179656 | tf_op jit(solution)/shard_map/while/body/eval_jaxpr/ppermute | solution.py:16
  226.1 12.4 %collective-permute-start.2 = (bf16[1,128,1536]{1,2,0:T(8,128)(2,1)}, bf16[1,128,1536]{1,2,0:T(8,128)(2,1)S(1)}, u32[]{:S(2)}, u32[]{:S(2)}) collective-permute-start(bf16[1,128,1536]{1,2,0:T(8,128)(2,1)} %get-tuple-element.982), channel_id=1, source_target_pairs={{0,30},{2,0},{4,2},{6,4},{8,6},{10,8},{12,10},{14,12},{16,14},{18,... | collective-permute-start | bytes 1179656 | tf_op jit(solution)/shard_map/while/body/eval_jaxpr/ppermute | solution.py:16
  239.3 16.8 %collective-permute-start.2 = (bf16[1,128,1536]{1,2,0:T(8,128)(2,1)}, bf16[1,128,1536]{1,2,0:T(8,128)(2,1)S(1)}, u32[]{:S(2)}, u32[]{:S(2)}) collective-permute-start(bf16[1,128,1536]{1,2,0:T(8,128)(2,1)} %get-tuple-element.982), channel_id=1, source_target_pairs={{0,30},{2,0},{4,2},{6,4},{8,6},{10,8},{12,10},{14,12},{16,14},{18,... | collective-permute-start | bytes 1179656 | tf_op jit(solution)/shard_map/while/body/eval_jaxpr/ppermute | solution.py:16
  256.9 16.8 %collective-permute-start.2 = (bf16[1,128,1536]{1,2,0:T(8,128)(2,1)}, bf16[1,128,1536]{1,2,0:T(8,128)(2,1)S(1)}, u32[]{:S(2)}, u32[]{:S(2)}) collective-permute-start(bf16[1,128,1536]{1,2,0:T(8,128)(2,1)} %get-tuple-element.982), channel_id=1, source_target_pairs={{0,30},{2,0},{4,2},{6,4},{8,6},{10,8},{12,10},{14,12},{16,14},{18,... | collective-permute-start | bytes 1179656 | tf_op jit(solution)/shard_map/while/body/eval_jaxpr/ppermute | solution.py:16
  274.6 16.8 %collective-permute-start.2 = (bf16[1,128,1536]{1,2,0:T(8,128)(2,1)}, bf16[1,128,1536]{1,2,0:T(8,128)(2,1)S(1)}, u32[]{:S(2)}, u32[]{:S(2)}) collective-permute-start(bf16[1,128,1536]{1,2,0:T(8,128)(2,1)} %get-tuple-element.982), channel_id=1, source_target_pairs={{0,30},{2,0},{4,2},{6,4},{8,6},{10,8},{12,10},{14,12},{16,14},{18,... | collective-permute-start | bytes 1179656 | tf_op jit(solution)/shard_map/while/body/eval_jaxpr/ppermute | solution.py:16
  292.3 16.8 %collective-permute-start.2 = (bf16[1,128,1536]{1,2,0:T(8,128)(2,1)}, bf16[1,128,1536]{1,2,0:T(8,128)(2,1)S(1)}, u32[]{:S(2)}, u32[]{:S(2)}) collective-permute-start(bf16[1,128,1536]{1,2,0:T(8,128)(2,1)} %get-tuple-element.982), channel_id=1, source_target_pairs={{0,30},{2,0},{4,2},{6,4},{8,6},{10,8},{12,10},{14,12},{16,14},{18,... | collective-permute-start | bytes 1179656 | tf_op jit(solution)/shard_map/while/body/eval_jaxpr/ppermute | solution.py:16
  309.9 16.8 %collective-permute-start.2 = (bf16[1,128,1536]{1,2,0:T(8,128)(2,1)}, bf16[1,128,1536]{1,2,0:T(8,128)(2,1)S(1)}, u32[]{:S(2)}, u32[]{:S(2)}) collective-permute-start(bf16[1,128,1536]{1,2,0:T(8,128)(2,1)} %get-tuple-element.982), channel_id=1, source_target_pairs={{0,30},{2,0},{4,2},{6,4},{8,6},{10,8},{12,10},{14,12},{16,14},{18,... | collective-permute-start | bytes 1179656 | tf_op jit(solution)/shard_map/while/body/eval_jaxpr/ppermute | solution.py:16
  327.6 16.8 %collective-permute-start.2 = (bf16[1,128,1536]{1,2,0:T(8,128)(2,1)}, bf16[1,128,1536]{1,2,0:T(8,128)(2,1)S(1)}, u32[]{:S(2)}, u32[]{:S(2)}) collective-permute-start(bf16[1,128,1536]{1,2,0:T(8,128)(2,1)} %get-tuple-element.982), channel_id=1, source_target_pairs={{0,30},{2,0},{4,2},{6,4},{8,6},{10,8},{12,10},{14,12},{16,14},{18,... | collective-permute-start | bytes 1179656 | tf_op jit(solution)/shard_map/while/body/eval_jaxpr/ppermute | solution.py:16
  345.3 16.8 %collective-permute-start.2 = (bf16[1,128,1536]{1,2,0:T(8,128)(2,1)}, bf16[1,128,1536]{1,2,0:T(8,128)(2,1)S(1)}, u32[]{:S(2)}, u32[]{:S(2)}) collective-permute-start(bf16[1,128,1536]{1,2,0:T(8,128)(2,1)} %get-tuple-element.982), channel_id=1, source_target_pairs={{0,30},{2,0},{4,2},{6,4},{8,6},{10,8},{12,10},{14,12},{16,14},{18,... | collective-permute-start | bytes 1179656 | tf_op jit(solution)/shard_map/while/body/eval_jaxpr/ppermute | solution.py:16
  362.9 16.8 %collective-permute-start.2 = (bf16[1,128,1536]{1,2,0:T(8,128)(2,1)}, bf16[1,128,1536]{1,2,0:T(8,128)(2,1)S(1)}, u32[]{:S(2)}, u32[]{:S(2)}) collective-permute-start(bf16[1,128,1536]{1,2,0:T(8,128)(2,1)} %get-tuple-element.982), channel_id=1, source_target_pairs={{0,30},{2,0},{4,2},{6,4},{8,6},{10,8},{12,10},{14,12},{16,14},{18,... | collective-permute-start | bytes 1179656 | tf_op jit(solution)/shard_map/while/body/eval_jaxpr/ppermute | solution.py:16
  380.6 16.8 %collective-permute-start.2 = (bf16[1,128,1536]{1,2,0:T(8,128)(2,1)}, bf16[1,128,1536]{1,2,0:T(8,128)(2,1)S(1)}, u32[]{:S(2)}, u32[]{:S(2)}) collective-permute-start(bf16[1,128,1536]{1,2,0:T(8,128)(2,1)} %get-tuple-element.982), channel_id=1, source_target_pairs={{0,30},{2,0},{4,2},{6,4},{8,6},{10,8},{12,10},{14,12},{16,14},{18,... | collective-permute-start | bytes 1179656 | tf_op jit(solution)/shard_map/while/body/eval_jaxpr/ppermute | solution.py:16
  398.3 16.8 %collective-permute-start.2 = (bf16[1,128,1536]{1,2,0:T(8,128)(2,1)}, bf16[1,128,1536]{1,2,0:T(8,128)(2,1)S(1)}, u32[]{:S(2)}, u32[]{:S(2)}) collective-permute-start(bf16[1,128,1536]{1,2,0:T(8,128)(2,1)} %get-tuple-element.982), channel_id=1, source_target_pairs={{0,30},{2,0},{4,2},{6,4},{8,6},{10,8},{12,10},{14,12},{16,14},{18,... | collective-permute-start | bytes 1179656 | tf_op jit(solution)/shard_map/while/body/eval_jaxpr/ppermute | solution.py:16
  415.9 16.8 %collective-permute-start.2 = (bf16[1,128,1536]{1,2,0:T(8,128)(2,1)}, bf16[1,128,1536]{1,2,0:T(8,128)(2,1)S(1)}, u32[]{:S(2)}, u32[]{:S(2)}) collective-permute-start(bf16[1,128,1536]{1,2,0:T(8,128)(2,1)} %get-tuple-element.982), channel_id=1, source_target_pairs={{0,30},{2,0},{4,2},{6,4},{8,6},{10,8},{12,10},{14,12},{16,14},{18,... | collective-permute-start | bytes 1179656 | tf_op jit(solution)/shard_map/while/body/eval_jaxpr/ppermute | solution.py:16
  433.6 16.8 %collective-permute-start.2 = (bf16[1,128,1536]{1,2,0:T(8,128)(2,1)}, bf16[1,128,1536]{1,2,0:T(8,128)(2,1)S(1)}, u32[]{:S(2)}, u32[]{:S(2)}) collective-permute-start(bf16[1,128,1536]{1,2,0:T(8,128)(2,1)} %get-tuple-element.982), channel_id=1, source_target_pairs={{0,30},{2,0},{4,2},{6,4},{8,6},{10,8},{12,10},{14,12},{16,14},{18,... | collective-permute-start | bytes 1179656 | tf_op jit(solution)/shard_map/while/body/eval_jaxpr/ppermute | solution.py:16
  451.2 16.8 %collective-permute-start.2 = (bf16[1,128,1536]{1,2,0:T(8,128)(2,1)}, bf16[1,128,1536]{1,2,0:T(8,128)(2,1)S(1)}, u32[]{:S(2)}, u32[]{:S(2)}) collective-permute-start(bf16[1,128,1536]{1,2,0:T(8,128)(2,1)} %get-tuple-element.982), channel_id=1, source_target_pairs={{0,30},{2,0},{4,2},{6,4},{8,6},{10,8},{12,10},{14,12},{16,14},{18,... | collective-permute-start | bytes 1179656 | tf_op jit(solution)/shard_map/while/body/eval_jaxpr/ppermute | solution.py:16
  468.9 16.8 %collective-permute-start.2 = (bf16[1,128,1536]{1,2,0:T(8,128)(2,1)}, bf16[1,128,1536]{1,2,0:T(8,128)(2,1)S(1)}, u32[]{:S(2)}, u32[]{:S(2)}) collective-permute-start(bf16[1,128,1536]{1,2,0:T(8,128)(2,1)} %get-tuple-element.982), channel_id=1, source_target_pairs={{0,30},{2,0},{4,2},{6,4},{8,6},{10,8},{12,10},{14,12},{16,14},{18,... | collective-permute-start | bytes 1179656 | tf_op jit(solution)/shard_map/while/body/eval_jaxpr/ppermute | solution.py:16
  489.4 120.5 %reduce-scatter.23.cloned.1.call-start = ((), (), s32[]{:S(2)}) async-start(), calls=%async_computation.11 | async-start | bytes 1253376
  489.4 10.4 %collective-permute-start.3 = (bf16[1,128,1536]{1,2,0:T(8,128)(2,1)}, bf16[1,128,1536]{1,2,0:T(8,128)(2,1)S(1)}, u32[]{:S(2)}, u32[]{:S(2)}) collective-permute-start(bf16[1,128,1536]{1,2,0:T(8,128)(2,1)} %get-tuple-element.514), channel_id=1, source_target_pairs={{0,30},{2,0},{4,2},{6,4},{8,6},{10,8},{12,10},{14,12},{16,14},{18,... | collective-permute-start | bytes 1179656 | tf_op jit(solution)/shard_map/ppermute | solution.py:16
  502.5 168.1 %reduce-scatter.21.cloned.1.call-start = ((), (), s32[]{:S(2)}) async-start(), calls=%async_computation.10 | async-start | bytes 1253376
  505.5 225.6 %reduce-scatter.13.cloned.1.call-start = ((), (), s32[]{:S(2)}) async-start(), calls=%async_computation.6 | async-start | bytes 1253376 | tf_op jit(solution)/shard_map/reduce_scatter | solution.py:291
  507.1 302.3 %reduce-scatter.15.cloned.1.call-start = ((), (), s32[]{:S(2)}) async-start(), calls=%async_computation.7 | async-start | bytes 5013504 | tf_op jit(solution)/shard_map/reduce_scatter | solution.py:303
  510.8 377.4 %reduce-scatter.17.cloned.1.call-start = ((), (), s32[]{:S(2)}) async-start(), calls=%async_computation.8 | async-start | bytes 5013504 | tf_op jit(solution)/shard_map/reduce_scatter | solution.py:309
  515.7 449.3 %all-reduce.14.cloned.1.call-start = ((), (), s32[]{:S(2)}) async-start(), calls=%async_computation.12 | async-start | bytes 2506752 | tf_op jit(solution)/shard_map/psum | solution.py:323
  (98 other events, 2517.1 us)
Sparse Core Ops, SparseCore 0:
  489.5 59.7 reduce-scatter.18
  552.9 56.9 reduce-scatter.22
  613.6 56.9 reduce-scatter.20
  674.0 56.9 reduce-scatter.12
  734.8 74.5 reduce-scatter.14
  813.6 74.5 reduce-scatter.16
  891.5 44.4 all-reduce.13
where the time goes:
time: 982 us; the launch traced here: 981 us
  waiting for transfers between devices  629 us (64%)
  matrix products  70.9 us (7%)
  starting transfers between devices  69.2 us (7%)
  other arithmetic  66.7 us (7%)
  local copies, waits for them, and re-layouts  64.1 us (7%)
  blocking collectives  63 us (6%)
  between operations  16.3 us (2%)
    ppermute x46, waiting for transfers between devices, passed_along(): return lax.ppermute(value, axis, pairs)  261 us
    unnamed x10, waiting for transfers between devices  152 us
    reduce_scatter x1, waiting for transfers between devices, on_device(): lax.psum_scatter(grad_down_weight.astype(jnp.bfloat16), 'seq', scatter_di...  78.8 us
    reduce_scatter x1, waiting for transfers between devices, on_device(): lax.psum_scatter(grad_up_weight.astype(jnp.bfloat16), 'seq', scatter_dime...  78.3 us
    ppermute x46, starting transfers between devices, passed_along(): return lax.ppermute(value, axis, pairs)  68.9 us
    reduce_scatter x1, waiting for transfers between devices, on_device(): lax.psum_scatter(grad_out_weight.astype(jnp.bfloat16), 'seq', scatter_dim...  58.8 us
    unnamed x1, blocking collectives  58.1 us
    while x75, local copies, waits for them, and re-layouts  22.6 us
  transfers between devices with their start and end apart: 53, of which 37 were waited for; matrix products, arithmetic and copies ran while one was open for 11% of the time, Pallas kernels for 0%

commit v1 on v0

v1 whole, which is shorter than its diff:
```python
import functools
from types import SimpleNamespace as Refs

import jax
import jax.numpy as jnp
from jax import lax
from jax.experimental import pallas as pl
from jax.experimental.pallas import tpu as pltpu
from jax.sharding import PartitionSpec as P

H = 12
HEAD = 64
EPSILON = 1e-05
NEGATIVE = -1e30
MASKED = -2e30
MESH = pl.DeviceIdType.MESH
F32 = jnp.float32
BF16 = jnp.bfloat16


def nn(left, right):
    return lax.dot_general(left, right, (((1,), (0,)), ((), ())), preferred_element_type=F32)


def nt(left, right):
    return lax.dot_general(left, right, (((1,), (1,)), ((), ())), preferred_element_type=F32)


def norm_parts(summed):
    centre = summed - jnp.mean(summed, axis=-1, keepdims=True)
    variance = jnp.mean(centre * centre, axis=-1, keepdims=True)
    scale_inv = lax.rsqrt(variance + EPSILON)
    return (centre * scale_inv, scale_inv)


def norm_back(upstream, normal, scale_inv):
    return scale_inv * (
        upstream
        - jnp.mean(upstream, axis=-1, keepdims=True)
        - normal * jnp.mean(upstream * normal, axis=-1, keepdims=True)
    )


def gelu_parts(hidden):
    cumulative = 0.5 * (1.0 + lax.erf(hidden * 0.7071067811865476))
    density = jnp.exp(-0.5 * hidden * hidden) * 0.3989422804014327
    return hidden * cumulative, cumulative + hidden * density


Q_BIAS, V_BIAS, OUT_BIAS, GAIN1, SHIFT1, DOWN_BIAS, GAIN2, SHIFT2, UP_BIAS = range(9)


def layer_kernel(names, S, R, *refs):
    n = Refs(**dict(zip(names, refs, strict=True)))
    D = n.x.shape[1]
    F = n.x.shape[0]
    FF = n.wd_hbm.shape[0]
    T, DH, FH = 2 * F, D // 2, FF // 2
    C = S // 2
    N = C // 2
    CR = D // C
    CD = FF // C
    pairs = DH // (2 * HEAD)
    heads = DH // HEAD
    TILE = 256
    roomy = C <= 8
    tiles = FH // TILE

    place = lax.axis_index("seq")
    row = lax.axis_index("row")
    core = lax.rem(place, 2)
    chip = place // 2
    pos = jnp.where(lax.rem(chip, 2) == 0, chip // 2, C - 1 - chip // 2)

    def around(steps):
        return lax.rem(pos + (steps + C), C)

    def chip_at(where):
        return jnp.where(where < N, 2 * where, 2 * (C - 1 - where) + 1)

    sibling = (2 * chip + 1 - core, row)
    right = (2 * chip_at(around(1)) + core, row)
    left = (2 * chip_at(around(-1)) + core, row)
    ring = (right, left)
    parity = lax.rem(row, 2)
    mate_row = row + 1 - 2 * parity
    mate = (place, mate_row)
    others = []
    for dr in range(R):
        for dc in range(2):
            if dr or dc:
                others.append((lax.rem(row + dr, R), lax.rem(core + dc, 2)))

    def remote(src, dst, send, recv, device):
        return pltpu.make_async_remote_copy(
            src_ref=src, dst_ref=dst, send_sem=send, recv_sem=recv, device_id=device, device_id_type=MESH
        )

    started = []

    def start(copy):
        copy.start()
        started.append(copy)

    half_d = pl.multiple_of(core * DH, 128)
    half_f = pl.multiple_of(core * FH, 128)
    loads = []
    for source, target in (
        (n.wq_hbm.at[:, pl.ds(half_d, DH)], n.wq),
        (n.wk_hbm.at[:, pl.ds(half_d, DH)], n.wk),
        (n.wv_hbm.at[:, pl.ds(half_d, DH)], n.wv),
        (n.wo_hbm, n.wo),
        (n.wu_hbm.at[:, pl.ds(half_f, FH)], n.wu),
        (n.wd_hbm.at[pl.ds(half_f, FH)], n.wd),
    ):
        loads.append(pltpu.make_async_copy(source, target, n.load_sem.at[len(loads)]))
        loads[-1].start()

    barrier = pltpu.get_barrier_semaphore()
    partners = [right, left] + [(2 * chip + c, r) for r, c in others]
    for device in partners:
        pl.semaphore_signal(barrier, inc=1, device_id=device, device_id_type=MESH)
    pl.semaphore_wait(barrier, len(partners))

    xa = n.xa
    own_rows = pl.multiple_of(core * F, F)
    other_rows = pl.multiple_of((1 - core) * F, F)
    xa[pos, pl.ds(own_rows, F)] = n.x[...]

    def hop_view(where, piece):
        return xa.at[where, pl.ds(pl.multiple_of(own_rows + piece * (F // 2), F // 2), F // 2)]

    def hop_send(d, h, piece):
        view = hop_view(around((h - 1) * (2 * d - 1)), piece)
        return remote(view, view, n.g_send.at[d, h - 1, piece], n.g_recv.at[d, h - 1, piece], ring[d])

    def hop_recv(d, h, piece):
        view = hop_view(around(h * (2 * d - 1)), piece)
        return remote(view, view, n.g_send.at[d, h - 1, piece], n.g_recv.at[d, h - 1, piece], ring[d])

    def share_send(where):
        view = xa.at[where, pl.ds(own_rows, F)]
        return remote(view, view, n.s_send.at[where], n.s_recv.at[where], sibling)

    def share_recv(where):
        view = xa.at[where, pl.ds(other_rows, F)]
        return remote(view, view, n.s_send.at[where], n.s_recv.at[where], sibling)

    for piece in range(2):
        hop_send(0, 1, piece).start()
        hop_send(1, 1, piece).start()
        if piece == 0:
            share_send(pos).start()

    def gather_step(step):
        h, piece = 1 + step // 2, lax.rem(step, 2)

        @pl.when(step < 2 * N - 2)
        def _():
            hop_recv(0, h, piece).wait_recv()
            hop_recv(1, h, piece).wait_recv()

            @pl.when((h < N - 1) | (piece == 0))
            def _():
                hop_send(0, h + 1, piece).start()

            @pl.when((h < N - 1) | (piece == 1))
            def _():
                hop_send(1, h + 1, piece).start()

            @pl.when(piece == 1)
            def _():
                share_send(around(-h)).start()
                share_send(around(h)).start()

        @pl.when(step == 2 * N - 2)
        def _():
            hop_recv(0, N, 0).wait_recv()
            hop_recv(1, N, 1).wait_recv()
            share_send(around(N)).start()

    def gather_sent():
        for h in range(1, N + 1):
            for piece in range(2):
                for d in range(2):
                    if h < N or piece == d:
                        hop_send(d, h, piece).wait_send()

        def shared(where, carry):
            share_send(where).wait_send()
            return carry

        lax.fori_loop(0, C, shared, 0)

    for index, vector in enumerate(
        (n.bias_q, n.bias_v, n.bias_o, n.gain1, n.shift1, n.bias_d, n.gain2, n.shift2)
    ):
        n.vec[index : index + 1] = vector[...].astype(F32).reshape(1, D)
    for index in range(FF // D):
        n.vec[UP_BIAS + index : UP_BIAS + index + 1] = (
            n.bias_u[D * index : D * (index + 1)].astype(F32).reshape(1, D)
        )

    ends = []
    total = 0
    for i in range(n.lens.shape[1]):
        total = total + n.lens[0, i]
        ends.append(total)

    def ids(positions, padding):
        counted = jnp.zeros_like(positions)
        for end in ends:
            counted = counted + (positions >= end).astype(jnp.int32)
        return jnp.where(positions < ends[-1], counted, padding)

    query_ids = ids(lax.broadcasted_iota(jnp.int32, (1, T), 1) + chip * T, -1)

    def set_bias(where):
        key_ids = ids(lax.broadcasted_iota(jnp.int32, (T, 1), 0) + chip_at(where) * T, -2)
        n.bias[...] = jnp.where(key_ids == query_ids, 0.0, MASKED)

    lane = lax.broadcasted_iota(jnp.int32, (T, 2 * HEAD), 1)

    def head_masked(values, target):
        for pair in range(pairs):
            both = values[:, 2 * HEAD * pair : 2 * HEAD * (pair + 1)]
            target[2 * pair] = jnp.where(lane < HEAD, both, 0.0).astype(BF16)
            target[2 * pair + 1] = jnp.where(lane < HEAD, 0.0, both).astype(BF16)

    def key_rows(where):
        return pl.ds(pl.multiple_of(where * T, T), T)

    def forward_block(where):
        xk = xa[where]
        keys = nn(xk, n.wk[...]).astype(BF16)
        n.ka[key_rows(where), :] = keys
        if roomy:
            n.kt[:, key_rows(where)] = keys.T
        values = (nn(xk, n.wv[...]) + n.vec[V_BIAS : V_BIAS + 1, pl.ds(half_d, DH)]).astype(BF16)
        n.va[key_rows(where), :] = values
        values_t = values.T
        set_bias(where)
        for j in range(heads):
            pair = j // 2
            st = nt(keys[:, 2 * HEAD * pair : 2 * HEAD * (pair + 1)], n.qm[j]) + n.bias[...]
            top = n.top[j : j + 1]
            new_top = jnp.maximum(top, jnp.max(st, axis=0, keepdims=True))
            weights = jnp.exp(st - new_top)
            factor = jnp.exp(top - new_top)
            n.tot[j : j + 1] = n.tot[j : j + 1] * factor + jnp.sum(weights, axis=0, keepdims=True)
            n.top[j : j + 1] = new_top
            span = slice(HEAD * j, HEAD * (j + 1))
            n.ot[span] = n.ot[span] * factor + nn(values_t[span], weights.astype(BF16))

    n.top[...] = jnp.full(n.top.shape, NEGATIVE, F32)
    n.tot[...] = jnp.zeros(n.tot.shape, F32)
    n.ot[...] = jnp.zeros(n.ot.shape, F32)
    small = n.small.at[core]
    small[...] = jnp.zeros(small.shape, F32)

    for load in loads[:3]:
        load.wait()
    share_recv(pos).wait_recv()
    queries = (nn(xa[pos], n.wq[...]) + n.vec[Q_BIAS : Q_BIAS + 1, pl.ds(half_d, DH)]).astype(BF16)
    head_masked(queries.astype(F32) * 0.125, n.qm)

    def forward_step(step, carry):
        gather_step(step)

        @pl.when(step != 1)
        def _():
            index = jnp.maximum(step - 1, 0)
            where = around((index + 1) // 2 * (1 - 2 * lax.rem(index, 2)))

            @pl.when(step > 0)
            def _():
                share_recv(where).wait_recv()

            forward_block(where)

        return carry

    lax.fori_loop(0, 2 * N + 1, forward_step, 0)

    def turn_block(where, carry):
        n.xt[:, key_rows(where)] = xa[where].T
        return carry

    def turn_blocks(first, last):
        lax.fori_loop(first, last, turn_block, 0)

    gather_sent()
    safe = jnp.where(n.tot[...] > 0.5, n.tot[...], 1.0)
    n.lse[...] = n.top[...] + jnp.log(safe)
    for j in range(heads):
        span = slice(HEAD * j, HEAD * (j + 1))
        n.ot[span] = n.ot[span] / safe[j : j + 1]

    def swap(index, src, dst, landed):
        send, recv = n.m_send.at[index], n.m_recv.at[index]
        start(remote(src, dst, send, recv, sibling))
        return remote(src, landed, send, recv, sibling)

    def lend(index, src, dst, device, landed, recv_index=None):
        recv_index = index if recv_index is None else recv_index
        start(remote(src, dst, n.y_send.at[index], n.y_recv.at[recv_index], device))
        return remote(src, landed, n.y_send.at[index], n.y_recv.at[index], device)

    def sent(copy):
        started[:] = [other for other in started if other is not copy]
        copy.wait_send()

    obt = n.obt
    own_half = pl.ds(pl.multiple_of(core * DH, DH), DH)
    other_half = pl.ds(pl.multiple_of((1 - core) * DH, DH), DH)
    obt[own_half] = n.ot[...].astype(BF16)
    swapped = swap(0, obt.at[own_half], obt.at[own_half], obt.at[other_half])
    turn_blocks(0, C // 8)
    loads[3].wait()
    swapped.wait_recv()

    def vec(index):
        return n.vec[index : index + 1]

    mixed = obt[:, pl.ds(own_rows, F)].T
    branch = nn(mixed, n.wo[...]) + vec(OUT_BIAS)
    first_normal, first_scale = norm_parts(n.x[...].astype(F32) + branch)
    n.n1[...] = first_normal
    normed = first_normal * vec(GAIN1) + vec(SHIFT1)
    n.x1[...] = normed
    xb = n.xb
    xb[pl.ds(own_rows, F)] = normed.astype(BF16)
    swapped = swap(1, xb.at[pl.ds(own_rows, F)], xb.at[pl.ds(own_rows, F)], xb.at[pl.ds(other_rows, F)])
    xb_copy = started[-1]
    xbm = n.xbm
    lent_xb = lend(0, xb.at[pl.ds(own_rows, F)], xbm.at[pl.ds(own_rows, F)], mate, xbm.at[pl.ds(own_rows, F)])
    xb_lent = started[-1]
    turn_blocks(C // 8, 3 * C // 8)
    loads[4].wait()
    swapped.wait_recv()

    act, slope = n.act, n.slope
    acto, att = n.acto, n.att
    du = act

    def up_tile(t, carry):
        cols = pl.ds(pl.multiple_of(t * DH, DH), DH)
        bias = n.vec[
            pl.ds(UP_BIAS + core * (FH // D) + t // 2, 1), pl.ds(pl.multiple_of(lax.rem(t, 2) * DH, DH), DH)
        ]
        value, tangent = gelu_parts(nn(xb[...], n.wu[:, cols]) + bias)
        low = value.astype(BF16)
        act[:, cols] = low
        turned = low.T
        for c in range(DH // CD):
            for half in range(2):
                first = CD * c + CD // 2 * half
                acto[t * (DH // CD) + c, half] = turned[first : first + CD // 2]
        slope[:, cols] = tangent.astype(slope.dtype)
        return carry

    lax.fori_loop(0, FH // DH, up_tile, 0)
    own_ff = pl.ds(core * (C // 2), C // 2)
    other_ff = pl.ds((1 - core) * (C // 2), C // 2)
    lent_act = lend(1, acto.at[:, 1 - parity], att.at[1, own_ff], mate, att.at[1, own_ff])
    swapped_act = swap(2, acto.at[:, parity], att.at[0, own_ff], att.at[0, other_ff])
    loads[5].wait()
    part, part_in = n.part, n.part_in

    def down_tile(t, carry):
        cols = pl.ds(pl.multiple_of(t * TILE, TILE), TILE)
        part[:, cols] = nn(act[...], n.wd[:, cols])
        return carry

    lax.fori_loop(0, D // TILE, down_tile, 0)
    swapped = swap(3, part.at[pl.ds(other_rows, F)], part_in, part_in)
    part_copy = started[-1]
    lent_xb.wait_recv()
    swapped_xbm = swap(8, xbm.at[pl.ds(own_rows, F)], xbm.at[pl.ds(own_rows, F)], xbm.at[pl.ds(other_rows, F)])
    turn_blocks(3 * C // 8, 4 * C // 8)
    n.xbt[...] = xb[...].T
    upstream = n.cot[...].astype(F32)
    small[SHIFT2 : SHIFT2 + 1] = jnp.sum(upstream, axis=0, keepdims=True)
    swapped.wait_recv()
    second_normal, second_scale = norm_parts(
        n.x1[...] + part[pl.ds(own_rows, F)] + part_in[...] + vec(DOWN_BIAS)
    )
    n.out[...] = (second_normal * vec(GAIN2) + vec(SHIFT2)).astype(BF16)
    residual = norm_back(upstream * vec(GAIN2), second_normal, second_scale)
    n.grad_x[...] = residual
    low = residual.astype(BF16)
    df = n.df
    df[pl.ds(own_rows, F)] = low
    swapped = swap(4, df.at[pl.ds(own_rows, F)], df.at[pl.ds(own_rows, F)], df.at[pl.ds(other_rows, F)])
    dfm = n.dfm
    lent_df = []
    for c in range(2):
        start(
            remote(
                df.at[pl.ds(own_rows, F), pl.ds(DH * c, DH)],
                dfm.at[pl.ds(own_rows, F)],
                n.y_send.at[2 + c],
                n.y_recv.at[2 + core],
                (2 * chip + c, mate_row),
            )
        )
        lent_df.append(
            remote(
                df.at[pl.ds(own_rows, F), pl.ds(DH * c, DH)],
                dfm.at[pl.ds(F * c, F)],
                n.y_send.at[2 + c],
                n.y_recv.at[2 + c],
                (2 * chip + c, mate_row),
            )
        )
    small[GAIN2 : GAIN2 + 1] = jnp.sum(upstream * second_normal, axis=0, keepdims=True)
    small[DOWN_BIAS : DOWN_BIAS + 1] = jnp.sum(low.astype(F32), axis=0, keepdims=True)
    turn_blocks(4 * C // 8, 7 * C // 8)
    swapped.wait_recv()

    class Flow:
        def __init__(self, index, chunk, landing, split, ready=None):
            self.index, self.chunk, self.landing, self.split, self.ready = index, chunk, landing, split, ready

        def parts(self, d, distance):
            where = around(distance if d == 0 else -distance)
            src, dst = self.chunk(where), self.landing.at[d, distance - 1]
            if distance == N:
                src, dst = src.at[self.split[d]], dst.at[self.split[d]]
            send, recv = n.r_send.at[self.index, d, distance - 1], n.r_recv.at[self.index, d, distance - 1]
            return remote(src, dst, send, recv, ring[d]), dst

        def begin(self):
            if self.ready is not None:
                self.ready(around(N))
            start(self.parts(0, N)[0])
            start(self.parts(1, N)[0])

        def step(self, distance):
            for d in range(2):
                where = around(distance if d == 0 else -distance)
                if self.ready is not None:
                    self.ready(where)
                arriving, landed = self.parts(d, distance + 1)
                arriving.wait_recv()
                target = self.chunk(where)
                if distance + 1 == N:
                    target = target.at[self.split[d]]
                target[...] = (target[...].astype(F32) + landed[...].astype(F32)).astype(BF16)
                start(self.parts(d, distance)[0])

        def end(self):
            if self.ready is not None:
                self.ready(pos)
            found = self.chunk(pos)[...].astype(F32)
            for d in range(2):
                arriving, landed = self.parts(d, 1)
                arriving.wait_recv()
                found = found + landed[...].astype(F32)
            return found

    def add_lent(where):
        c = chip_at(where)
        lent_chunk(c).wait_recv()
        n.ap[c, parity] = (n.ap[c, parity].astype(F32) + n.am[c].astype(F32)).astype(BF16)

    def lent_chunk(c):
        return remote(
            n.ap.at[c, 1 - parity, pl.ds(0, 3)], n.am.at[c, pl.ds(0, 3)], n.ya_send.at[c], n.ya_recv.at[c], mate
        )

    whole = slice(None)
    flow_d = Flow(
        0, lambda where: n.gd_sum.at[chip_at(where)], n.gd_in, [pl.ds(0, CD // 4), pl.ds(CD // 4, CD // 4)]
    )
    flow_u = Flow(
        1,
        lambda where: n.gu_sum.at[chip_at(where)],
        n.gu_in,
        [(whole, pl.ds(0, FH // 4)), (whole, pl.ds(FH // 4, FH // 4))],
    )
    flow_a = Flow(
        2, lambda where: n.ap.at[chip_at(where), parity], n.ga_in, [pl.ds(0, 2), pl.ds(2, 2)], add_lent
    )
    flow_x = Flow(3, lambda where: n.ix_sum.at[where], n.ix_in, [pl.ds(0, F // 2), pl.ds(F // 2, F // 2)])

    def hidden_tile(t, carry):
        cols = pl.ds(pl.multiple_of(t * TILE, TILE), TILE)
        low = (nt(df[...], n.wd[cols, :]) * slope[:, cols].astype(F32)).astype(BF16)
        du[:, cols] = low
        small[
            pl.ds(UP_BIAS + core * (FH // D) + t // (D // TILE), 1),
            pl.ds(pl.multiple_of(lax.rem(t, D // TILE) * TILE, TILE), TILE),
        ] = jnp.sum(low.astype(F32), axis=0, keepdims=True)
        return carry

    lax.fori_loop(0, tiles, hidden_tile, 0)

    quarter = pl.multiple_of(parity * (FH // 2), FH // 2)
    other_quarter = pl.multiple_of((1 - parity) * (FH // 2), FH // 2)
    lent_du = lend(4, du.at[:, pl.ds(other_quarter, FH // 2)], n.dum, mate, n.dum)
    def back_tile(t, carry):
        cols = pl.ds(pl.multiple_of(t * TILE, TILE), TILE)
        part[:, cols] = nt(du[...], n.wu[cols, :])
        return carry

    sent(part_copy)
    lax.fori_loop(0, D // TILE, back_tile, 0)
    swapped = swap(5, part.at[pl.ds(other_rows, F)], part_in, part_in)
    part_copy = started[-1]

    turn_blocks(7 * C // 8, C)
    swapped.wait_recv()
    grad_normed = n.grad_x[...] + part[pl.ds(own_rows, F)] + part_in[...]
    normal = n.n1[...]
    small[GAIN1 : GAIN1 + 1] = jnp.sum(grad_normed * normal, axis=0, keepdims=True)
    small[SHIFT1 : SHIFT1 + 1] = jnp.sum(grad_normed, axis=0, keepdims=True)
    grad_branch = norm_back(grad_normed * vec(GAIN1), normal, first_scale)
    n.x1[...] = grad_branch
    low = grad_branch.astype(BF16)
    sent(xb_copy)
    sent(xb_lent)
    da = xb
    da[pl.ds(own_rows, F)] = low
    swapped = swap(6, da.at[pl.ds(own_rows, F)], da.at[pl.ds(own_rows, F)], da.at[pl.ds(other_rows, F)])
    small[OUT_BIAS : OUT_BIAS + 1] = jnp.sum(low.astype(F32), axis=0, keepdims=True)
    swapped_xbm.wait_recv()
    n.xmt[...] = xbm[...].T
    lent_act.wait_recv()
    swapped_actm = swap(9, att.at[1, own_ff], att.at[1, own_ff], att.at[1, other_ff])
    att[0, own_ff] = acto[:, parity]
    swapped.wait_recv()

    grad_mixed = nt(da[...], n.wo[own_half]).astype(BF16).astype(F32)
    head_masked(grad_mixed, n.dm)
    grad_mixed_t = grad_mixed.T
    for j in range(heads):
        span = slice(HEAD * j, HEAD * (j + 1))
        n.delta[j : j + 1] = jnp.sum(grad_mixed_t[span] * n.ot[span], axis=0, keepdims=True)

    def grad_down():
        swapped_act.wait_recv()
        swapped_actm.wait_recv()
        for lent in lent_df:
            lent.wait_recv()

        def tile(t, carry):
            two = pl.ds(2 * t, 2)
            found = nn(att[0, two].reshape(CD, T), df[:, pl.ds(half_d, DH)])
            found = found + nn(att[1, two].reshape(CD, T), dfm[...])
            n.gd_sum[two] = found.astype(BF16).reshape(2, CD // 2, DH)
            return carry

        lax.fori_loop(0, C // 2, tile, 0)

    def grad_up():
        lent_du.wait_recv()

        def tile(t, carry):
            cols = pl.ds(pl.multiple_of(t * TILE, TILE), TILE)
            found = nn(n.xbt[...], du[:, pl.ds(pl.multiple_of(quarter + t * TILE, TILE), TILE)])
            found = (found + nn(n.xmt[...], n.dum[:, cols])).astype(BF16)
            for c in range(C):
                n.gu_sum[c, :, cols] = found[CR * c : CR * (c + 1)]
            return carry

        lax.fori_loop(0, FH // 2 // TILE, tile, 0)

    def grad_attention(index, left, right):
        for t in range(2):
            found = nn(left(pl.ds(DH * t, DH)), right)
            for c in range(DH // CR):
                for half in range(2):
                    first = CR * c + CR // 2 * half
                    n.ap[DH // CR * t + c, half, index] = found[first : first + CR // 2].astype(BF16)

    n.dqt[...] = jnp.zeros(n.dqt.shape, F32)
    n.vsum[...] = jnp.zeros(n.vsum.shape, F32)

    def backward_block(where):
        rows = key_rows(where)
        set_bias(where)
        for pair in range(pairs):
            cols = slice(2 * HEAD * pair, 2 * HEAD * (pair + 1))
            keys, values = n.ka[rows, cols], n.va[rows, cols]
            grad_key, grad_value = 0.0, 0.0
            keys_t = n.kt[cols, rows] if roomy else keys.T
            for j in (2 * pair, 2 * pair + 1):
                st = nt(keys, n.qm[j]) + n.bias[...]
                probs = jnp.exp(st - n.lse[j : j + 1])
                grad_probs = nt(values, n.dm[j])
                grad_scores = (probs * (grad_probs - n.delta[j : j + 1])).astype(BF16)
                grad_value = grad_value + nn(probs.astype(BF16), n.dm[j])
                grad_key = grad_key + nn(grad_scores, n.qm[j])
                span = slice(HEAD * j, HEAD * (j + 1))
                n.dqt[span] += nn(keys_t[HEAD * (j % 2) : HEAD * (j % 2 + 1)], grad_scores)
            n.ka[rows, cols] = grad_key.astype(BF16)
            low = grad_value.astype(BF16)
            n.va[rows, cols] = low
            n.vsum[:, cols] += jnp.sum(low.astype(F32), axis=0, keepdims=True)
        return nt(n.ka[rows], n.wk[...]) + nt(n.va[rows], n.wv[...])

    def cross(where):
        send, recv = n.c_send.at[where], n.c_recv.at[where]
        return remote(xa.at[where, pl.ds(0, F)], xa.at[where, pl.ds(F, F)], send, recv, sibling)

    def key_block(where, extra=None):
        found = backward_block(where)
        if extra is not None:
            found = found + extra()
        part[...] = found
        xa[where, pl.ds(0, F)] = part[pl.ds(other_rows, F)].astype(BF16)
        n.ix_sum[where] = part[pl.ds(own_rows, F)].astype(BF16)

    def join(where):
        cross(where).wait_recv()
        n.ix_sum[where] = (
            n.ix_sum[where].astype(F32) + xa[where, pl.ds(F, F)].astype(F32)
        ).astype(BF16)

    sent(part_copy)
    key_block(around(N))
    start(cross(around(N)))
    grad_down()
    flow_d.begin()
    join(around(N))
    flow_x.begin()
    for distance in range(N - 1, 0, -1):

        def two_keys(i, carry, distance=distance):
            key_block(around((1 - 2 * i) * distance))
            return carry

        lax.fori_loop(0, 2, two_keys, 0)
        start(cross(around(distance)))
        start(cross(around(-distance)))
        if distance == N - 1:
            grad_up()
            flow_u.begin()
            grad_attention(3, lambda rows: obt[rows], da[:, pl.ds(half_d, DH)])
            lent_out = lend(5, n.ap.at[:, 1 - parity, 3], n.am.at[:, 3], mate, n.am.at[:, 3])
        join(around(distance))
        join(around(-distance))
        flow_x.step(distance)

    feed_steps = list(range(N - 1, -1, -1))

    def feed_step():
        if not feed_steps:
            return
        distance = feed_steps.pop(0)
        if distance > 0:
            flow_d.step(distance)
            flow_u.step(distance)
        else:
            n.fd[...] = flow_d.end().astype(n.fd.dtype)
            spread(0, n.fd, n.yd)
            found = flow_u.end()
            for c in range(2):
                n.fu[c] = found[CR // 2 * c : CR // 2 * (c + 1)].astype(n.fu.dtype)
            scatter(1, n.fu, n.yu, True)

    def query_part():
        grad_query = (n.dqt[...] * 0.125).T.astype(BF16)
        n.dq[...] = grad_query
        return nt(grad_query, n.wq[...])

    key_block(pos, query_part)
    start(cross(pos))
    small[Q_BIAS : Q_BIAS + 1, pl.ds(half_d, DH)] = jnp.sum(n.dq[...].astype(F32), axis=0, keepdims=True)
    small[V_BIAS : V_BIAS + 1, pl.ds(half_d, DH)] = n.vsum[...]
    small_swap = swap(7, small, small, n.small.at[1 - core])

    grad_attention(0, lambda rows: n.xt[rows, key_rows(pos)], n.dq[...])
    grad_attention(1, lambda rows: n.xt[rows], n.ka[...])
    grad_attention(2, lambda rows: n.xt[rows], n.va[...])
    for distance in range(N, -1, -1):
        for where in [around(distance)] + ([around(-distance)] if 0 < distance < N else []):
            start(lent_chunk(chip_at(where)))

    feed_step()
    small_swap.wait_recv()
    around_small = n.small_ring
    mine = pl.ds(pl.multiple_of(core * 8, 8), 8)
    around_small[pos] = n.small[0, mine] + n.small[1, mine]

    def small_send(d, h):
        view = around_small.at[around(1 - h if d == 0 else h - 1)]
        return remote(view, view, n.sr_send.at[d, h - 1], n.sr_recv.at[d, h - 1], ring[d])

    def small_recv(d, h):
        view = around_small.at[around(-h if d == 0 else h)]
        return remote(view, view, n.sr_send.at[d, h - 1], n.sr_recv.at[d, h - 1], ring[d])

    start(small_send(0, 1))
    start(small_send(1, 1))

    def scatter(index, source, gathered, split):
        gathered[row, core] = source[core] if split else source[...]
        for k, (r, c) in enumerate(others):
            view = source.at[c] if split else source
            start(
                remote(
                    view,
                    gathered.at[row, core],
                    n.f_send.at[index, k],
                    n.f_recv.at[index, row, core],
                    (2 * chip + c, r),
                )
            )

    def collect(index, source, gathered, split):
        for r, c in others:
            view = source.at[c] if split else source
            remote(
                view, gathered.at[r, c], n.f_send.at[index, 0], n.f_recv.at[index, r, c], (2 * chip + c, r)
            ).wait_recv()

    def spread(index, source, gathered):
        @pl.when(core == parity)
        def _():
            gathered[row // 2, core] = source[...]

        for k in range(R):
            copy = spread_copy(index, source, gathered, k)
            if k == 0:
                pl.when(core != parity)(copy.start)
            else:
                copy.start()

    def spread_copy(index, source, gathered, k):
        device = (2 * chip + parity, lax.rem(row + k, R))
        return remote(
            source, gathered.at[row // 2, core], n.f_send.at[index, k], n.f_recv.at[index, row // 2, core], device
        )

    def spread_done(index, source, gathered):
        for q in range(R // 2):
            for c in range(2):
                arriving = remote(
                    source, gathered.at[q, c], n.f_send.at[index, 0], n.f_recv.at[index, q, c], sibling
                )
                pl.when((2 * q + core != row) | (core != c))(arriving.wait_recv)
        for k in range(R):
            copy = spread_copy(index, source, gathered, k)
            if k == 0:
                pl.when(core != parity)(copy.wait_send)
            else:
                copy.wait_send()

    feed_step()
    lent_out.wait_recv()
    flow_a.begin()
    feed_step()
    join(pos)
    n.grad_x[...] = n.x1[...] + flow_x.end()

    for h in range(1, N + 1):
        small_recv(0, h).wait_recv()
        if h < N:
            small_recv(1, h).wait_recv()
            start(small_send(0, h + 1))
            if h + 1 < N:
                start(small_send(1, h + 1))
        if h < N:
            flow_a.step(N - h)
            feed_step()
    found = around_small[0]
    for where in range(1, C):
        found = found + around_small[where]
    n.fs[...] = found
    scatter(3, n.fs, n.ys, False)
    n.fa[...] = flow_a.end().astype(n.fa.dtype)
    spread(2, n.fa, n.ya)
    while feed_steps:
        feed_step()
    spread_done(0, n.fd, n.yd)
    collect(1, n.fu, n.yu, True)
    collect(3, n.fs, n.ys, False)
    spread_done(2, n.fa, n.ya)
    for copy in started:
        copy.wait_send()


def finish_kernel(out, grad_x, yd, yu, ya, ys, *targets):
    (
        to_out,
        to_grad_x,
        to_query,
        to_query_bias,
        to_key,
        to_value,
        to_value_bias,
        to_o,
        to_out_bias,
        to_gain1,
        to_shift1,
        to_up,
        to_up_bias,
        to_down,
        to_down_bias,
        to_gain2,
        to_shift2,
    ) = targets
    R = yu.shape[0]
    D = out.shape[1]
    place = lax.axis_index("seq")

    def over_rows(gathered, *index, first=0, by=1):
        found = gathered[(first, *index)].astype(F32)
        for r in range(first + by, gathered.shape[0], by):
            found = found + gathered[(r, *index)].astype(F32)
        return found

    to_out[...] = out[...]
    to_grad_x[...] = grad_x[...]
    for c in range(2):
        width = yd.shape[-1]
        to_down[:, width * c : width * (c + 1)] = over_rows(yd, c)
        for index, target in enumerate((to_query, to_key, to_value, to_o)):
            target[:, width * c : width * (c + 1)] = over_rows(ya, c, index)
        width = yu.shape[-1]
        for half in range(2):
            first = width * (2 * c + half)
            to_up[:, first : first + width] = over_rows(yu, c, first=half, by=2)
    sums = jnp.concatenate([over_rows(ys, 0), over_rows(ys, 1)])
    width = to_query_bias.shape[0]
    turned = pltpu.roll(sums, lax.rem(D - place * width, D), 1)
    for index, target in (
        (Q_BIAS, to_query_bias),
        (V_BIAS, to_value_bias),
        (OUT_BIAS, to_out_bias),
        (GAIN1, to_gain1),
        (SHIFT1, to_shift1),
        (DOWN_BIAS, to_down_bias),
        (GAIN2, to_gain2),
        (SHIFT2, to_shift2),
    ):
        target[...] = turned[index, :width]
    width = to_up_bias.shape[0]
    per = D // width
    turned = pltpu.roll(sums, lax.rem(D - lax.rem(place, per) * width, D), 1)
    line = lax.broadcasted_iota(jnp.int32, sums.shape, 0) == UP_BIAS + place // per
    to_up_bias[...] = jnp.sum(jnp.where(line, turned, 0.0), axis=0)[:width]


def on_device(
    inputs,
    cotangent,
    clip_lengths,
    query_weight,
    query_bias,
    key_weight,
    value_weight,
    value_bias,
    out_weight,
    out_bias,
    first_gain,
    first_shift,
    up_weight,
    up_bias,
    down_weight,
    down_bias,
    second_gain,
    second_shift,
):
    S, R = lax.axis_size("seq"), lax.axis_size("row")
    _, F, D = inputs.shape
    FF = up_weight.shape[1]
    C = S // 2
    N = C // 2
    T, DH, FH, CR, CD = 2 * F, D // 2, FF // 2, D // C, FF // C
    heads = DH // HEAD
    keys = C * T
    wire = BF16 if CR % 32 == 0 else F32
    wire_d = BF16 if CD % 32 == 0 else F32
    vmem = pl.BlockSpec(memory_space=pltpu.VMEM)
    hbm = pl.BlockSpec(memory_space=pl.ANY)
    operands = dict(
        x=(inputs[0], vmem),
        cot=(cotangent[0], vmem),
        lens=(clip_lengths, pl.BlockSpec(memory_space=pltpu.SMEM)),
        bias_q=(query_bias, vmem),
        bias_v=(value_bias, vmem),
        bias_o=(out_bias, vmem),
        gain1=(first_gain, vmem),
        shift1=(first_shift, vmem),
        bias_d=(down_bias, vmem),
        gain2=(second_gain, vmem),
        shift2=(second_shift, vmem),
        bias_u=(up_bias, vmem),
        wq_hbm=(query_weight, hbm),
        wk_hbm=(key_weight, hbm),
        wv_hbm=(value_weight, hbm),
        wo_hbm=(out_weight, hbm),
        wu_hbm=(up_weight, hbm),
        wd_hbm=(down_weight, hbm),
    )
    results = dict(
        out=((F, D), BF16),
        grad_x=((F, D), F32),
        yd=((R // 2, 2, CD // 2, DH), wire_d),
        yu=((R, 2, CR // 2, FH // 2), wire),
        ya=((R // 2, 2, 4, CR // 2, DH), wire),
        ys=((R, 2, 8, D), F32),
    )
    dma = pltpu.SemaphoreType.DMA
    scratch = dict(
        wq=pltpu.VMEM((D, DH), BF16),
        wk=pltpu.VMEM((D, DH), BF16),
        wv=pltpu.VMEM((D, DH), BF16),
        wo=pltpu.VMEM((D, D), BF16),
        wu=pltpu.VMEM((D, FH), BF16),
        wd=pltpu.VMEM((FH, D), BF16),
        xa=pltpu.VMEM((C, T, D), BF16),
        xt=pltpu.VMEM((D, keys), BF16),
        ka=pltpu.VMEM((keys, DH), BF16),
        va=pltpu.VMEM((keys, DH), BF16),
        bias=pltpu.VMEM((T, T), F32),
        qm=pltpu.VMEM((heads, T, 2 * HEAD), BF16),
        dm=pltpu.VMEM((heads, T, 2 * HEAD), BF16),
        vec=pltpu.VMEM((8 + FF // D, D), F32),
        top=pltpu.VMEM((8, T), F32),
        tot=pltpu.VMEM((8, T), F32),
        lse=pltpu.VMEM((8, T), F32),
        delta=pltpu.VMEM((8, T), F32),
        ot=pltpu.VMEM((DH, T), F32),
        dqt=pltpu.VMEM((DH, T), F32),
        dq=pltpu.VMEM((T, DH), BF16),
        vsum=pltpu.VMEM((1, DH), F32),
        obt=pltpu.VMEM((D, T), BF16),
        n1=pltpu.VMEM((F, D), F32),
        x1=pltpu.VMEM((F, D), F32),
        xb=pltpu.VMEM((T, D), BF16),
        xbt=pltpu.VMEM((D, T), BF16),
        df=pltpu.VMEM((T, D), BF16),
        act=pltpu.VMEM((T, FH), BF16),
        acto=pltpu.VMEM((C // 2, 2, CD // 2, T), BF16),
        att=pltpu.VMEM((2, C, CD // 2, T), BF16),
        xbm=pltpu.VMEM((T, D), BF16),
        xmt=pltpu.VMEM((D, T), BF16),
        dfm=pltpu.VMEM((T, DH), BF16),
        dum=pltpu.VMEM((T, FH // 2), BF16),
        slope=pltpu.VMEM((T, FH), F32 if C <= 8 else BF16),
        part=pltpu.VMEM((T, D), F32),
        part_in=pltpu.VMEM((F, D), F32),
        gd_sum=pltpu.VMEM((C, CD // 2, DH), BF16),
        gd_in=pltpu.VMEM((2, N, CD // 2, DH), BF16),
        gu_sum=pltpu.VMEM((C, CR, FH // 2), BF16),
        gu_in=pltpu.VMEM((2, N, CR, FH // 2), BF16),
        ap=pltpu.VMEM((C, 2, 4, CR // 2, DH), BF16),
        am=pltpu.VMEM((C, 4, CR // 2, DH), BF16),
        ga_in=pltpu.VMEM((2, N, 4, CR // 2, DH), BF16),
        ix_sum=pltpu.VMEM((C, F, D), BF16),
        ix_in=pltpu.VMEM((2, N, F, D), BF16),
        fd=pltpu.VMEM((CD // 2, DH), wire_d),
        fu=pltpu.VMEM((2, CR // 2, FH // 2), wire),
        fa=pltpu.VMEM((4, CR // 2, DH), wire),
        small=pltpu.VMEM((2, 16, D), F32),
        small_ring=pltpu.VMEM((C, 8, D), F32),
        fs=pltpu.VMEM((8, D), F32),
        load_sem=dma((6,)),
        g_send=dma((2, N, 2)),
        g_recv=dma((2, N, 2)),
        s_send=dma((C,)),
        s_recv=dma((C,)),
        m_send=dma((10,)),
        m_recv=dma((10,)),
        r_send=dma((4, 2, N)),
        r_recv=dma((4, 2, N)),
        y_send=dma((6,)),
        y_recv=dma((6,)),
        ya_send=dma((C,)),
        ya_recv=dma((C,)),
        c_send=dma((C,)),
        c_recv=dma((C,)),
        sr_send=dma((2, N)),
        sr_recv=dma((2, N)),
        f_send=dma((4, 2 * R - 1)),
        f_recv=dma((4, R, 2)),
    )
    if C <= 8:
        scratch.update(kt=pltpu.VMEM((DH, keys), BF16))
    names = [*operands, *results, *scratch]
    found = pl.pallas_call(
        functools.partial(layer_kernel, names, S, R),
        out_shape=[jax.ShapeDtypeStruct(shape, kind) for shape, kind in results.values()],
        in_specs=[spec for _, spec in operands.values()],
        out_specs=[vmem] * len(results),
        scratch_shapes=list(scratch.values()),
        compiler_params=pltpu.CompilerParams(
            collective_id=0, has_side_effects=True, vmem_limit_bytes=62 * 1024 * 1024
        ),
        name="layer",
    )(*[value for value, _ in operands.values()])
    shapes = [(F, D), (F, D), (D // S, D), (D // S,), (D // S, D), (D // S, D), (D // S,), (D // S, D)]
    shapes += [(D // S,)] * 3 + [(D // S, FF), (FF // S,), (FF // S, D)] + [(D // S,)] * 3
    kinds = [BF16] + [F32] * (len(shapes) - 1)
    final = pl.pallas_call(
        finish_kernel,
        out_shape=[jax.ShapeDtypeStruct(shape, kind) for shape, kind in zip(shapes, kinds, strict=True)],
        in_specs=[vmem] * len(found),
        out_specs=[vmem] * len(shapes),
        name="finish",
    )(*found)
    return (final[0][None], final[1][None], *final[2:])


def solution(mesh):
    shared = P("seq", None)
    part = P("seq")
    return jax.shard_map(
        on_device,
        mesh=mesh,
        in_specs=(P("row", "seq", None), P("row", "seq", None), P("row", None)) + (P(),) * 15,
        out_specs=(
            P("row", "seq", None),
            P("row", "seq", None),
            shared,
            part,
            shared,
            shared,
            part,
            shared,
            part,
            part,
            part,
            shared,
            part,
            shared,
            part,
            part,
            part,
        ),
        check_vma=False,
    )
```

time: 982 us -> 130 us (0.13)
  waiting for transfers between devices: 629 us -> 0 us
  Pallas kernels: 0 us -> 129 us
  matrix products: 70.9 us -> 0 us
  starting transfers between devices: 69.2 us -> 0 us
  other arithmetic: 66.7 us -> 0 us
  local copies, waits for them, and re-layouts: 64.1 us -> 0 us
  blocking collectives: 63 us -> 0 us
  between operations: 16.3 us -> 0.83 us
    ppermute x46 -> x0, waiting for transfers between devices: 261 us -> none  [passed_along(): return lax.ppermute(value, axis, pairs)]
    reduce_scatter x3 -> x0, waiting for transfers between devices: 216 us -> none  [the longest x1 78.8 us: on_device(): lax.psum_scatter(grad_down_weight.astype(jnp.bfloat16), 'seq', scatter_di...]
    unnamed x10 -> x0, waiting for transfers between devices: 152 us -> none
    pallas_call x0 -> x2, Pallas kernels: none -> 129 us  [the longest x1 126 us: on_device(): pl.pallas_call(functools.partial(layer_kernel, names, S, R), out_shape=[j...]
    dot_general x129 -> x0, matrix products: 70.9 us -> none  [the longest x16 6.71 us: backward_piece(): jnp.einsum('rqhd,rkhd->rhqk', grad_heads, value_heads, preferred_element_...]
    ppermute x46 -> x0, starting transfers between devices: 68.9 us -> none  [passed_along(): return lax.ppermute(value, axis, pairs)]
    unnamed x1 -> x0, blocking collectives: 58.1 us -> none
    while x76 -> x0, local copies, waits for them, and re-layouts: 22.8 us -> none
  transfers between devices with their start and end apart: 53 -> 0, of which waited for: 37 -> 0; matrix products, arithmetic and copies ran while one was open for 11% -> 0% of each run, Pallas kernels for 0% -> 0%
where the time goes in v1:
time: 130 us
  Pallas kernels  129 us (99%)
    pallas_call x1, Pallas kernels, on_device(): pl.pallas_call(functools.partial(layer_kernel, names, S, R), out_shape=[j...  126 us
    pallas_call x1, Pallas kernels, on_device(): pl.pallas_call(finish_kernel, out_shape=[jax.ShapeDtypeStruct(shape, kind...  2.82 us

profile of v1, /device:TPU:0, one launch (start us, length us, event | category | flops | bytes accessed | tf_op | source)
XLA Modules:
  0.0 129.8 jit_solution(1514268612513655105)
XLA Ops:
  0.7 126.2 %layer.1 = (bf16[128,768]{1,0:T(8,128)(2,1)}, f32[128,768]{1,0:T(8,128)}, bf16[1,2,192,384]{3,2,1,0:T(8,128)(2,1)}, bf16[2,2,48,768]{3,2,1,0:T(8,128)(2,1)}, bf1...) custom-call(bf16[128,768]{1,0:T(8,128)(2,1)} %bitcast.4, bf16[128,768]{1,0:T(8,128)(2,1)} %bitcast.5, ...), custom_call_target="tpu_custom_call" | custom-call | tf_op jit(solution)/shard_map/layer/pallas_call | solution.py:985
  126.8 2.8 %finish.1 = (bf16[128,768]{1,0:T(8,128)(2,1)}, f32[128,768]{1,0:T(8,128)}, f32[48,768]{1,0:T(8,128)}, f32[48]{0:T(128)}, f32[48,768]{1,0:T(8,128)}, /*index=5*/f...) custom-call(bf16[128,768]{1,0:T(8,128)(2,1)} %get-tuple-element.40.o, ...), custom_call_target="tpu_custom_call" | custom-call | tf_op jit(solution)/shard_map/finish/pallas_call | solution.py:999

commit v2 on v1

--- a/solution.py
+++ b/solution.py
@@ -10,6 +10,7 @@
 
 H = 12
 HEAD = 64
+PIECES = 4
 EPSILON = 1e-05
 NEGATIVE = -1e30
 MASKED = -2e30
@@ -107,8 +108,8 @@
     loads = []
     for source, target in (
         (n.wq_hbm.at[:, pl.ds(half_d, DH)], n.wq),
-        (n.wk_hbm.at[:, pl.ds(half_d, DH)], n.wk),
-        (n.wv_hbm.at[:, pl.ds(half_d, DH)], n.wv),
+        (n.wk_hbm.at[:, pl.ds(half_d, DH)], n.wkv.at[:, pl.ds(0, DH)]),
+        (n.wv_hbm.at[:, pl.ds(half_d, DH)], n.wkv.at[:, pl.ds(DH, DH)]),
         (n.wo_hbm, n.wo),
         (n.wu_hbm.at[:, pl.ds(half_f, FH)], n.wu),
         (n.wd_hbm.at[pl.ds(half_f, FH)], n.wd),
@@ -127,8 +128,10 @@
     other_rows = pl.multiple_of((1 - core) * F, F)
     xa[pos, pl.ds(own_rows, F)] = n.x[...]
 
+    step_rows = F // PIECES
+
     def hop_view(where, piece):
-        return xa.at[where, pl.ds(pl.multiple_of(own_rows + piece * (F // 2), F // 2), F // 2)]
+        return xa.at[where, pl.ds(pl.multiple_of(own_rows + piece * step_rows, step_rows), step_rows)]
 
     def hop_send(d, h, piece):
         view = hop_view(around((h - 1) * (2 * d - 1)), piece)
@@ -146,44 +149,39 @@
         view = xa.at[where, pl.ds(other_rows, F)]
         return remote(view, view, n.s_send.at[where], n.s_recv.at[where], sibling)
 
-    for piece in range(2):
+    for piece in range(PIECES):
         hop_send(0, 1, piece).start()
         hop_send(1, 1, piece).start()
         if piece == 0:
             share_send(pos).start()
 
-    def gather_step(step):
-        h, piece = 1 + step // 2, lax.rem(step, 2)
-
-        @pl.when(step < 2 * N - 2)
+    def gather_step(h, piece):
+        hop_recv(0, h, piece).wait_recv()
+        hop_recv(1, h, piece).wait_recv()
+
+        @pl.when((h < N - 1) | (piece < PIECES // 2))
         def _():
-            hop_recv(0, h, piece).wait_recv()
-            hop_recv(1, h, piece).wait_recv()
-
-            @pl.when((h < N - 1) | (piece == 0))
-            def _():
-                hop_send(0, h + 1, piece).start()
-
-            @pl.when((h < N - 1) | (piece == 1))
-            def _():
-                hop_send(1, h + 1, piece).start()
-
-            @pl.when(piece == 1)
-            def _():
-                share_send(around(-h)).start()
-                share_send(around(h)).start()
-
-        @pl.when(step == 2 * N - 2)
+            hop_send(0, h + 1, piece).start()
+
+        @pl.when((h < N - 1) | (piece >= PIECES // 2))
         def _():
-            hop_recv(0, N, 0).wait_recv()
-            hop_recv(1, N, 1).wait_recv()
-            share_send(around(N)).start()
+            hop_send(1, h + 1, piece).start()
+
+        @pl.when(piece == PIECES - 1)
+        def _():
+            share_send(around(-h)).start()
+            share_send(around(h)).start()
+
+    def gather_last():
+        for piece in range(PIECES):
+            hop_recv(2 * piece // PIECES, N, piece).wait_recv()
+        share_send(around(N)).start()
 
     def gather_sent():
         for h in range(1, N + 1):
-            for piece in range(2):
+            for piece in range(PIECES):
                 for d in range(2):
-                    if h < N or piece == d:
+                    if h < N or 2 * piece // PIECES == d:
                         hop_send(d, h, piece).wait_send()
 
         def shared(where, carry):
@@ -215,42 +213,55 @@
 
     query_ids = ids(lax.broadcasted_iota(jnp.int32, (1, T), 1) + chip * T, -1)
 
-    def set_bias(where):
+    def score_bias(where):
         key_ids = ids(lax.broadcasted_iota(jnp.int32, (T, 1), 0) + chip_at(where) * T, -2)
-        n.bias[...] = jnp.where(key_ids == query_ids, 0.0, MASKED)
+        found = jnp.where(key_ids == query_ids, 0.0, MASKED)
+        return jnp.concatenate([found, found], axis=1)
 
     lane = lax.broadcasted_iota(jnp.int32, (T, 2 * HEAD), 1)
 
     def head_masked(values, target):
         for pair in range(pairs):
             both = values[:, 2 * HEAD * pair : 2 * HEAD * (pair + 1)]
-            target[2 * pair] = jnp.where(lane < HEAD, both, 0.0).astype(BF16)
-            target[2 * pair + 1] = jnp.where(lane < HEAD, 0.0, both).astype(BF16)
+            target[pair, :T] = jnp.where(lane < HEAD, both, 0.0).astype(BF16)
+            target[pair, T:] = jnp.where(lane < HEAD, 0.0, both).astype(BF16)
+
+    def of_pair(j):
+        return slice(T * (j % 2), T * (j % 2 + 1))
+
+    def of_head(j):
+        return slice(HEAD * j, HEAD * (j + 1))
 
     def key_rows(where):
         return pl.ds(pl.multiple_of(where * T, T), T)
 
     def forward_block(where):
         xk = xa[where]
-        keys = nn(xk, n.wk[...]).astype(BF16)
-        n.ka[key_rows(where), :] = keys
+        both = nn(xk, n.wkv[...])
+        keys = both[:, :DH].astype(BF16)
+        scores = [nt(keys[:, 2 * HEAD * p : 2 * HEAD * (p + 1)], n.qm[p]) for p in range(pairs)]
+        n.kva[key_rows(where), :DH] = keys
         if roomy:
             n.kt[:, key_rows(where)] = keys.T
-        values = (nn(xk, n.wv[...]) + n.vec[V_BIAS : V_BIAS + 1, pl.ds(half_d, DH)]).astype(BF16)
-        n.va[key_rows(where), :] = values
+        values = (both[:, DH:] + n.vec[V_BIAS : V_BIAS + 1, pl.ds(half_d, DH)]).astype(BF16)
+        n.kva[key_rows(where), DH:] = values
         values_t = values.T
-        set_bias(where)
+        n.xt[:, key_rows(where)] = xk.T
+        bias = score_bias(where)
+        weights, factors = [], []
+        for p in range(pairs):
+            st = scores[p] + bias
+            top = n.top[p]
+            new_top = jnp.maximum(top, jnp.max(st, axis=0, keepdims=True))
+            found = jnp.exp(st - new_top)
+            factors.append(jnp.exp(top - new_top))
+            n.tot[p] = n.tot[p] * factors[p] + jnp.sum(found, axis=0, keepdims=True)
+            n.top[p] = new_top
+            weights.append(found.astype(BF16))
         for j in range(heads):
-            pair = j // 2
-            st = nt(keys[:, 2 * HEAD * pair : 2 * HEAD * (pair + 1)], n.qm[j]) + n.bias[...]
-            top = n.top[j : j + 1]
-            new_top = jnp.maximum(top, jnp.max(st, axis=0, keepdims=True))
-            weights = jnp.exp(st - new_top)
-            factor = jnp.exp(top - new_top)
-            n.tot[j : j + 1] = n.tot[j : j + 1] * factor + jnp.sum(weights, axis=0, keepdims=True)
-            n.top[j : j + 1] = new_top
-            span = slice(HEAD * j, HEAD * (j + 1))
-            n.ot[span] = n.ot[span] * factor + nn(values_t[span], weights.astype(BF16))
+            n.ot[of_head(j)] = n.ot[of_head(j)] * factors[j // 2][:, of_pair(j)] + nn(
+                values_t[of_head(j)], weights[j // 2][:, of_pair(j)]
+            )
 
     n.top[...] = jnp.full(n.top.shape, NEGATIVE, F32)
     n.tot[...] = jnp.zeros(n.tot.shape, F32)
@@ -265,12 +276,12 @@
     head_masked(queries.astype(F32) * 0.125, n.qm)
 
     def forward_step(step, carry):
-        gather_step(step)
-
-        @pl.when(step != 1)
+        h, piece = 1 + step // PIECES, lax.rem(step, PIECES)
+        gather_step(h, piece)
+
+        @pl.when((step == 0) | ((h > 1) & (piece < 2)))
         def _():
-            index = jnp.maximum(step - 1, 0)
-            where = around((index + 1) // 2 * (1 - 2 * lax.rem(index, 2)))
+            where = around((h - 1) * (2 * piece - 1))
 
             @pl.when(step > 0)
             def _():
@@ -280,21 +291,26 @@
 
         return carry
 
-    lax.fori_loop(0, 2 * N + 1, forward_step, 0)
-
-    def turn_block(where, carry):
-        n.xt[:, key_rows(where)] = xa[where].T
+    lax.fori_loop(0, PIECES * (N - 1), forward_step, 0)
+
+    def forward_last(step, carry):
+        where = around((N - 1) * (2 * step - 1) - lax.div(step, 2) * (2 * N - 3))
+
+        @pl.when(step == 2)
+        def _():
+            gather_last()
+
+        share_recv(where).wait_recv()
+        forward_block(where)
         return carry
 
-    def turn_blocks(first, last):
-        lax.fori_loop(first, last, turn_block, 0)
+    lax.fori_loop(0, 3, forward_last, 0)
 
     gather_sent()
     safe = jnp.where(n.tot[...] > 0.5, n.tot[...], 1.0)
     n.lse[...] = n.top[...] + jnp.log(safe)
     for j in range(heads):
-        span = slice(HEAD * j, HEAD * (j + 1))
-        n.ot[span] = n.ot[span] / safe[j : j + 1]
+        n.ot[of_head(j)] = n.ot[of_head(j)] / safe[j // 2][:, of_pair(j)]
 
     def swap(index, src, dst, landed):
         send, recv = n.m_send.at[index], n.m_recv.at[index]
@@ -315,7 +331,6 @@
     other_half = pl.ds(pl.multiple_of((1 - core) * DH, DH), DH)
     obt[own_half] = n.ot[...].astype(BF16)
     swapped = swap(0, obt.at[own_half], obt.at[own_half], obt.at[other_half])
-    turn_blocks(0, C // 8)
     loads[3].wait()
     swapped.wait_recv()
 
@@ -335,7 +350,6 @@
     xbm = n.xbm
     lent_xb = lend(0, xb.at[pl.ds(own_rows, F)], xbm.at[pl.ds(own_rows, F)], mate, xbm.at[pl.ds(own_rows, F)])
     xb_lent = started[-1]
-    turn_blocks(C // 8, 3 * C // 8)
     loads[4].wait()
     swapped.wait_recv()
 
@@ -356,7 +370,7 @@
             for half in range(2):
                 first = CD * c + CD // 2 * half
                 acto[t * (DH // CD) + c, half] = turned[first : first + CD // 2]
-        slope[:, cols] = tangent.astype(slope.dtype)
+        slope[:, cols] = tangent
         return carry
 
     lax.fori_loop(0, FH // DH, up_tile, 0)
@@ -377,7 +391,6 @@
     part_copy = started[-1]
     lent_xb.wait_recv()
     swapped_xbm = swap(8, xbm.at[pl.ds(own_rows, F)], xbm.at[pl.ds(own_rows, F)], xbm.at[pl.ds(other_rows, F)])
-    turn_blocks(3 * C // 8, 4 * C // 8)
     n.xbt[...] = xb[...].T
     upstream = n.cot[...].astype(F32)
     small[SHIFT2 : SHIFT2 + 1] = jnp.sum(upstream, axis=0, keepdims=True)
@@ -415,7 +428,6 @@
         )
     small[GAIN2 : GAIN2 + 1] = jnp.sum(upstream * second_normal, axis=0, keepdims=True)
     small[DOWN_BIAS : DOWN_BIAS + 1] = jnp.sum(low.astype(F32), axis=0, keepdims=True)
-    turn_blocks(4 * C // 8, 7 * C // 8)
     swapped.wait_recv()
 
     class Flow:
@@ -486,7 +498,7 @@
 
     def hidden_tile(t, carry):
         cols = pl.ds(pl.multiple_of(t * TILE, TILE), TILE)
-        low = (nt(df[...], n.wd[cols, :]) * slope[:, cols].astype(F32)).astype(BF16)
+        low = (nt(df[...], n.wd[cols, :]) * slope[:, cols]).astype(BF16)
         du[:, cols] = low
         small[
             pl.ds(UP_BIAS + core * (FH // D) + t // (D // TILE), 1),
@@ -509,7 +521,6 @@
     swapped = swap(5, part.at[pl.ds(other_rows, F)], part_in, part_in)
     part_copy = started[-1]
 
-    turn_blocks(7 * C // 8, C)
     swapped.wait_recv()
     grad_normed = n.grad_x[...] + part[pl.ds(own_rows, F)] + part_in[...]
     normal = n.n1[...]
@@ -535,8 +546,7 @@
     head_masked(grad_mixed, n.dm)
     grad_mixed_t = grad_mixed.T
     for j in range(heads):
-        span = slice(HEAD * j, HEAD * (j + 1))
-        n.delta[j : j + 1] = jnp.sum(grad_mixed_t[span] * n.ot[span], axis=0, keepdims=True)
+        n.delta[j // 2, :, of_pair(j)] = jnp.sum(grad_mixed_t[of_head(j)] * n.ot[of_head(j)], axis=0, keepdims=True)
 
     def grad_down():
         swapped_act.wait_recv()
@@ -566,39 +576,46 @@
 
         lax.fori_loop(0, FH // 2 // TILE, tile, 0)
 
-    def grad_attention(index, left, right):
+    def grad_attention(indices, left, right):
         for t in range(2):
             found = nn(left(pl.ds(DH * t, DH)), right)
-            for c in range(DH // CR):
-                for half in range(2):
-                    first = CR * c + CR // 2 * half
-                    n.ap[DH // CR * t + c, half, index] = found[first : first + CR // 2].astype(BF16)
+            for k, index in enumerate(indices):
+                for c in range(DH // CR):
+                    for half in range(2):
+                        first = CR * c + CR // 2 * half
+                        n.ap[DH // CR * t + c, half, index] = found[
+                            first : first + CR // 2, DH * k : DH * (k + 1)
+                        ].astype(BF16)
 
     n.dqt[...] = jnp.zeros(n.dqt.shape, F32)
     n.vsum[...] = jnp.zeros(n.vsum.shape, F32)
 
     def backward_block(where):
         rows = key_rows(where)
-        set_bias(where)
-        for pair in range(pairs):
-            cols = slice(2 * HEAD * pair, 2 * HEAD * (pair + 1))
-            keys, values = n.ka[rows, cols], n.va[rows, cols]
-            grad_key, grad_value = 0.0, 0.0
-            keys_t = n.kt[cols, rows] if roomy else keys.T
-            for j in (2 * pair, 2 * pair + 1):
-                st = nt(keys, n.qm[j]) + n.bias[...]
-                probs = jnp.exp(st - n.lse[j : j + 1])
-                grad_probs = nt(values, n.dm[j])
-                grad_scores = (probs * (grad_probs - n.delta[j : j + 1])).astype(BF16)
-                grad_value = grad_value + nn(probs.astype(BF16), n.dm[j])
-                grad_key = grad_key + nn(grad_scores, n.qm[j])
-                span = slice(HEAD * j, HEAD * (j + 1))
-                n.dqt[span] += nn(keys_t[HEAD * (j % 2) : HEAD * (j % 2 + 1)], grad_scores)
-            n.ka[rows, cols] = grad_key.astype(BF16)
-            low = grad_value.astype(BF16)
-            n.va[rows, cols] = low
-            n.vsum[:, cols] += jnp.sum(low.astype(F32), axis=0, keepdims=True)
-        return nt(n.ka[rows], n.wk[...]) + nt(n.va[rows], n.wv[...])
+        bias = score_bias(where)
+        keys_t = n.kt[:, rows] if roomy else n.kva[rows, :DH].T
+
+        def wide(p, first=0):
+            return slice(first + 2 * HEAD * p, first + 2 * HEAD * (p + 1))
+
+        def long(p):
+            return slice(2 * T * p, 2 * T * (p + 1))
+
+        for p in range(pairs):
+            n.slope[:, long(p)] = nt(n.kva[rows, wide(p)], n.qm[p])
+            n.grad_probs[:, long(p)] = nt(n.kva[rows, wide(p, DH)], n.dm[p])
+        for p in range(pairs):
+            probs = jnp.exp(n.slope[:, long(p)] + bias - n.lse[p])
+            n.probs[:, long(p)] = probs.astype(BF16)
+            n.grad_scores[:, long(p)] = (probs * (n.grad_probs[:, long(p)] - n.delta[p])).astype(BF16)
+        for p in range(pairs):
+            low = nn(n.probs[:, long(p)], n.dm[p]).astype(BF16)
+            n.kva[rows, wide(p, DH)] = low
+            n.kva[rows, wide(p)] = nn(n.grad_scores[:, long(p)], n.qm[p]).astype(BF16)
+            n.vsum[:, wide(p)] += jnp.sum(low.astype(F32), axis=0, keepdims=True)
+        for j in range(heads):
+            n.dqt[of_head(j)] += nn(keys_t[of_head(j)], n.grad_scores[:, T * j : T * (j + 1)])
+        return nt(n.kva[rows], n.wkv[...])
 
     def cross(where):
         send, recv = n.c_send.at[where], n.c_recv.at[where]
@@ -625,6 +642,46 @@
     flow_d.begin()
     join(around(N))
     flow_x.begin()
+
+    def down_end():
+        n.fd[...] = flow_d.end().astype(n.fd.dtype)
+        spread(0, n.fd, n.yd)
+
+    def up_end():
+        found = flow_u.end()
+        for c in range(2):
+            n.fu[c] = found[CR // 2 * c : CR // 2 * (c + 1)].astype(n.fu.dtype)
+        scatter(1, n.fu, n.yu, True)
+
+    def input_step(distance):
+        join(around(distance))
+        join(around(-distance))
+        flow_x.step(distance)
+
+    def input_end():
+        join(pos)
+        n.grad_x[...] = n.x1[...] + flow_x.end()
+
+    def attention_begin():
+        lent_out.wait_recv()
+        flow_a.begin()
+
+    def attention_end():
+        n.fa[...] = flow_a.end().astype(n.fa.dtype)
+        spread(2, n.fa, n.ya)
+
+    def chain(step, end):
+        return [functools.partial(step, distance) for distance in range(N - 1, 0, -1)] + [end]
+
+    chain_d = chain(flow_d.step, down_end)
+    chain_u = chain(flow_u.step, up_end)
+    chain_x = chain(input_step, input_end)
+    chain_a = [attention_begin] + chain(flow_a.step, attention_end)
+
+    def advance(one):
+        if one:
+            one.pop(0)()
+
     for distance in range(N - 1, 0, -1):
 
         def two_keys(i, carry, distance=distance):
@@ -634,31 +691,15 @@
         lax.fori_loop(0, 2, two_keys, 0)
         start(cross(around(distance)))
         start(cross(around(-distance)))
-        if distance == N - 1:
+        if distance < N - 1:
+            advance(chain_x)
+        if distance == N - 2:
             grad_up()
             flow_u.begin()
-            grad_attention(3, lambda rows: obt[rows], da[:, pl.ds(half_d, DH)])
+            grad_attention([3], lambda rows: obt[rows], da[:, pl.ds(half_d, DH)])
             lent_out = lend(5, n.ap.at[:, 1 - parity, 3], n.am.at[:, 3], mate, n.am.at[:, 3])
-        join(around(distance))
-        join(around(-distance))
-        flow_x.step(distance)
-
-    feed_steps = list(range(N - 1, -1, -1))
-
-    def feed_step():
-        if not feed_steps:
-            return
-        distance = feed_steps.pop(0)
-        if distance > 0:
-            flow_d.step(distance)
-            flow_u.step(distance)
-        else:
-            n.fd[...] = flow_d.end().astype(n.fd.dtype)
-            spread(0, n.fd, n.yd)
-            found = flow_u.end()
-            for c in range(2):
-                n.fu[c] = found[CR // 2 * c : CR // 2 * (c + 1)].astype(n.fu.dtype)
-            scatter(1, n.fu, n.yu, True)
+        if distance >= N - 2:
+            advance(chain_d)
 
     def query_part():
         grad_query = (n.dqt[...] * 0.125).T.astype(BF16)
@@ -667,18 +708,17 @@
 
     key_block(pos, query_part)
     start(cross(pos))
+    advance(chain_u)
     small[Q_BIAS : Q_BIAS + 1, pl.ds(half_d, DH)] = jnp.sum(n.dq[...].astype(F32), axis=0, keepdims=True)
     small[V_BIAS : V_BIAS + 1, pl.ds(half_d, DH)] = n.vsum[...]
     small_swap = swap(7, small, small, n.small.at[1 - core])
 
-    grad_attention(0, lambda rows: n.xt[rows, key_rows(pos)], n.dq[...])
-    grad_attention(1, lambda rows: n.xt[rows], n.ka[...])
-    grad_attention(2, lambda rows: n.xt[rows], n.va[...])
+    grad_attention([0], lambda rows: n.xt[rows, key_rows(pos)], n.dq[...])
+    grad_attention([1, 2], lambda rows: n.xt[rows], n.kva[...])
     for distance in range(N, -1, -1):
         for where in [around(distance)] + ([around(-distance)] if 0 < distance < N else []):
             start(lent_chunk(chip_at(where)))
 
-    feed_step()
     small_swap.wait_recv()
     around_small = n.small_ring
     mine = pl.ds(pl.multiple_of(core * 8, 8), 8)
@@ -748,32 +788,28 @@
             else:
                 copy.wait_send()
 
-    feed_step()
-    lent_out.wait_recv()
-    flow_a.begin()
-    feed_step()
-    join(pos)
-    n.grad_x[...] = n.x1[...] + flow_x.end()
-
-    for h in range(1, N + 1):
+    def small_step(h):
         small_recv(0, h).wait_recv()
         if h < N:
             small_recv(1, h).wait_recv()
             start(small_send(0, h + 1))
             if h + 1 < N:
                 start(small_send(1, h + 1))
-        if h < N:
-            flow_a.step(N - h)
-            feed_step()
-    found = around_small[0]
-    for where in range(1, C):
-        found = found + around_small[where]
-    n.fs[...] = found
-    scatter(3, n.fs, n.ys, False)
-    n.fa[...] = flow_a.end().astype(n.fa.dtype)
-    spread(2, n.fa, n.ya)
-    while feed_steps:
-        feed_step()
+
+    def small_end():
+        found = around_small[0]
+        for where in range(1, C):
+            found = found + around_small[where]
+        n.fs[...] = found
+        scatter(3, n.fs, n.ys, False)
+
+    chain_s = [functools.partial(small_step, h) for h in range(1, N + 1)] + [small_end]
+    while chain_d or chain_x or chain_a or chain_u or chain_s:
+        advance(chain_d)
+        advance(chain_x)
+        advance(chain_a)
+        advance(chain_u)
+        advance(chain_s)
     spread_done(0, n.fd, n.yd)
     collect(1, n.fu, n.yu, True)
     collect(3, n.fs, n.ys, False)
@@ -907,23 +943,23 @@
     dma = pltpu.SemaphoreType.DMA
     scratch = dict(
         wq=pltpu.VMEM((D, DH), BF16),
-        wk=pltpu.VMEM((D, DH), BF16),
-        wv=pltpu.VMEM((D, DH), BF16),
+        wkv=pltpu.VMEM((D, D), BF16),
         wo=pltpu.VMEM((D, D), BF16),
         wu=pltpu.VMEM((D, FH), BF16),
         wd=pltpu.VMEM((FH, D), BF16),
         xa=pltpu.VMEM((C, T, D), BF16),
         xt=pltpu.VMEM((D, keys), BF16),
-        ka=pltpu.VMEM((keys, DH), BF16),
-        va=pltpu.VMEM((keys, DH), BF16),
-        bias=pltpu.VMEM((T, T), F32),
-        qm=pltpu.VMEM((heads, T, 2 * HEAD), BF16),
-        dm=pltpu.VMEM((heads, T, 2 * HEAD), BF16),
+        kva=pltpu.VMEM((keys, D), BF16),
+        qm=pltpu.VMEM((heads // 2, 2 * T, 2 * HEAD), BF16),
+        dm=pltpu.VMEM((heads // 2, 2 * T, 2 * HEAD), BF16),
+        grad_probs=pltpu.VMEM((T, heads * T), F32),
+        probs=pltpu.VMEM((T, heads * T), BF16),
+        grad_scores=pltpu.VMEM((T, heads * T), BF16),
         vec=pltpu.VMEM((8 + FF // D, D), F32),
-        top=pltpu.VMEM((8, T), F32),
-        tot=pltpu.VMEM((8, T), F32),
-        lse=pltpu.VMEM((8, T), F32),
-        delta=pltpu.VMEM((8, T), F32),
+        top=pltpu.VMEM((heads // 2, 1, 2 * T), F32),
+        tot=pltpu.VMEM((heads // 2, 1, 2 * T), F32),
+        lse=pltpu.VMEM((heads // 2, 1, 2 * T), F32),
+        delta=pltpu.VMEM((heads // 2, 1, 2 * T), F32),
         ot=pltpu.VMEM((DH, T), F32),
         dqt=pltpu.VMEM((DH, T), F32),
         dq=pltpu.VMEM((T, DH), BF16),
@@ -941,7 +977,7 @@
         xmt=pltpu.VMEM((D, T), BF16),
         dfm=pltpu.VMEM((T, DH), BF16),
         dum=pltpu.VMEM((T, FH // 2), BF16),
-        slope=pltpu.VMEM((T, FH), F32 if C <= 8 else BF16),
+        slope=pltpu.VMEM((T, FH), F32),
         part=pltpu.VMEM((T, D), F32),
         part_in=pltpu.VMEM((F, D), F32),
         gd_sum=pltpu.VMEM((C, CD // 2, DH), BF16),
@@ -960,8 +996,8 @@
         small_ring=pltpu.VMEM((C, 8, D), F32),
         fs=pltpu.VMEM((8, D), F32),
         load_sem=dma((6,)),
-        g_send=dma((2, N, 2)),
-        g_recv=dma((2, N, 2)),
+        g_send=dma((2, N, PIECES)),
+        g_recv=dma((2, N, PIECES)),
         s_send=dma((C,)),
         s_recv=dma((C,)),
         m_send=dma((10,)),

time: 130 us -> 116 us (0.89)
  Pallas kernels: 129 us -> 115 us
    pallas_call x1, Pallas kernels: 126 us -> 112 us  [on_device(): pl.pallas_call(functools.partial(layer_kernel, names, S, R), out_shape=[j...]
where the time goes in v2:
time: 116 us
  Pallas kernels  115 us (99%)
    pallas_call x1, Pallas kernels, on_device(): pl.pallas_call(functools.partial(layer_kernel, names, S, R), out_shape=[j...  112 us
    pallas_call x1, Pallas kernels, on_device(): pl.pallas_call(finish_kernel, out_shape=[jax.ShapeDtypeStruct(shape, kind...  2.82 us

profile of v2, /device:TPU:0, one launch (start us, length us, event | category | flops | bytes accessed | tf_op | source)
XLA Modules:
  0.0 115.6 jit_solution(17466938480917069515)
XLA Ops:
  0.7 111.9 %layer.1 = (bf16[128,768]{1,0:T(8,128)(2,1)}, f32[128,768]{1,0:T(8,128)}, bf16[1,2,192,384]{3,2,1,0:T(8,128)(2,1)}, bf16[2,2,48,768]{3,2,1,0:T(8,128)(2,1)}, bf1...) custom-call(bf16[128,768]{1,0:T(8,128)(2,1)} %bitcast.4, bf16[128,768]{1,0:T(8,128)(2,1)} %bitcast.5, ...), custom_call_target="tpu_custom_call" | custom-call | tf_op jit(solution)/shard_map/layer/pallas_call | solution.py:1021
  112.6 2.8 %finish.1 = (bf16[128,768]{1,0:T(8,128)(2,1)}, f32[128,768]{1,0:T(8,128)}, f32[48,768]{1,0:T(8,128)}, f32[48]{0:T(128)}, f32[48,768]{1,0:T(8,128)}, /*index=5*/f...) custom-call(bf16[128,768]{1,0:T(8,128)(2,1)} %get-tuple-element.40.o, ...), custom_call_target="tpu_custom_call" | custom-call | tf_op jit(solution)/shard_map/finish/pallas_call | solution.py:1035

commit v3 on v2

--- a/solution.py
+++ b/solution.py
@@ -103,6 +103,11 @@
         copy.start()
         started.append(copy)
 
+    barrier = pltpu.get_barrier_semaphore()
+    partners = [right, left] + [(2 * chip + c, r) for r, c in others]
+    for device in partners:
+        pl.semaphore_signal(barrier, inc=1, device_id=device, device_id_type=MESH)
+
     half_d = pl.multiple_of(core * DH, 128)
     half_f = pl.multiple_of(core * FH, 128)
     loads = []
@@ -117,79 +122,10 @@
         loads.append(pltpu.make_async_copy(source, target, n.load_sem.at[len(loads)]))
         loads[-1].start()
 
-    barrier = pltpu.get_barrier_semaphore()
-    partners = [right, left] + [(2 * chip + c, r) for r, c in others]
-    for device in partners:
-        pl.semaphore_signal(barrier, inc=1, device_id=device, device_id_type=MESH)
-    pl.semaphore_wait(barrier, len(partners))
-
     xa = n.xa
     own_rows = pl.multiple_of(core * F, F)
     other_rows = pl.multiple_of((1 - core) * F, F)
     xa[pos, pl.ds(own_rows, F)] = n.x[...]
-
-    step_rows = F // PIECES
-
-    def hop_view(where, piece):
-        return xa.at[where, pl.ds(pl.multiple_of(own_rows + piece * step_rows, step_rows), step_rows)]
-
-    def hop_send(d, h, piece):
-        view = hop_view(around((h - 1) * (2 * d - 1)), piece)
-        return remote(view, view, n.g_send.at[d, h - 1, piece], n.g_recv.at[d, h - 1, piece], ring[d])
-
-    def hop_recv(d, h, piece):
-        view = hop_view(around(h * (2 * d - 1)), piece)
-        return remote(view, view, n.g_send.at[d, h - 1, piece], n.g_recv.at[d, h - 1, piece], ring[d])
-
-    def share_send(where):
-        view = xa.at[where, pl.ds(own_rows, F)]
-        return remote(view, view, n.s_send.at[where], n.s_recv.at[where], sibling)
-
-    def share_recv(where):
-        view = xa.at[where, pl.ds(other_rows, F)]
-        return remote(view, view, n.s_send.at[where], n.s_recv.at[where], sibling)
-
-    for piece in range(PIECES):
-        hop_send(0, 1, piece).start()
-        hop_send(1, 1, piece).start()
-        if piece == 0:
-            share_send(pos).start()
-
-    def gather_step(h, piece):
-        hop_recv(0, h, piece).wait_recv()
-        hop_recv(1, h, piece).wait_recv()
-
-        @pl.when((h < N - 1) | (piece < PIECES // 2))
-        def _():
-            hop_send(0, h + 1, piece).start()
-
-        @pl.when((h < N - 1) | (piece >= PIECES // 2))
-        def _():
-            hop_send(1, h + 1, piece).start()
-
-        @pl.when(piece == PIECES - 1)
-        def _():
-            share_send(around(-h)).start()
-            share_send(around(h)).start()
-
-    def gather_last():
-        for piece in range(PIECES):
-            hop_recv(2 * piece // PIECES, N, piece).wait_recv()
-        share_send(around(N)).start()
-
-    def gather_sent():
-        for h in range(1, N + 1):
-            for piece in range(PIECES):
-                for d in range(2):
-                    if h < N or 2 * piece // PIECES == d:
-                        hop_send(d, h, piece).wait_send()
-
-        def shared(where, carry):
-            share_send(where).wait_send()
-            return carry
-
-        lax.fori_loop(0, C, shared, 0)
-
     for index, vector in enumerate(
         (n.bias_q, n.bias_v, n.bias_o, n.gain1, n.shift1, n.bias_d, n.gain2, n.shift2)
     ):
@@ -198,6 +134,63 @@
         n.vec[UP_BIAS + index : UP_BIAS + index + 1] = (
             n.bias_u[D * index : D * (index + 1)].astype(F32).reshape(1, D)
         )
+    pl.semaphore_wait(barrier, len(partners))
+
+    step_rows = F // PIECES
+
+    def hop_view(where, piece):
+        return xa.at[where, pl.ds(pl.multiple_of(own_rows + piece * step_rows, step_rows), step_rows)]
+
+    def hop_send(d, h, turn):
+        view = hop_view(around((h - 1) * (2 * d - 1)), lax.rem(turn + d * (PIECES // 2), PIECES))
+        return remote(view, view, n.g_send.at[d, turn], n.g_recv.at[d, h - 1, turn], ring[d])
+
+    def hop_recv(d, h, turn):
+        view = hop_view(around(h * (2 * d - 1)), lax.rem(turn + d * (PIECES // 2), PIECES))
+        return remote(view, view, n.g_send.at[d, turn], n.g_recv.at[d, h - 1, turn], ring[d])
+
+    def share_send(where, d=0):
+        view = xa.at[where, pl.ds(own_rows, F)]
+        return remote(view, view, n.s_send.at[d], n.s_recv.at[where], sibling)
+
+    def share_recv(where):
+        view = xa.at[where, pl.ds(other_rows, F)]
+        return remote(view, view, n.s_send.at[0], n.s_recv.at[where], sibling)
+
+    for turn in range(PIECES):
+        hop_send(0, 1, turn).start()
+        hop_send(1, 1, turn).start()
+        if turn == 0:
+            share_send(pos).start()
+
+    def gather_step(h, turn):
+        for d in range(2):
+            hop_recv(d, h, turn).wait_recv()
+            hop_send(d, h, turn).wait_send()
+
+        @pl.when((h < N - 1) | (turn < PIECES // 2))
+        def _():
+            hop_send(0, h + 1, turn).start()
+            hop_send(1, h + 1, turn).start()
+
+        @pl.when(turn == PIECES - 1)
+        def _():
+            share_send(pos, 0).wait_send()
+            pl.when(h > 1)(share_send(pos, 1).wait_send)
+            share_send(around(-h), 0).start()
+            share_send(around(h), 1).start()
+
+    def gather_last():
+        for turn in range(PIECES // 2):
+            for d in range(2):
+                hop_recv(d, N, turn).wait_recv()
+                hop_send(d, N, turn).wait_send()
+        share_send(pos, 0).wait_send()
+        share_send(around(N), 0).start()
+
+    def gather_sent():
+        share_send(pos, 0).wait_send()
+        share_send(pos, 1).wait_send()
 
     ends = []
     total = 0
@@ -276,12 +269,12 @@
     head_masked(queries.astype(F32) * 0.125, n.qm)
 
     def forward_step(step, carry):
-        h, piece = 1 + step // PIECES, lax.rem(step, PIECES)
-        gather_step(h, piece)
-
-        @pl.when((step == 0) | ((h > 1) & (piece < 2)))
+        h, turn = 1 + step // PIECES, lax.rem(step, PIECES)
+        gather_step(h, turn)
+
+        @pl.when((step == 0) | ((h > 1) & (turn < 2)))
         def _():
-            where = around((h - 1) * (2 * piece - 1))
+            where = around((h - 1) * (2 * turn - 1))
 
             @pl.when(step > 0)
             def _():
@@ -296,7 +289,7 @@
     def forward_last(step, carry):
         where = around((N - 1) * (2 * step - 1) - lax.div(step, 2) * (2 * N - 3))
 
-        @pl.when(step == 2)
+        @pl.when(step == 1)
         def _():
             gather_last()
 
@@ -321,6 +314,13 @@
         recv_index = index if recv_index is None else recv_index
         start(remote(src, dst, n.y_send.at[index], n.y_recv.at[recv_index], device))
         return remote(src, landed, n.y_send.at[index], n.y_recv.at[index], device)
+
+    def deliver(src, dst, index):
+        copy = pltpu.make_async_copy(src, dst, n.out_sem.at[index])
+        copy.start()
+        delivered.append(copy)
+
+    delivered = []
 
     def sent(copy):
         started[:] = [other for other in started if other is not copy]
@@ -332,13 +332,13 @@
     obt[own_half] = n.ot[...].astype(BF16)
     swapped = swap(0, obt.at[own_half], obt.at[own_half], obt.at[other_half])
     loads[3].wait()
+    branch = nn(obt[own_half, pl.ds(own_rows, F)].T, n.wo[own_half])
     swapped.wait_recv()
 
     def vec(index):
         return n.vec[index : index + 1]
 
-    mixed = obt[:, pl.ds(own_rows, F)].T
-    branch = nn(mixed, n.wo[...]) + vec(OUT_BIAS)
+    branch = branch + nn(obt[other_half, pl.ds(own_rows, F)].T, n.wo[other_half]) + vec(OUT_BIAS)
     first_normal, first_scale = norm_parts(n.x[...].astype(F32) + branch)
     n.n1[...] = first_normal
     normed = first_normal * vec(GAIN1) + vec(SHIFT1)
@@ -346,61 +346,59 @@
     xb = n.xb
     xb[pl.ds(own_rows, F)] = normed.astype(BF16)
     swapped = swap(1, xb.at[pl.ds(own_rows, F)], xb.at[pl.ds(own_rows, F)], xb.at[pl.ds(other_rows, F)])
-    xb_copy = started[-1]
     xbm = n.xbm
     lent_xb = lend(0, xb.at[pl.ds(own_rows, F)], xbm.at[pl.ds(own_rows, F)], mate, xbm.at[pl.ds(own_rows, F)])
-    xb_lent = started[-1]
     loads[4].wait()
-    swapped.wait_recv()
 
     act, slope = n.act, n.slope
     acto, att = n.acto, n.att
     du = act
 
-    def up_tile(t, carry):
-        cols = pl.ds(pl.multiple_of(t * DH, DH), DH)
-        bias = n.vec[
-            pl.ds(UP_BIAS + core * (FH // D) + t // 2, 1), pl.ds(pl.multiple_of(lax.rem(t, 2) * DH, DH), DH)
-        ]
-        value, tangent = gelu_parts(nn(xb[...], n.wu[:, cols]) + bias)
-        low = value.astype(BF16)
-        act[:, cols] = low
-        turned = low.T
-        for c in range(DH // CD):
-            for half in range(2):
-                first = CD * c + CD // 2 * half
-                acto[t * (DH // CD) + c, half] = turned[first : first + CD // 2]
-        slope[:, cols] = tangent
-        return carry
-
-    lax.fori_loop(0, FH // DH, up_tile, 0)
+    def up_rows(rows):
+        for t in range(FH // D):
+            cols = slice(D * t, D * (t + 1))
+            bias = n.vec[pl.ds(UP_BIAS + core * (FH // D) + t, 1)]
+            value, tangent = gelu_parts(nn(xb[rows], n.wu[:, cols]) + bias)
+            low = value.astype(BF16)
+            act[rows, cols] = low
+            turned = low.T
+            for c in range(D // CD):
+                for half in range(2):
+                    for side in range(2):
+                        first = CD * c + CD // 2 * half + CD // 4 * side
+                        acto[side, D // CD * t + c, half, :, rows] = turned[first : first + CD // 4]
+            slope[rows, cols] = tangent
+
+    up_rows(pl.ds(own_rows, F))
+    swapped.wait_recv()
+    up_rows(pl.ds(other_rows, F))
     own_ff = pl.ds(core * (C // 2), C // 2)
     other_ff = pl.ds((1 - core) * (C // 2), C // 2)
-    lent_act = lend(1, acto.at[:, 1 - parity], att.at[1, own_ff], mate, att.at[1, own_ff])
-    swapped_act = swap(2, acto.at[:, parity], att.at[0, own_ff], att.at[0, other_ff])
+    lent_act = lend(1, acto.at[1, :, 1 - parity], att.at[1, own_ff], mate, att.at[1, own_ff])
+    swapped_first = swap(10, acto.at[0], n.atf.at[own_ff], n.atf.at[other_ff])
+    swapped_act = swap(2, acto.at[1, :, parity], att.at[0, own_ff], att.at[0, other_ff])
+    n.atf[own_ff] = acto[0]
+    att[0, own_ff] = acto[1, :, parity]
     loads[5].wait()
-    part, part_in = n.part, n.part_in
-
-    def down_tile(t, carry):
-        cols = pl.ds(pl.multiple_of(t * TILE, TILE), TILE)
-        part[:, cols] = nn(act[...], n.wd[:, cols])
-        return carry
-
-    lax.fori_loop(0, D // TILE, down_tile, 0)
-    swapped = swap(3, part.at[pl.ds(other_rows, F)], part_in, part_in)
-    part_copy = started[-1]
-    lent_xb.wait_recv()
-    swapped_xbm = swap(8, xbm.at[pl.ds(own_rows, F)], xbm.at[pl.ds(own_rows, F)], xbm.at[pl.ds(other_rows, F)])
+    part = n.part
+
+    def part_swap(index):
+        n.part_out[index] = part[pl.ds(other_rows, F)].astype(BF16)
+        return swap(3 + 2 * index, n.part_out.at[index], n.part_in.at[index], n.part_in.at[index])
+
+    part[...] = nn(act[...], n.wd[...])
+    part_arrives = part_swap(0)
     n.xbt[...] = xb[...].T
     upstream = n.cot[...].astype(F32)
     small[SHIFT2 : SHIFT2 + 1] = jnp.sum(upstream, axis=0, keepdims=True)
-    swapped.wait_recv()
+    part_arrives.wait_recv()
     second_normal, second_scale = norm_parts(
-        n.x1[...] + part[pl.ds(own_rows, F)] + part_in[...] + vec(DOWN_BIAS)
+        n.x1[...] + part[pl.ds(own_rows, F)] + n.part_in[0].astype(F32) + vec(DOWN_BIAS)
     )
-    n.out[...] = (second_normal * vec(GAIN2) + vec(SHIFT2)).astype(BF16)
+    n.out_low[...] = (second_normal * vec(GAIN2) + vec(SHIFT2)).astype(BF16)
+    deliver(n.out_low, n.out, 0)
     residual = norm_back(upstream * vec(GAIN2), second_normal, second_scale)
-    n.grad_x[...] = residual
+    n.dh2[...] = residual
     low = residual.astype(BF16)
     df = n.df
     df[pl.ds(own_rows, F)] = low
@@ -433,20 +431,31 @@
     class Flow:
         def __init__(self, index, chunk, landing, split, ready=None):
             self.index, self.chunk, self.landing, self.split, self.ready = index, chunk, landing, split, ready
+            self.last = [None, None]
 
         def parts(self, d, distance):
             where = around(distance if d == 0 else -distance)
             src, dst = self.chunk(where), self.landing.at[d, distance - 1]
             if distance == N:
                 src, dst = src.at[self.split[d]], dst.at[self.split[d]]
-            send, recv = n.r_send.at[self.index, d, distance - 1], n.r_recv.at[self.index, d, distance - 1]
+            send, recv = n.r_send.at[self.index, d], n.r_recv.at[self.index, d, distance - 1]
             return remote(src, dst, send, recv, ring[d]), dst
+
+        def put(self, d, distance):
+            if distance < N:
+                self.last[d].wait_send()
+            self.last[d] = self.parts(d, distance)[0]
+            self.last[d].start()
+
+        def sent(self):
+            for copy in self.last:
+                copy.wait_send()
 
         def begin(self):
             if self.ready is not None:
                 self.ready(around(N))
-            start(self.parts(0, N)[0])
-            start(self.parts(1, N)[0])
+            self.put(0, N)
+            self.put(1, N)
 
         def step(self, distance):
             for d in range(2):
@@ -459,7 +468,7 @@
                 if distance + 1 == N:
                     target = target.at[self.split[d]]
                 target[...] = (target[...].astype(F32) + landed[...].astype(F32)).astype(BF16)
-                start(self.parts(d, distance)[0])
+                self.put(d, distance)
 
         def end(self):
             if self.ready is not None:
@@ -478,13 +487,16 @@
 
     def lent_chunk(c):
         return remote(
-            n.ap.at[c, 1 - parity, pl.ds(0, 3)], n.am.at[c, pl.ds(0, 3)], n.ya_send.at[c], n.ya_recv.at[c], mate
+            n.ap.at[c, 1 - parity, pl.ds(0, 3)], n.am.at[c, pl.ds(0, 3)], n.ya_send.at[0], n.ya_recv.at[c], mate
         )
 
     whole = slice(None)
-    flow_d = Flow(
-        0, lambda where: n.gd_sum.at[chip_at(where)], n.gd_in, [pl.ds(0, CD // 4), pl.ds(CD // 4, CD // 4)]
-    )
+    if CD % 128 == 0:
+        split_d = [pl.ds(0, CD // 8), pl.ds(CD // 8, CD // 8)]
+    else:
+        split_d = [(whole, pl.ds(0, 128)), (whole, pl.ds(128, DH - 128))]
+    flow_d = Flow(0, lambda where: n.gd_sum.at[chip_at(where)], n.gd_in, split_d)
+    flow_e = Flow(4, lambda where: n.ge_sum.at[chip_at(where)], n.ge_in, [pl.ds(0, 1), pl.ds(1, 1)])
     flow_u = Flow(
         1,
         lambda where: n.gu_sum.at[chip_at(where)],
@@ -496,50 +508,135 @@
     )
     flow_x = Flow(3, lambda where: n.ix_sum.at[where], n.ix_in, [pl.ds(0, F // 2), pl.ds(F // 2, F // 2)])
 
-    def hidden_tile(t, carry):
-        cols = pl.ds(pl.multiple_of(t * TILE, TILE), TILE)
+    def scatter(index, source, gathered, split):
+        deliver(source.at[core] if split else source, gathered.at[row, core], 2 + index)
+        for k, (r, c) in enumerate(others):
+            view = source.at[c] if split else source
+            start(
+                remote(
+                    view,
+                    gathered.at[row, core],
+                    n.f_send.at[index, k],
+                    n.f_recv.at[index, row, core],
+                    (2 * chip + c, r),
+                )
+            )
+
+    def collect(index, source, gathered, split):
+        for r, c in others:
+            view = source.at[c] if split else source
+            remote(
+                view, gathered.at[r, c], n.f_send.at[index, 0], n.f_recv.at[index, r, c], (2 * chip + c, r)
+            ).wait_recv()
+
+    def spread(index, source, gathered):
+        pl.when(core == parity)(spread_own(index, source, gathered).start)
+        for k in range(R):
+            copy = spread_copy(index, source, gathered, k)
+            if k == 0:
+                pl.when(core != parity)(copy.start)
+            else:
+                copy.start()
+
+    def spread_own(index, source, gathered):
+        return pltpu.make_async_copy(source, gathered.at[row // 2, core], n.out_sem.at[2 + index])
+
+    def spread_copy(index, source, gathered, k):
+        device = (2 * chip + parity, lax.rem(row + k, R))
+        return remote(
+            source, gathered.at[row // 2, core], n.f_send.at[index, k], n.f_recv.at[index, row // 2, core], device
+        )
+
+    def spread_done(index, source, gathered):
+        for q in range(R // 2):
+            for c in range(2):
+                arriving = remote(
+                    source, gathered.at[q, c], n.f_send.at[index, 0], n.f_recv.at[index, q, c], sibling
+                )
+                pl.when((2 * q + core != row) | (core != c))(arriving.wait_recv)
+        pl.when(core == parity)(spread_own(index, source, gathered).wait)
+        for k in range(R):
+            copy = spread_copy(index, source, gathered, k)
+            if k == 0:
+                pl.when(core != parity)(copy.wait_send)
+            else:
+                copy.wait_send()
+
+    def down_end():
+        n.fd[...] = flow_d.end().astype(n.fd.dtype)
+        spread(0, n.fd, n.yd)
+
+    def first_end():
+        n.fe[...] = flow_e.end().astype(n.fe.dtype)
+        scatter(4, n.fe, n.ye, True)
+
+    def up_end():
+        found = flow_u.end()
+        for c in range(2):
+            n.fu[c] = found[CR // 2 * c : CR // 2 * (c + 1)].astype(n.fu.dtype)
+        scatter(1, n.fu, n.yu, True)
+
+    def input_step(distance):
+        join(around(distance))
+        join(around(-distance))
+        flow_x.step(distance)
+
+    def input_end():
+        join(pos)
+        n.dh2[...] = n.x1[...] + flow_x.end()
+        deliver(n.dh2, n.grad_x, 1)
+
+    def attention_begin():
+        lent_out.wait_recv()
+        flow_a.begin()
+
+    def attention_end():
+        n.fa[...] = flow_a.end().astype(n.fa.dtype)
+        spread(2, n.fa, n.ya)
+
+    def chain(step, end):
+        return [functools.partial(step, distance) for distance in range(N - 1, 0, -1)] + [end]
+
+    chain_d = chain(flow_d.step, down_end)
+    chain_u = chain(flow_u.step, up_end)
+    chain_e = chain(flow_e.step, first_end)
+    chain_x = chain(input_step, input_end)
+    chain_a = [attention_begin] + chain(flow_a.step, attention_end)
+
+    def advance(one):
+        one.pop(0)()
+
+    swapped_first.wait_recv()
+    for t in range(C // 2):
+        two = slice(2 * t, 2 * t + 2)
+        found = nn(n.atf[two].reshape(CD, T), df[:, pl.ds(half_d, DH)])
+        n.ge_sum[two] = found.astype(BF16).reshape(2, 2, CD // 4, DH)
+    flow_e.begin()
+    for t in range(FH // D):
+        cols = slice(D * t, D * (t + 1))
         low = (nt(df[...], n.wd[cols, :]) * slope[:, cols]).astype(BF16)
         du[:, cols] = low
-        small[
-            pl.ds(UP_BIAS + core * (FH // D) + t // (D // TILE), 1),
-            pl.ds(pl.multiple_of(lax.rem(t, D // TILE) * TILE, TILE), TILE),
-        ] = jnp.sum(low.astype(F32), axis=0, keepdims=True)
-        return carry
-
-    lax.fori_loop(0, tiles, hidden_tile, 0)
+        small[pl.ds(UP_BIAS + core * (FH // D) + t, 1)] = jnp.sum(low.astype(F32), axis=0, keepdims=True)
 
     quarter = pl.multiple_of(parity * (FH // 2), FH // 2)
     other_quarter = pl.multiple_of((1 - parity) * (FH // 2), FH // 2)
     lent_du = lend(4, du.at[:, pl.ds(other_quarter, FH // 2)], n.dum, mate, n.dum)
-    def back_tile(t, carry):
-        cols = pl.ds(pl.multiple_of(t * TILE, TILE), TILE)
-        part[:, cols] = nt(du[...], n.wu[cols, :])
-        return carry
-
-    sent(part_copy)
-    lax.fori_loop(0, D // TILE, back_tile, 0)
-    swapped = swap(5, part.at[pl.ds(other_rows, F)], part_in, part_in)
-    part_copy = started[-1]
-
-    swapped.wait_recv()
-    grad_normed = n.grad_x[...] + part[pl.ds(own_rows, F)] + part_in[...]
+    part[...] = nt(du[...], n.wu[...])
+    part_arrives = part_swap(1)
+
+    part_arrives.wait_recv()
+    grad_normed = n.dh2[...] + part[pl.ds(own_rows, F)] + n.part_in[1].astype(F32)
     normal = n.n1[...]
     small[GAIN1 : GAIN1 + 1] = jnp.sum(grad_normed * normal, axis=0, keepdims=True)
     small[SHIFT1 : SHIFT1 + 1] = jnp.sum(grad_normed, axis=0, keepdims=True)
     grad_branch = norm_back(grad_normed * vec(GAIN1), normal, first_scale)
     n.x1[...] = grad_branch
     low = grad_branch.astype(BF16)
-    sent(xb_copy)
-    sent(xb_lent)
-    da = xb
+    da = n.da
     da[pl.ds(own_rows, F)] = low
     swapped = swap(6, da.at[pl.ds(own_rows, F)], da.at[pl.ds(own_rows, F)], da.at[pl.ds(other_rows, F)])
     small[OUT_BIAS : OUT_BIAS + 1] = jnp.sum(low.astype(F32), axis=0, keepdims=True)
-    swapped_xbm.wait_recv()
-    n.xmt[...] = xbm[...].T
-    lent_act.wait_recv()
-    swapped_actm = swap(9, att.at[1, own_ff], att.at[1, own_ff], att.at[1, other_ff])
-    att[0, own_ff] = acto[:, parity]
+    advance(chain_e)
     swapped.wait_recv()
 
     grad_mixed = nt(da[...], n.wo[own_half]).astype(BF16).astype(F32)
@@ -551,30 +648,29 @@
     def grad_down():
         swapped_act.wait_recv()
         swapped_actm.wait_recv()
+        rows = CD // 2
         for lent in lent_df:
             lent.wait_recv()
-
-        def tile(t, carry):
-            two = pl.ds(2 * t, 2)
-            found = nn(att[0, two].reshape(CD, T), df[:, pl.ds(half_d, DH)])
-            found = found + nn(att[1, two].reshape(CD, T), dfm[...])
-            n.gd_sum[two] = found.astype(BF16).reshape(2, CD // 2, DH)
-            return carry
-
-        lax.fori_loop(0, C // 2, tile, 0)
+        for t in range(C // 2):
+            two = slice(2 * t, 2 * t + 2)
+            found = nn(att[0, two].reshape(rows, T), df[:, pl.ds(half_d, DH)])
+            found = found + nn(att[1, two].reshape(rows, T), dfm[...])
+            n.gd_sum[two] = found.astype(BF16).reshape(2, CD // 4, DH)
+
+    def forward_xb():
+        lent_xb.wait_recv()
+        return swap(8, xbm.at[pl.ds(own_rows, F)], xbm.at[pl.ds(own_rows, F)], xbm.at[pl.ds(other_rows, F)])
 
     def grad_up():
+        swapped_xbm.wait_recv()
+        n.xmt[...] = xbm[...].T
         lent_du.wait_recv()
-
-        def tile(t, carry):
-            cols = pl.ds(pl.multiple_of(t * TILE, TILE), TILE)
+        for t in range(FH // 2 // TILE):
+            cols = slice(TILE * t, TILE * (t + 1))
             found = nn(n.xbt[...], du[:, pl.ds(pl.multiple_of(quarter + t * TILE, TILE), TILE)])
             found = (found + nn(n.xmt[...], n.dum[:, cols])).astype(BF16)
             for c in range(C):
                 n.gu_sum[c, :, cols] = found[CR * c : CR * (c + 1)]
-            return carry
-
-        lax.fori_loop(0, FH // 2 // TILE, tile, 0)
 
     def grad_attention(indices, left, right):
         for t in range(2):
@@ -617,8 +713,16 @@
             n.dqt[of_head(j)] += nn(keys_t[of_head(j)], n.grad_scores[:, T * j : T * (j + 1)])
         return nt(n.kva[rows], n.wkv[...])
 
+    crossing, turn_of_cross = [], [0]
+
+    def put_cross(where):
+        if len(crossing) == 2:
+            crossing.pop(0).wait_send()
+        crossing.append(cross(where))
+        crossing[-1].start()
+
     def cross(where):
-        send, recv = n.c_send.at[where], n.c_recv.at[where]
+        send, recv = n.c_send.at[turn_of_cross[0] % 2], n.c_recv.at[where]
         return remote(xa.at[where, pl.ds(0, F)], xa.at[where, pl.ds(F, F)], send, recv, sibling)
 
     def key_block(where, extra=None):
@@ -635,80 +739,58 @@
             n.ix_sum[where].astype(F32) + xa[where, pl.ds(F, F)].astype(F32)
         ).astype(BF16)
 
-    sent(part_copy)
-    key_block(around(N))
-    start(cross(around(N)))
-    grad_down()
-    flow_d.begin()
-    join(around(N))
-    flow_x.begin()
-
-    def down_end():
-        n.fd[...] = flow_d.end().astype(n.fd.dtype)
-        spread(0, n.fd, n.yd)
-
-    def up_end():
-        found = flow_u.end()
-        for c in range(2):
-            n.fu[c] = found[CR // 2 * c : CR // 2 * (c + 1)].astype(n.fu.dtype)
-        scatter(1, n.fu, n.yu, True)
-
-    def input_step(distance):
-        join(around(distance))
-        join(around(-distance))
-        flow_x.step(distance)
-
-    def input_end():
-        join(pos)
-        n.grad_x[...] = n.x1[...] + flow_x.end()
-
-    def attention_begin():
-        lent_out.wait_recv()
-        flow_a.begin()
-
-    def attention_end():
-        n.fa[...] = flow_a.end().astype(n.fa.dtype)
-        spread(2, n.fa, n.ya)
-
-    def chain(step, end):
-        return [functools.partial(step, distance) for distance in range(N - 1, 0, -1)] + [end]
-
-    chain_d = chain(flow_d.step, down_end)
-    chain_u = chain(flow_u.step, up_end)
-    chain_x = chain(input_step, input_end)
-    chain_a = [attention_begin] + chain(flow_a.step, attention_end)
-
-    def advance(one):
-        if one:
-            one.pop(0)()
-
-    for distance in range(N - 1, 0, -1):
-
-        def two_keys(i, carry, distance=distance):
-            key_block(around((1 - 2 * i) * distance))
-            return carry
-
-        lax.fori_loop(0, 2, two_keys, 0)
-        start(cross(around(distance)))
-        start(cross(around(-distance)))
-        if distance < N - 1:
-            advance(chain_x)
-        if distance == N - 2:
-            grad_up()
-            flow_u.begin()
-            grad_attention([3], lambda rows: obt[rows], da[:, pl.ds(half_d, DH)])
-            lent_out = lend(5, n.ap.at[:, 1 - parity, 3], n.am.at[:, 3], mate, n.am.at[:, 3])
-        if distance >= N - 2:
-            advance(chain_d)
-
     def query_part():
         grad_query = (n.dqt[...] * 0.125).T.astype(BF16)
         n.dq[...] = grad_query
         return nt(grad_query, n.wq[...])
 
-    key_block(pos, query_part)
-    start(cross(pos))
-    advance(chain_u)
+    blocks = [N] + [side * d for d in range(N - 1, 0, -1) for side in (1, -1)] + [0]
+    if N == 4:
+        due = [""] * 8
+        due[0], due[1], due[3], due[4], due[5], due[6], due[7] = "mFD", "e", "x", "ed", "U", "x", "ed"
+        last = "uasuasuasduasxdsax"
+    else:
+        due = ["mFD", "e"] + ["ed"[b % 4 // 2] if b % 2 == 0 else "x" for b in range(2, 2 * N)]
+        due[4] += "U"
+        last = "eaxdus" * (N + 2)
+    chains = dict(e=chain_e, d=chain_d, u=chain_u, x=chain_x, a=chain_a, s=[])
+
+    def begin_input():
+        join(around(N))
+        flow_x.begin()
+
+    def begin_down():
+        grad_down()
+        flow_d.begin()
+
+    def begin_up():
+        nonlocal swapped_xbm, lent_out
+        swapped_xbm = forward_xb()
+        grad_attention([3], lambda rows: obt[rows], da[:, pl.ds(half_d, DH)])
+        lent_out = lend(5, n.ap.at[:, 1 - parity, 3], n.am.at[:, 3], mate, n.am.at[:, 3])
+        grad_up()
+        flow_u.begin()
+
+    def mate_hidden():
+        nonlocal swapped_actm
+        lent_act.wait_recv()
+        swapped_actm = swap(9, att.at[1, own_ff], att.at[1, own_ff], att.at[1, other_ff])
+
+    swapped_xbm = lent_out = swapped_actm = None
+    begins = dict(m=mate_hidden, F=begin_input, D=begin_down, U=begin_up)
+
+    def work(letters):
+        for letter in letters:
+            if letter in begins:
+                begins[letter]()
+            elif chains[letter]:
+                chains[letter].pop(0)()
+
+    for index, step in enumerate(blocks):
+        key_block(around(step), query_part if step == 0 else None)
+        turn_of_cross[0] = index
+        put_cross(around(step))
+        work(due[index])
     small[Q_BIAS : Q_BIAS + 1, pl.ds(half_d, DH)] = jnp.sum(n.dq[...].astype(F32), axis=0, keepdims=True)
     small[V_BIAS : V_BIAS + 1, pl.ds(half_d, DH)] = n.vsum[...]
     small_swap = swap(7, small, small, n.small.at[1 - core])
@@ -717,7 +799,7 @@
     grad_attention([1, 2], lambda rows: n.xt[rows], n.kva[...])
     for distance in range(N, -1, -1):
         for where in [around(distance)] + ([around(-distance)] if 0 < distance < N else []):
-            start(lent_chunk(chip_at(where)))
+            lent_chunk(chip_at(where)).start()
 
     small_swap.wait_recv()
     around_small = n.small_ring
@@ -726,75 +808,30 @@
 
     def small_send(d, h):
         view = around_small.at[around(1 - h if d == 0 else h - 1)]
-        return remote(view, view, n.sr_send.at[d, h - 1], n.sr_recv.at[d, h - 1], ring[d])
+        return remote(view, view, n.sr_send.at[d], n.sr_recv.at[d, h - 1], ring[d])
 
     def small_recv(d, h):
         view = around_small.at[around(-h if d == 0 else h)]
-        return remote(view, view, n.sr_send.at[d, h - 1], n.sr_recv.at[d, h - 1], ring[d])
-
-    start(small_send(0, 1))
-    start(small_send(1, 1))
-
-    def scatter(index, source, gathered, split):
-        gathered[row, core] = source[core] if split else source[...]
-        for k, (r, c) in enumerate(others):
-            view = source.at[c] if split else source
-            start(
-                remote(
-                    view,
-                    gathered.at[row, core],
-                    n.f_send.at[index, k],
-                    n.f_recv.at[index, row, core],
-                    (2 * chip + c, r),
-                )
-            )
-
-    def collect(index, source, gathered, split):
-        for r, c in others:
-            view = source.at[c] if split else source
-            remote(
-                view, gathered.at[r, c], n.f_send.at[index, 0], n.f_recv.at[index, r, c], (2 * chip + c, r)
-            ).wait_recv()
-
-    def spread(index, source, gathered):
-        @pl.when(core == parity)
-        def _():
-            gathered[row // 2, core] = source[...]
-
-        for k in range(R):
-            copy = spread_copy(index, source, gathered, k)
-            if k == 0:
-                pl.when(core != parity)(copy.start)
-            else:
-                copy.start()
-
-    def spread_copy(index, source, gathered, k):
-        device = (2 * chip + parity, lax.rem(row + k, R))
-        return remote(
-            source, gathered.at[row // 2, core], n.f_send.at[index, k], n.f_recv.at[index, row // 2, core], device
-        )
-
-    def spread_done(index, source, gathered):
-        for q in range(R // 2):
-            for c in range(2):
-                arriving = remote(
-                    source, gathered.at[q, c], n.f_send.at[index, 0], n.f_recv.at[index, q, c], sibling
-                )
-                pl.when((2 * q + core != row) | (core != c))(arriving.wait_recv)
-        for k in range(R):
-            copy = spread_copy(index, source, gathered, k)
-            if k == 0:
-                pl.when(core != parity)(copy.wait_send)
-            else:
-                copy.wait_send()
+        return remote(view, view, n.sr_send.at[d], n.sr_recv.at[d, h - 1], ring[d])
+
+    small_last = [None, None]
+
+    def small_put(d, h):
+        if small_last[d] is not None:
+            small_last[d].wait_send()
+        small_last[d] = small_send(d, h)
+        small_last[d].start()
+
+    small_put(0, 1)
+    small_put(1, 1)
 
     def small_step(h):
         small_recv(0, h).wait_recv()
         if h < N:
             small_recv(1, h).wait_recv()
-            start(small_send(0, h + 1))
+            small_put(0, h + 1)
             if h + 1 < N:
-                start(small_send(1, h + 1))
+                small_put(1, h + 1)
 
     def small_end():
         found = around_small[0]
@@ -804,21 +841,31 @@
         scatter(3, n.fs, n.ys, False)
 
     chain_s = [functools.partial(small_step, h) for h in range(1, N + 1)] + [small_end]
-    while chain_d or chain_x or chain_a or chain_u or chain_s:
-        advance(chain_d)
-        advance(chain_x)
-        advance(chain_a)
-        advance(chain_u)
-        advance(chain_s)
+    chains.update(s=chain_s)
+    work(last)
+    assert not any(chains.values())
     spread_done(0, n.fd, n.yd)
     collect(1, n.fu, n.yu, True)
+    collect(4, n.fe, n.ye, True)
     collect(3, n.fs, n.ys, False)
     spread_done(2, n.fa, n.ya)
     for copy in started:
         copy.wait_send()
-
-
-def finish_kernel(out, grad_x, yd, yu, ya, ys, *targets):
+    for copy in delivered:
+        copy.wait()
+    for flow in (flow_e, flow_d, flow_u, flow_x, flow_a):
+        flow.sent()
+    remote(
+        n.ap.at[:, 1 - parity, pl.ds(0, 3)], n.am.at[:, pl.ds(0, 3)], n.ya_send.at[0], n.ya_recv.at[0], mate
+    ).wait_send()
+    for copy in crossing:
+        copy.wait_send()
+    for copy in small_last:
+        if copy is not None:
+            copy.wait_send()
+
+
+def finish_kernel(out, grad_x, yd, ye, yu, ya, ys, *targets):
     (
         to_out,
         to_grad_x,
@@ -852,7 +899,9 @@
     to_grad_x[...] = grad_x[...]
     for c in range(2):
         width = yd.shape[-1]
-        to_down[:, width * c : width * (c + 1)] = over_rows(yd, c)
+        rows = yd.shape[2]
+        to_down[:rows, width * c : width * (c + 1)] = over_rows(ye, c)
+        to_down[rows:, width * c : width * (c + 1)] = over_rows(yd, c)
         for index, target in enumerate((to_query, to_key, to_value, to_o)):
             target[:, width * c : width * (c + 1)] = over_rows(ya, c, index)
         width = yu.shape[-1]
@@ -909,7 +958,7 @@
     heads = DH // HEAD
     keys = C * T
     wire = BF16 if CR % 32 == 0 else F32
-    wire_d = BF16 if CD % 32 == 0 else F32
+    wire_d = BF16 if CD % 64 == 0 else F32
     vmem = pl.BlockSpec(memory_space=pltpu.VMEM)
     hbm = pl.BlockSpec(memory_space=pl.ANY)
     operands = dict(
@@ -935,7 +984,8 @@
     results = dict(
         out=((F, D), BF16),
         grad_x=((F, D), F32),
-        yd=((R // 2, 2, CD // 2, DH), wire_d),
+        yd=((R // 2, 2, CD // 4, DH), wire_d),
+        ye=((R, 2, CD // 4, DH), wire_d),
         yu=((R, 2, CR // 2, FH // 2), wire),
         ya=((R // 2, 2, 4, CR // 2, DH), wire),
         ys=((R, 2, 8, D), F32),
@@ -955,6 +1005,8 @@
         grad_probs=pltpu.VMEM((T, heads * T), F32),
         probs=pltpu.VMEM((T, heads * T), BF16),
         grad_scores=pltpu.VMEM((T, heads * T), BF16),
+        out_low=pltpu.VMEM((F, D), BF16),
+        dh2=pltpu.VMEM((F, D), F32),
         vec=pltpu.VMEM((8 + FF // D, D), F32),
         top=pltpu.VMEM((heads // 2, 1, 2 * T), F32),
         tot=pltpu.VMEM((heads // 2, 1, 2 * T), F32),
@@ -970,18 +1022,23 @@
         xb=pltpu.VMEM((T, D), BF16),
         xbt=pltpu.VMEM((D, T), BF16),
         df=pltpu.VMEM((T, D), BF16),
+        da=pltpu.VMEM((T, D), BF16),
         act=pltpu.VMEM((T, FH), BF16),
-        acto=pltpu.VMEM((C // 2, 2, CD // 2, T), BF16),
-        att=pltpu.VMEM((2, C, CD // 2, T), BF16),
+        acto=pltpu.VMEM((2, C // 2, 2, CD // 4, T), BF16),
+        atf=pltpu.VMEM((C, 2, CD // 4, T), BF16),
+        att=pltpu.VMEM((2, C, CD // 4, T), BF16),
         xbm=pltpu.VMEM((T, D), BF16),
         xmt=pltpu.VMEM((D, T), BF16),
         dfm=pltpu.VMEM((T, DH), BF16),
         dum=pltpu.VMEM((T, FH // 2), BF16),
         slope=pltpu.VMEM((T, FH), F32),
         part=pltpu.VMEM((T, D), F32),
-        part_in=pltpu.VMEM((F, D), F32),
-        gd_sum=pltpu.VMEM((C, CD // 2, DH), BF16),
-        gd_in=pltpu.VMEM((2, N, CD // 2, DH), BF16),
+        part_in=pltpu.VMEM((2, F, D), BF16),
+        part_out=pltpu.VMEM((2, F, D), BF16),
+        gd_sum=pltpu.VMEM((C, CD // 4, DH), BF16),
+        gd_in=pltpu.VMEM((2, N, CD // 4, DH), BF16),
+        ge_sum=pltpu.VMEM((C, 2, CD // 4, DH), BF16),
+        ge_in=pltpu.VMEM((2, N, 2, CD // 4, DH), BF16),
         gu_sum=pltpu.VMEM((C, CR, FH // 2), BF16),
         gu_in=pltpu.VMEM((2, N, CR, FH // 2), BF16),
         ap=pltpu.VMEM((C, 2, 4, CR // 2, DH), BF16),
@@ -989,31 +1046,33 @@
         ga_in=pltpu.VMEM((2, N, 4, CR // 2, DH), BF16),
         ix_sum=pltpu.VMEM((C, F, D), BF16),
         ix_in=pltpu.VMEM((2, N, F, D), BF16),
-        fd=pltpu.VMEM((CD // 2, DH), wire_d),
+        fd=pltpu.VMEM((CD // 4, DH), wire_d),
+        fe=pltpu.VMEM((2, CD // 4, DH), wire_d),
         fu=pltpu.VMEM((2, CR // 2, FH // 2), wire),
         fa=pltpu.VMEM((4, CR // 2, DH), wire),
         small=pltpu.VMEM((2, 16, D), F32),
         small_ring=pltpu.VMEM((C, 8, D), F32),
         fs=pltpu.VMEM((8, D), F32),
         load_sem=dma((6,)),
-        g_send=dma((2, N, PIECES)),
+        g_send=dma((2, PIECES)),
         g_recv=dma((2, N, PIECES)),
-        s_send=dma((C,)),
+        s_send=dma((2,)),
         s_recv=dma((C,)),
-        m_send=dma((10,)),
-        m_recv=dma((10,)),
-        r_send=dma((4, 2, N)),
-        r_recv=dma((4, 2, N)),
+        m_send=dma((11,)),
+        m_recv=dma((11,)),
+        r_send=dma((5, 2)),
+        r_recv=dma((5, 2, N)),
+        out_sem=dma((7,)),
         y_send=dma((6,)),
         y_recv=dma((6,)),
-        ya_send=dma((C,)),
+        ya_send=dma((1,)),
         ya_recv=dma((C,)),
-        c_send=dma((C,)),
+        c_send=dma((2,)),
         c_recv=dma((C,)),
-        sr_send=dma((2, N)),
+        sr_send=dma((2,)),
         sr_recv=dma((2, N)),
-        f_send=dma((4, 2 * R - 1)),
-        f_recv=dma((4, R, 2)),
+        f_send=dma((5, 2 * R - 1)),
+        f_recv=dma((5, R, 2)),
     )
     if C <= 8:
         scratch.update(kt=pltpu.VMEM((DH, keys), BF16))
@@ -1022,7 +1081,7 @@
         functools.partial(layer_kernel, names, S, R),
         out_shape=[jax.ShapeDtypeStruct(shape, kind) for shape, kind in results.values()],
         in_specs=[spec for _, spec in operands.values()],
-        out_specs=[vmem] * len(results),
+        out_specs=[hbm] * len(results),
         scratch_shapes=list(scratch.values()),
         compiler_params=pltpu.CompilerParams(
             collective_id=0, has_side_effects=True, vmem_limit_bytes=62 * 1024 * 1024

time: 116 us -> 103 us (0.89)
  Pallas kernels: 115 us -> 102 us
    pallas_call x1, Pallas kernels: 112 us -> 99.1 us  [on_device(): pl.pallas_call(functools.partial(layer_kernel, names, S, R), out_shape=[j...]
where the time goes in v3:
time: 103 us
  Pallas kernels  102 us (99%)
    pallas_call x1, Pallas kernels, on_device(): pl.pallas_call(functools.partial(layer_kernel, names, S, R), out_shape=[j...  99.1 us
    pallas_call x1, Pallas kernels, on_device(): pl.pallas_call(finish_kernel, out_shape=[jax.ShapeDtypeStruct(shape, kind...  2.86 us

profile of v3, /device:TPU:0, one launch (start us, length us, event | category | flops | bytes accessed | tf_op | source)
XLA Modules:
  0.0 102.8 jit_solution(6208833417785382822)
XLA Ops:
  0.7 99.1 %layer.1 = (bf16[128,768]{1,0:T(8,128)(2,1)}, f32[128,768]{1,0:T(8,128)}, bf16[1,2,96,384]{3,2,1,0:T(8,128)(2,1)}, bf16[2,2,96,384]{3,2,1,0:T(8,128)(2,1)}, bf16...) custom-call(bf16[128,768]{1,0:T(8,128)(2,1)} %bitcast.4, ...), custom_call_target="tpu_custom_call" | custom-call | tf_op jit(solution)/shard_map/layer/pallas_call | solution.py:1080
  99.7 2.9 %finish.1 = (bf16[128,768]{1,0:T(8,128)(2,1)}, f32[128,768]{1,0:T(8,128)}, f32[48,768]{1,0:T(8,128)}, f32[48]{0:T(128)}, f32[48,768]{1,0:T(8,128)}, /*index=5*/f...) custom-call(bf16[128,768]{1,0:T(8,128)(2,1)} %get-tuple-element.41.o, ...), custom_call_target="tpu_custom_call" | custom-call | tf_op jit(solution)/shard_map/finish/pallas_call | solution.py:1094

commit v4 on v3

--- a/solution.py
+++ b/solution.py
@@ -108,32 +108,35 @@
     for device in partners:
         pl.semaphore_signal(barrier, inc=1, device_id=device, device_id_type=MESH)
 
+    xa = n.xa
+    own_rows = pl.multiple_of(core * F, F)
+    other_rows = pl.multiple_of((1 - core) * F, F)
     half_d = pl.multiple_of(core * DH, 128)
     half_f = pl.multiple_of(core * FH, 128)
     loads = []
     for source, target in (
+        (n.x, xa.at[pos, pl.ds(own_rows, F)]),
         (n.wq_hbm.at[:, pl.ds(half_d, DH)], n.wq),
         (n.wk_hbm.at[:, pl.ds(half_d, DH)], n.wkv.at[:, pl.ds(0, DH)]),
         (n.wv_hbm.at[:, pl.ds(half_d, DH)], n.wkv.at[:, pl.ds(DH, DH)]),
+        (n.lens_hbm, n.lens),
+        (n.bias_q, n.thin0),
+        (n.bias_v, n.thin1),
+        (n.bias_o, n.thin2),
+        (n.gain1, n.thin3),
+        (n.shift1, n.thin4),
+        (n.bias_d, n.thin5),
+        (n.gain2, n.thin6),
+        (n.shift2, n.thin7),
+        (n.bias_u, n.thin_u),
         (n.wo_hbm, n.wo),
         (n.wu_hbm.at[:, pl.ds(half_f, FH)], n.wu),
         (n.wd_hbm.at[pl.ds(half_f, FH)], n.wd),
+        (n.cot_hbm, n.cot),
     ):
         loads.append(pltpu.make_async_copy(source, target, n.load_sem.at[len(loads)]))
         loads[-1].start()
 
-    xa = n.xa
-    own_rows = pl.multiple_of(core * F, F)
-    other_rows = pl.multiple_of((1 - core) * F, F)
-    xa[pos, pl.ds(own_rows, F)] = n.x[...]
-    for index, vector in enumerate(
-        (n.bias_q, n.bias_v, n.bias_o, n.gain1, n.shift1, n.bias_d, n.gain2, n.shift2)
-    ):
-        n.vec[index : index + 1] = vector[...].astype(F32).reshape(1, D)
-    for index in range(FF // D):
-        n.vec[UP_BIAS + index : UP_BIAS + index + 1] = (
-            n.bias_u[D * index : D * (index + 1)].astype(F32).reshape(1, D)
-        )
     pl.semaphore_wait(barrier, len(partners))
 
     step_rows = F // PIECES
@@ -145,6 +148,11 @@
         view = hop_view(around((h - 1) * (2 * d - 1)), lax.rem(turn + d * (PIECES // 2), PIECES))
         return remote(view, view, n.g_send.at[d, turn], n.g_recv.at[d, h - 1, turn], ring[d])
 
+    def hop_first(d, turn):
+        first = lax.rem(turn + d * (PIECES // 2), PIECES)
+        src = n.x.at[pl.ds(first * step_rows, step_rows)]
+        return remote(src, hop_view(pos, first), n.g_send.at[d, turn], n.g_recv.at[d, 0, turn], ring[d])
+
     def hop_recv(d, h, turn):
         view = hop_view(around(h * (2 * d - 1)), lax.rem(turn + d * (PIECES // 2), PIECES))
         return remote(view, view, n.g_send.at[d, turn], n.g_recv.at[d, h - 1, turn], ring[d])
@@ -158,10 +166,10 @@
         return remote(view, view, n.s_send.at[0], n.s_recv.at[where], sibling)
 
     for turn in range(PIECES):
-        hop_send(0, 1, turn).start()
-        hop_send(1, 1, turn).start()
+        hop_first(0, turn).start()
+        hop_first(1, turn).start()
         if turn == 0:
-            share_send(pos).start()
+            remote(n.x, xa.at[pos, pl.ds(own_rows, F)], n.s_send.at[0], n.s_recv.at[pos], sibling).start()
 
     def gather_step(h, turn):
         for d in range(2):
@@ -191,6 +199,15 @@
     def gather_sent():
         share_send(pos, 0).wait_send()
         share_send(pos, 1).wait_send()
+
+    for load in loads[:14]:
+        load.wait()
+    for index, thin in enumerate((n.thin0, n.thin1, n.thin2, n.thin3, n.thin4, n.thin5, n.thin6, n.thin7)):
+        n.vec[index : index + 1] = thin[...].astype(F32).reshape(1, D)
+    for index in range(FF // D):
+        n.vec[UP_BIAS + index : UP_BIAS + index + 1] = (
+            n.thin_u[D * index : D * (index + 1)].astype(F32).reshape(1, D)
+        )
 
     ends = []
     total = 0
@@ -262,8 +279,6 @@
     small = n.small.at[core]
     small[...] = jnp.zeros(small.shape, F32)
 
-    for load in loads[:3]:
-        load.wait()
     share_recv(pos).wait_recv()
     queries = (nn(xa[pos], n.wq[...]) + n.vec[Q_BIAS : Q_BIAS + 1, pl.ds(half_d, DH)]).astype(BF16)
     head_masked(queries.astype(F32) * 0.125, n.qm)
@@ -305,9 +320,14 @@
     for j in range(heads):
         n.ot[of_head(j)] = n.ot[of_head(j)] / safe[j // 2][:, of_pair(j)]
 
+    swaps = []
+
     def swap(index, src, dst, landed):
-        send, recv = n.m_send.at[index], n.m_recv.at[index]
+        if len(swaps) >= 3:
+            sent(swaps[-3])
+        send, recv = n.m_send.at[len(swaps) % 3], n.m_recv.at[index]
         start(remote(src, dst, send, recv, sibling))
+        swaps.append(started[-1])
         return remote(src, landed, send, recv, sibling)
 
     def lend(index, src, dst, device, landed, recv_index=None):
@@ -331,7 +351,7 @@
     other_half = pl.ds(pl.multiple_of((1 - core) * DH, DH), DH)
     obt[own_half] = n.ot[...].astype(BF16)
     swapped = swap(0, obt.at[own_half], obt.at[own_half], obt.at[other_half])
-    loads[3].wait()
+    loads[14].wait()
     branch = nn(obt[own_half, pl.ds(own_rows, F)].T, n.wo[own_half])
     swapped.wait_recv()
 
@@ -339,7 +359,7 @@
         return n.vec[index : index + 1]
 
     branch = branch + nn(obt[other_half, pl.ds(own_rows, F)].T, n.wo[other_half]) + vec(OUT_BIAS)
-    first_normal, first_scale = norm_parts(n.x[...].astype(F32) + branch)
+    first_normal, first_scale = norm_parts(xa[pos, pl.ds(own_rows, F)].astype(F32) + branch)
     n.n1[...] = first_normal
     normed = first_normal * vec(GAIN1) + vec(SHIFT1)
     n.x1[...] = normed
@@ -348,7 +368,7 @@
     swapped = swap(1, xb.at[pl.ds(own_rows, F)], xb.at[pl.ds(own_rows, F)], xb.at[pl.ds(other_rows, F)])
     xbm = n.xbm
     lent_xb = lend(0, xb.at[pl.ds(own_rows, F)], xbm.at[pl.ds(own_rows, F)], mate, xbm.at[pl.ds(own_rows, F)])
-    loads[4].wait()
+    loads[15].wait()
 
     act, slope = n.act, n.slope
     acto, att = n.acto, n.att
@@ -379,7 +399,8 @@
     swapped_act = swap(2, acto.at[1, :, parity], att.at[0, own_ff], att.at[0, other_ff])
     n.atf[own_ff] = acto[0]
     att[0, own_ff] = acto[1, :, parity]
-    loads[5].wait()
+    loads[16].wait()
+    loads[17].wait()
     part = n.part
 
     def part_swap(index):
@@ -480,15 +501,18 @@
                 found = found + landed[...].astype(F32)
             return found
 
-    def add_lent(where):
+    def add_lent(first, lent, where):
         c = chip_at(where)
-        lent_chunk(c).wait_recv()
-        n.ap[c, parity] = (n.ap[c, parity].astype(F32) + n.am[c].astype(F32)).astype(BF16)
-
-    def lent_chunk(c):
-        return remote(
-            n.ap.at[c, 1 - parity, pl.ds(0, 3)], n.am.at[c, pl.ds(0, 3)], n.ya_send.at[0], n.ya_recv.at[c], mate
-        )
+        lent(c).wait_recv()
+        both = pl.ds(first, 2)
+        n.ap[c, parity, both] = (n.ap[c, parity, both].astype(F32) + n.am[c, both].astype(F32)).astype(BF16)
+
+    def lent_query(c):
+        return remote(n.ap.at[c, 1 - parity, 0], n.am.at[c, 0], n.yq_send.at[0], n.yq_recv.at[c], mate)
+
+    def lent_pair(c):
+        both = pl.ds(2, 2)
+        return remote(n.ap.at[c, 1 - parity, both], n.am.at[c, both], n.ya_send.at[0], n.ya_recv.at[c], mate)
 
     whole = slice(None)
     if CD % 128 == 0:
@@ -504,29 +528,41 @@
         [(whole, pl.ds(0, FH // 4)), (whole, pl.ds(FH // 4, FH // 4))],
     )
     flow_a = Flow(
-        2, lambda where: n.ap.at[chip_at(where), parity], n.ga_in, [pl.ds(0, 2), pl.ds(2, 2)], add_lent
+        2,
+        lambda where: n.ap.at[chip_at(where), parity, pl.ds(2, 2)],
+        n.ga_in,
+        [pl.ds(0, 1), pl.ds(1, 1)],
+        functools.partial(add_lent, 2, lent_pair),
+    )
+    flow_b = Flow(
+        5,
+        lambda where: n.ap.at[chip_at(where), parity, pl.ds(0, 2)],
+        n.gb_in,
+        [pl.ds(0, 1), pl.ds(1, 1)],
+        functools.partial(add_lent, 0, lent_query),
     )
     flow_x = Flow(3, lambda where: n.ix_sum.at[where], n.ix_in, [pl.ds(0, F // 2), pl.ds(F // 2, F // 2)])
 
+    scattered = []
+
     def scatter(index, source, gathered, split):
+        while scattered:
+            sent(scattered.pop())
         deliver(source.at[core] if split else source, gathered.at[row, core], 2 + index)
         for k, (r, c) in enumerate(others):
             view = source.at[c] if split else source
             start(
                 remote(
-                    view,
-                    gathered.at[row, core],
-                    n.f_send.at[index, k],
-                    n.f_recv.at[index, row, core],
-                    (2 * chip + c, r),
+                    view, gathered.at[row, core], n.f_send.at[k], n.f_recv.at[index, row, core], (2 * chip + c, r)
                 )
             )
+            scattered.append(started[-1])
 
     def collect(index, source, gathered, split):
         for r, c in others:
             view = source.at[c] if split else source
             remote(
-                view, gathered.at[r, c], n.f_send.at[index, 0], n.f_recv.at[index, r, c], (2 * chip + c, r)
+                view, gathered.at[r, c], n.f_send.at[0], n.f_recv.at[index, r, c], (2 * chip + c, r)
             ).wait_recv()
 
     def spread(index, source, gathered):
@@ -544,14 +580,14 @@
     def spread_copy(index, source, gathered, k):
         device = (2 * chip + parity, lax.rem(row + k, R))
         return remote(
-            source, gathered.at[row // 2, core], n.f_send.at[index, k], n.f_recv.at[index, row // 2, core], device
+            source, gathered.at[row // 2, core], n.h_send.at[index, k], n.f_recv.at[index, row // 2, core], device
         )
 
     def spread_done(index, source, gathered):
         for q in range(R // 2):
             for c in range(2):
                 arriving = remote(
-                    source, gathered.at[q, c], n.f_send.at[index, 0], n.f_recv.at[index, q, c], sibling
+                    source, gathered.at[q, c], n.h_send.at[index, 0], n.f_recv.at[index, q, c], sibling
                 )
                 pl.when((2 * q + core != row) | (core != c))(arriving.wait_recv)
         pl.when(core == parity)(spread_own(index, source, gathered).wait)
@@ -574,7 +610,7 @@
         found = flow_u.end()
         for c in range(2):
             n.fu[c] = found[CR // 2 * c : CR // 2 * (c + 1)].astype(n.fu.dtype)
-        scatter(1, n.fu, n.yu, True)
+        scatter(5, n.fu, n.yu, True)
 
     def input_step(distance):
         join(around(distance))
@@ -586,13 +622,13 @@
         n.dh2[...] = n.x1[...] + flow_x.end()
         deliver(n.dh2, n.grad_x, 1)
 
-    def attention_begin():
+    def query_begin():
         lent_out.wait_recv()
-        flow_a.begin()
-
-    def attention_end():
-        n.fa[...] = flow_a.end().astype(n.fa.dtype)
-        spread(2, n.fa, n.ya)
+        flow_b.begin()
+
+    def attention_end(flow, index, source, gathered):
+        source[...] = flow.end().astype(source.dtype)
+        spread(index, source, gathered)
 
     def chain(step, end):
         return [functools.partial(step, distance) for distance in range(N - 1, 0, -1)] + [end]
@@ -601,7 +637,8 @@
     chain_u = chain(flow_u.step, up_end)
     chain_e = chain(flow_e.step, first_end)
     chain_x = chain(input_step, input_end)
-    chain_a = [attention_begin] + chain(flow_a.step, attention_end)
+    chain_a = [flow_a.begin] + chain(flow_a.step, functools.partial(attention_end, flow_a, 2, n.fa, n.ya))
+    chain_b = [query_begin] + chain(flow_b.step, functools.partial(attention_end, flow_b, 1, n.fb, n.yb))
 
     def advance(one):
         one.pop(0)()
@@ -744,67 +781,8 @@
         n.dq[...] = grad_query
         return nt(grad_query, n.wq[...])
 
-    blocks = [N] + [side * d for d in range(N - 1, 0, -1) for side in (1, -1)] + [0]
-    if N == 4:
-        due = [""] * 8
-        due[0], due[1], due[3], due[4], due[5], due[6], due[7] = "mFD", "e", "x", "ed", "U", "x", "ed"
-        last = "uasuasuasduasxdsax"
-    else:
-        due = ["mFD", "e"] + ["ed"[b % 4 // 2] if b % 2 == 0 else "x" for b in range(2, 2 * N)]
-        due[4] += "U"
-        last = "eaxdus" * (N + 2)
-    chains = dict(e=chain_e, d=chain_d, u=chain_u, x=chain_x, a=chain_a, s=[])
-
-    def begin_input():
-        join(around(N))
-        flow_x.begin()
-
-    def begin_down():
-        grad_down()
-        flow_d.begin()
-
-    def begin_up():
-        nonlocal swapped_xbm, lent_out
-        swapped_xbm = forward_xb()
-        grad_attention([3], lambda rows: obt[rows], da[:, pl.ds(half_d, DH)])
-        lent_out = lend(5, n.ap.at[:, 1 - parity, 3], n.am.at[:, 3], mate, n.am.at[:, 3])
-        grad_up()
-        flow_u.begin()
-
-    def mate_hidden():
-        nonlocal swapped_actm
-        lent_act.wait_recv()
-        swapped_actm = swap(9, att.at[1, own_ff], att.at[1, own_ff], att.at[1, other_ff])
-
-    swapped_xbm = lent_out = swapped_actm = None
-    begins = dict(m=mate_hidden, F=begin_input, D=begin_down, U=begin_up)
-
-    def work(letters):
-        for letter in letters:
-            if letter in begins:
-                begins[letter]()
-            elif chains[letter]:
-                chains[letter].pop(0)()
-
-    for index, step in enumerate(blocks):
-        key_block(around(step), query_part if step == 0 else None)
-        turn_of_cross[0] = index
-        put_cross(around(step))
-        work(due[index])
-    small[Q_BIAS : Q_BIAS + 1, pl.ds(half_d, DH)] = jnp.sum(n.dq[...].astype(F32), axis=0, keepdims=True)
-    small[V_BIAS : V_BIAS + 1, pl.ds(half_d, DH)] = n.vsum[...]
-    small_swap = swap(7, small, small, n.small.at[1 - core])
-
-    grad_attention([0], lambda rows: n.xt[rows, key_rows(pos)], n.dq[...])
-    grad_attention([1, 2], lambda rows: n.xt[rows], n.kva[...])
-    for distance in range(N, -1, -1):
-        for where in [around(distance)] + ([around(-distance)] if 0 < distance < N else []):
-            lent_chunk(chip_at(where)).start()
-
-    small_swap.wait_recv()
     around_small = n.small_ring
     mine = pl.ds(pl.multiple_of(core * 8, 8), 8)
-    around_small[pos] = n.small[0, mine] + n.small[1, mine]
 
     def small_send(d, h):
         view = around_small.at[around(1 - h if d == 0 else h - 1)]
@@ -822,8 +800,6 @@
         small_last[d] = small_send(d, h)
         small_last[d].start()
 
-    small_put(0, 1)
-    small_put(1, 1)
 
     def small_step(h):
         small_recv(0, h).wait_recv()
@@ -841,23 +817,94 @@
         scatter(3, n.fs, n.ys, False)
 
     chain_s = [functools.partial(small_step, h) for h in range(1, N + 1)] + [small_end]
-    chains.update(s=chain_s)
+    blocks = [N] + [side * d for d in range(N - 1, 0, -1) for side in (1, -1)] + [0]
+    if N == 4:
+        due = [""] * 8
+        due[0], due[1], due[3], due[4], due[5], due[7] = "mF", "De", "dOx", "U", "e", "uSx"
+        last = "basubasduaebsduabsxdsabx"
+    else:
+        due = ["mFD", "e"] + ["ed"[b % 4 // 2] if b % 2 == 0 else "x" for b in range(2, 2 * N)]
+        due[4] += "OU"
+        due[2 * N - 1] += "S"
+        last = "ebaxdus" * (N + 2)
+    chains = dict(e=chain_e, d=chain_d, u=chain_u, x=chain_x, a=chain_a, b=chain_b, s=chain_s)
+
+    def begin_input():
+        join(around(N))
+        flow_x.begin()
+
+    def begin_down():
+        grad_down()
+        flow_d.begin()
+
+    def begin_up():
+        nonlocal swapped_xbm
+        swapped_xbm = forward_xb()
+        grad_up()
+        flow_u.begin()
+
+    def begin_out():
+        nonlocal lent_out
+        grad_attention([1], lambda rows: obt[rows], da[:, pl.ds(half_d, DH)])
+        lent_out = lend(5, n.ap.at[:, 1 - parity, 1], n.am.at[:, 1], mate, n.am.at[:, 1])
+
+    def begin_small():
+        small_swap.wait_recv()
+        around_small[pos] = n.small[0, mine] + n.small[1, mine]
+        small_put(0, 1)
+        small_put(1, 1)
+
+    def mate_hidden():
+        nonlocal swapped_actm
+        lent_act.wait_recv()
+        swapped_actm = swap(9, att.at[1, own_ff], att.at[1, own_ff], att.at[1, other_ff])
+
+    swapped_xbm = lent_out = swapped_actm = small_swap = None
+    begins = dict(m=mate_hidden, F=begin_input, D=begin_down, U=begin_up, O=begin_out, S=begin_small)
+
+    def work(letters):
+        for letter in letters:
+            if letter in begins:
+                begins[letter]()
+            elif chains[letter]:
+                chains[letter].pop(0)()
+
+    for index, step in enumerate(blocks):
+        key_block(around(step), query_part if step == 0 else None)
+        turn_of_cross[0] = index
+        put_cross(around(step))
+        if step == 0:
+            small[Q_BIAS : Q_BIAS + 1, pl.ds(half_d, DH)] = jnp.sum(n.dq[...].astype(F32), axis=0, keepdims=True)
+            small[V_BIAS : V_BIAS + 1, pl.ds(half_d, DH)] = n.vsum[...]
+            small_swap = swap(7, small, small, n.small.at[1 - core])
+        work(due[index])
+    grad_attention([0], lambda rows: n.xt[rows, key_rows(pos)], n.dq[...])
+    ordered = [around(d) for d in [N] + [side * d for d in range(N - 1, 0, -1) for side in (1, -1)] + [0]]
+    for where in ordered[:3]:
+        lent_query(chip_at(where)).start()
+    grad_attention([2, 3], lambda rows: n.xt[rows], n.kva[...])
+    for k, where in enumerate(ordered):
+        if k >= 3:
+            lent_query(chip_at(where)).start()
+        lent_pair(chip_at(where)).start()
+
     work(last)
     assert not any(chains.values())
     spread_done(0, n.fd, n.yd)
-    collect(1, n.fu, n.yu, True)
+    collect(5, n.fu, n.yu, True)
     collect(4, n.fe, n.ye, True)
     collect(3, n.fs, n.ys, False)
     spread_done(2, n.fa, n.ya)
+    spread_done(1, n.fb, n.yb)
     for copy in started:
         copy.wait_send()
     for copy in delivered:
         copy.wait()
-    for flow in (flow_e, flow_d, flow_u, flow_x, flow_a):
+    for flow in (flow_e, flow_d, flow_u, flow_x, flow_a, flow_b):
         flow.sent()
-    remote(
-        n.ap.at[:, 1 - parity, pl.ds(0, 3)], n.am.at[:, pl.ds(0, 3)], n.ya_send.at[0], n.ya_recv.at[0], mate
-    ).wait_send()
+    remote(n.ap.at[:, 1 - parity, 0], n.am.at[:, 0], n.yq_send.at[0], n.yq_recv.at[0], mate).wait_send()
+    both = pl.ds(2, 2)
+    remote(n.ap.at[:, 1 - parity, both], n.am.at[:, both], n.ya_send.at[0], n.ya_recv.at[0], mate).wait_send()
     for copy in crossing:
         copy.wait_send()
     for copy in small_last:
@@ -865,7 +912,7 @@
             copy.wait_send()
 
 
-def finish_kernel(out, grad_x, yd, ye, yu, ya, ys, *targets):
+def finish_kernel(out, grad_x, yd, ye, yu, ya, yb, ys, *targets):
     (
         to_out,
         to_grad_x,
@@ -902,8 +949,8 @@
         rows = yd.shape[2]
         to_down[:rows, width * c : width * (c + 1)] = over_rows(ye, c)
         to_down[rows:, width * c : width * (c + 1)] = over_rows(yd, c)
-        for index, target in enumerate((to_query, to_key, to_value, to_o)):
-            target[:, width * c : width * (c + 1)] = over_rows(ya, c, index)
+        for gathered, index, target in ((yb, 0, to_query), (yb, 1, to_o), (ya, 0, to_key), (ya, 1, to_value)):
+            target[:, width * c : width * (c + 1)] = over_rows(gathered, c, index)
         width = yu.shape[-1]
         for half in range(2):
             first = width * (2 * c + half)
@@ -962,18 +1009,18 @@
     vmem = pl.BlockSpec(memory_space=pltpu.VMEM)
     hbm = pl.BlockSpec(memory_space=pl.ANY)
     operands = dict(
-        x=(inputs[0], vmem),
-        cot=(cotangent[0], vmem),
-        lens=(clip_lengths, pl.BlockSpec(memory_space=pltpu.SMEM)),
-        bias_q=(query_bias, vmem),
-        bias_v=(value_bias, vmem),
-        bias_o=(out_bias, vmem),
-        gain1=(first_gain, vmem),
-        shift1=(first_shift, vmem),
-        bias_d=(down_bias, vmem),
-        gain2=(second_gain, vmem),
-        shift2=(second_shift, vmem),
-        bias_u=(up_bias, vmem),
+        x=(inputs[0], hbm),
+        cot_hbm=(cotangent[0], hbm),
+        lens_hbm=(clip_lengths, hbm),
+        bias_q=(query_bias, hbm),
+        bias_v=(value_bias, hbm),
+        bias_o=(out_bias, hbm),
+        gain1=(first_gain, hbm),
+        shift1=(first_shift, hbm),
+        bias_d=(down_bias, hbm),
+        gain2=(second_gain, hbm),
+        shift2=(second_shift, hbm),
+        bias_u=(up_bias, hbm),
         wq_hbm=(query_weight, hbm),
         wk_hbm=(key_weight, hbm),
         wv_hbm=(value_weight, hbm),
@@ -987,7 +1034,8 @@
         yd=((R // 2, 2, CD // 4, DH), wire_d),
         ye=((R, 2, CD // 4, DH), wire_d),
         yu=((R, 2, CR // 2, FH // 2), wire),
-        ya=((R // 2, 2, 4, CR // 2, DH), wire),
+        ya=((R // 2, 2, 2, CR // 2, DH), wire),
+        yb=((R // 2, 2, 2, CR // 2, DH), wire),
         ys=((R, 2, 8, D), F32),
     )
     dma = pltpu.SemaphoreType.DMA
@@ -1005,6 +1053,17 @@
         grad_probs=pltpu.VMEM((T, heads * T), F32),
         probs=pltpu.VMEM((T, heads * T), BF16),
         grad_scores=pltpu.VMEM((T, heads * T), BF16),
+        cot=pltpu.VMEM((F, D), BF16),
+        lens=pltpu.SMEM(clip_lengths.shape, jnp.int32),
+        thin0=pltpu.VMEM((D,), BF16),
+        thin1=pltpu.VMEM((D,), BF16),
+        thin2=pltpu.VMEM((D,), BF16),
+        thin3=pltpu.VMEM((D,), BF16),
+        thin4=pltpu.VMEM((D,), BF16),
+        thin5=pltpu.VMEM((D,), BF16),
+        thin6=pltpu.VMEM((D,), BF16),
+        thin7=pltpu.VMEM((D,), BF16),
+        thin_u=pltpu.VMEM((FF,), BF16),
         out_low=pltpu.VMEM((F, D), BF16),
         dh2=pltpu.VMEM((F, D), F32),
         vec=pltpu.VMEM((8 + FF // D, D), F32),
@@ -1043,54 +1102,62 @@
         gu_in=pltpu.VMEM((2, N, CR, FH // 2), BF16),
         ap=pltpu.VMEM((C, 2, 4, CR // 2, DH), BF16),
         am=pltpu.VMEM((C, 4, CR // 2, DH), BF16),
-        ga_in=pltpu.VMEM((2, N, 4, CR // 2, DH), BF16),
+        ga_in=pltpu.VMEM((2, N, 2, CR // 2, DH), BF16),
+        gb_in=pltpu.VMEM((2, N, 2, CR // 2, DH), BF16),
         ix_sum=pltpu.VMEM((C, F, D), BF16),
         ix_in=pltpu.VMEM((2, N, F, D), BF16),
         fd=pltpu.VMEM((CD // 4, DH), wire_d),
         fe=pltpu.VMEM((2, CD // 4, DH), wire_d),
         fu=pltpu.VMEM((2, CR // 2, FH // 2), wire),
-        fa=pltpu.VMEM((4, CR // 2, DH), wire),
+        fa=pltpu.VMEM((2, CR // 2, DH), wire),
+        fb=pltpu.VMEM((2, CR // 2, DH), wire),
         small=pltpu.VMEM((2, 16, D), F32),
         small_ring=pltpu.VMEM((C, 8, D), F32),
         fs=pltpu.VMEM((8, D), F32),
-        load_sem=dma((6,)),
+        load_sem=dma((18,)),
         g_send=dma((2, PIECES)),
         g_recv=dma((2, N, PIECES)),
         s_send=dma((2,)),
         s_recv=dma((C,)),
-        m_send=dma((11,)),
+        m_send=dma((3,)),
         m_recv=dma((11,)),
-        r_send=dma((5, 2)),
-        r_recv=dma((5, 2, N)),
-        out_sem=dma((7,)),
+        r_send=dma((6, 2)),
+        r_recv=dma((6, 2, N)),
+        out_sem=dma((8,)),
         y_send=dma((6,)),
         y_recv=dma((6,)),
         ya_send=dma((1,)),
         ya_recv=dma((C,)),
+        yq_send=dma((1,)),
+        yq_recv=dma((C,)),
         c_send=dma((2,)),
         c_recv=dma((C,)),
         sr_send=dma((2,)),
         sr_recv=dma((2, N)),
-        f_send=dma((5, 2 * R - 1)),
-        f_recv=dma((5, R, 2)),
+        f_send=dma((2 * R - 1,)),
+        h_send=dma((3, R)),
+        f_recv=dma((6, R, 2)),
     )
     if C <= 8:
         scratch.update(kt=pltpu.VMEM((DH, keys), BF16))
     names = [*operands, *results, *scratch]
+    roomy = C <= 8
     found = pl.pallas_call(
         functools.partial(layer_kernel, names, S, R),
-        out_shape=[jax.ShapeDtypeStruct(shape, kind) for shape, kind in results.values()],
+        out_shape=[(pltpu.VMEM if roomy else jax.ShapeDtypeStruct)(shape, kind) for shape, kind in results.values()],
         in_specs=[spec for _, spec in operands.values()],
         out_specs=[hbm] * len(results),
         scratch_shapes=list(scratch.values()),
         compiler_params=pltpu.CompilerParams(
-            collective_id=0, has_side_effects=True, vmem_limit_bytes=62 * 1024 * 1024
+            collective_id=0, has_side_effects=True, vmem_limit_bytes=(56 if roomy else 62) * 1024 * 1024
         ),
         name="layer",
     )(*[value for value, _ in operands.values()])
     shapes = [(F, D), (F, D), (D // S, D), (D // S,), (D // S, D), (D // S, D), (D // S,), (D // S, D)]
     shapes += [(D // S,)] * 3 + [(D // S, FF), (FF // S,), (FF // S, D)] + [(D // S,)] * 3
     kinds = [BF16] + [F32] * (len(shapes) - 1)
+    if roomy:
+        found = [pltpu.with_memory_space_constraint(one, pltpu.VMEM) for one in found]
     final = pl.pallas_call(
         finish_kernel,
         out_shape=[jax.ShapeDtypeStruct(shape, kind) for shape, kind in zip(shapes, kinds, strict=True)],

time: 103 us -> 100 us (0.971)
  Pallas kernels: 102 us -> 99.2 us
    pallas_call x1, Pallas kernels: 2.86 us -> 1.48 us  [on_device(): pl.pallas_call(finish_kernel, out_shape=[jax.ShapeDtypeStruct(shape, kind...]
    pallas_call x1, Pallas kernels: 99.1 us -> 97.7 us  [on_device(): pl.pallas_call(functools.partial(layer_kernel, names, S, R), out_shape=[(...]
where the time goes in v4:
time: 100 us
  Pallas kernels  99.2 us (99%)
    pallas_call x1, Pallas kernels, on_device(): pl.pallas_call(functools.partial(layer_kernel, names, S, R), out_shape=[(...  97.7 us

profile of v4, /device:TPU:0, one launch (start us, length us, event | category | flops | bytes accessed | tf_op | source)
XLA Modules:
  0.0 100.1 jit_solution(8858709920411190760)
XLA Ops:
  0.7 97.7 %layer.1 = (bf16[128,768]{1,0:T(8,128)(2,1)S(1)}, f32[128,768]{1,0:T(8,128)S(1)}, bf16[1,2,96,384]{3,2,1,0:T(8,128)(2,1)S(1)}, bf16[2,2,96,384]{3,2,1,0:T(8,128)...) custom-call(bf16[128,768]{1,0:T(8,128)(2,1)} %bitcast.4, ...), custom_call_target="tpu_custom_call" | custom-call | tf_op jit(solution)/shard_map/layer/pallas_call | solution.py:1145
  98.4 1.5 %finish.1 = (bf16[128,768]{1,0:T(8,128)(2,1)}, f32[128,768]{1,0:T(8,128)}, f32[48,768]{1,0:T(8,128)}, f32[48]{0:T(128)}, f32[48,768]{1,0:T(8,128)}, /*index=5*/f...) custom-call(bf16[128,768]{1,0:T(8,128)(2,1)S(1)} %get-tuple-element., ...), custom_call_target="tpu_custom_call" | custom-call | tf_op jit(solution)/shard_map/finish/pallas_call | solution.py:1161

commit v5 on v4

--- a/solution.py
+++ b/solution.py
@@ -223,8 +223,9 @@
 
     query_ids = ids(lax.broadcasted_iota(jnp.int32, (1, T), 1) + chip * T, -1)
 
-    def score_bias(where):
-        key_ids = ids(lax.broadcasted_iota(jnp.int32, (T, 1), 0) + chip_at(where) * T, -2)
+    def score_bias(where, first=0, size=None):
+        size = T if size is None else size
+        key_ids = ids(lax.broadcasted_iota(jnp.int32, (size, 1), 0) + (chip_at(where) * T + first), -2)
         found = jnp.where(key_ids == query_ids, 0.0, MASKED)
         return jnp.concatenate([found, found], axis=1)
 
@@ -245,19 +246,21 @@
     def key_rows(where):
         return pl.ds(pl.multiple_of(where * T, T), T)
 
-    def forward_block(where):
-        xk = xa[where]
+    def forward_block(where, first=0, size=None):
+        size = T if size is None else size
+        rows = pl.ds(pl.multiple_of(where * T + first, size), size)
+        xk = xa[where, pl.ds(first, size)]
         both = nn(xk, n.wkv[...])
         keys = both[:, :DH].astype(BF16)
         scores = [nt(keys[:, 2 * HEAD * p : 2 * HEAD * (p + 1)], n.qm[p]) for p in range(pairs)]
-        n.kva[key_rows(where), :DH] = keys
+        n.kva[rows, :DH] = keys
         if roomy:
-            n.kt[:, key_rows(where)] = keys.T
+            n.kt[:, rows] = keys.T
         values = (both[:, DH:] + n.vec[V_BIAS : V_BIAS + 1, pl.ds(half_d, DH)]).astype(BF16)
-        n.kva[key_rows(where), DH:] = values
+        n.kva[rows, DH:] = values
         values_t = values.T
-        n.xt[:, key_rows(where)] = xk.T
-        bias = score_bias(where)
+        n.xt[:, rows] = xk.T
+        bias = score_bias(where, first, size)
         weights, factors = [], []
         for p in range(pairs):
             st = scores[p] + bias
@@ -302,7 +305,7 @@
     lax.fori_loop(0, PIECES * (N - 1), forward_step, 0)
 
     def forward_last(step, carry):
-        where = around((N - 1) * (2 * step - 1) - lax.div(step, 2) * (2 * N - 3))
+        where = around((N - 1) * (2 * step - 1))
 
         @pl.when(step == 1)
         def _():
@@ -312,7 +315,17 @@
         forward_block(where)
         return carry
 
-    lax.fori_loop(0, 3, forward_last, 0)
+    lax.fori_loop(0, 2, forward_last, 0)
+
+    def forward_half(step, carry):
+        @pl.when(step == 1)
+        def _():
+            share_recv(around(N)).wait_recv()
+
+        forward_block(around(N), pl.multiple_of(own_rows + step * (other_rows - own_rows), F), F)
+        return carry
+
+    lax.fori_loop(0, 2, forward_half, 0)
 
     gather_sent()
     safe = jnp.where(n.tot[...] > 0.5, n.tot[...], 1.0)
@@ -397,8 +410,6 @@
     lent_act = lend(1, acto.at[1, :, 1 - parity], att.at[1, own_ff], mate, att.at[1, own_ff])
     swapped_first = swap(10, acto.at[0], n.atf.at[own_ff], n.atf.at[other_ff])
     swapped_act = swap(2, acto.at[1, :, parity], att.at[0, own_ff], att.at[0, other_ff])
-    n.atf[own_ff] = acto[0]
-    att[0, own_ff] = acto[1, :, parity]
     loads[16].wait()
     loads[17].wait()
     part = n.part
@@ -409,6 +420,8 @@
 
     part[...] = nn(act[...], n.wd[...])
     part_arrives = part_swap(0)
+    n.atf[own_ff] = acto[0]
+    att[0, own_ff] = acto[1, :, parity]
     n.xbt[...] = xb[...].T
     upstream = n.cot[...].astype(F32)
     small[SHIFT2 : SHIFT2 + 1] = jnp.sum(upstream, axis=0, keepdims=True)
@@ -417,7 +430,6 @@
         n.x1[...] + part[pl.ds(own_rows, F)] + n.part_in[0].astype(F32) + vec(DOWN_BIAS)
     )
     n.out_low[...] = (second_normal * vec(GAIN2) + vec(SHIFT2)).astype(BF16)
-    deliver(n.out_low, n.out, 0)
     residual = norm_back(upstream * vec(GAIN2), second_normal, second_scale)
     n.dh2[...] = residual
     low = residual.astype(BF16)
@@ -643,6 +655,46 @@
     def advance(one):
         one.pop(0)()
 
+    def wide(p, first=0):
+        return slice(first + 2 * HEAD * p, first + 2 * HEAD * (p + 1))
+
+    def long(p):
+        return slice(2 * T * p, 2 * T * (p + 1))
+
+    def find_probs(where):
+        rows, bias = key_rows(where), score_bias(where)
+        for p in range(pairs):
+            n.slope[:, long(p)] = nt(n.kva[rows, wide(p)], n.qm[p])
+        for p in range(pairs):
+            probs = jnp.exp(n.slope[:, long(p)] + bias - n.lse[p])
+            n.slope[:, long(p)] = probs
+            n.probs[:, long(p)] = probs.astype(BF16)
+
+    def backward_block(where, ready):
+        rows = key_rows(where)
+        bias = None if ready else score_bias(where)
+        keys_t = n.kt[:, rows] if roomy else n.kva[rows, :DH].T
+
+        for p in range(pairs):
+            if not ready:
+                n.slope[:, long(p)] = nt(n.kva[rows, wide(p)], n.qm[p])
+            n.grad_probs[:, long(p)] = nt(n.kva[rows, wide(p, DH)], n.dm[p])
+        for p in range(pairs):
+            if ready:
+                probs = n.slope[:, long(p)]
+            else:
+                probs = jnp.exp(n.slope[:, long(p)] + bias - n.lse[p])
+                n.probs[:, long(p)] = probs.astype(BF16)
+            n.grad_scores[:, long(p)] = (probs * (n.grad_probs[:, long(p)] - n.delta[p])).astype(BF16)
+        for p in range(pairs):
+            low = nn(n.probs[:, long(p)], n.dm[p]).astype(BF16)
+            n.kva[rows, wide(p, DH)] = low
+            n.kva[rows, wide(p)] = nn(n.grad_scores[:, long(p)], n.qm[p]).astype(BF16)
+            n.vsum[:, wide(p)] += jnp.sum(low.astype(F32), axis=0, keepdims=True)
+        for j in range(heads):
+            n.dqt[of_head(j)] += nn(keys_t[of_head(j)], n.grad_scores[:, T * j : T * (j + 1)])
+        return nt(n.kva[rows], n.wkv[...])
+
     swapped_first.wait_recv()
     for t in range(C // 2):
         two = slice(2 * t, 2 * t + 2)
@@ -661,6 +713,7 @@
     part[...] = nt(du[...], n.wu[...])
     part_arrives = part_swap(1)
 
+    find_probs(around(N))
     part_arrives.wait_recv()
     grad_normed = n.dh2[...] + part[pl.ds(own_rows, F)] + n.part_in[1].astype(F32)
     normal = n.n1[...]
@@ -673,9 +726,9 @@
     da[pl.ds(own_rows, F)] = low
     swapped = swap(6, da.at[pl.ds(own_rows, F)], da.at[pl.ds(own_rows, F)], da.at[pl.ds(other_rows, F)])
     small[OUT_BIAS : OUT_BIAS + 1] = jnp.sum(low.astype(F32), axis=0, keepdims=True)
+    swapped.wait_recv()
+
     advance(chain_e)
-    swapped.wait_recv()
-
     grad_mixed = nt(da[...], n.wo[own_half]).astype(BF16).astype(F32)
     head_masked(grad_mixed, n.dm)
     grad_mixed_t = grad_mixed.T
@@ -723,33 +776,6 @@
     n.dqt[...] = jnp.zeros(n.dqt.shape, F32)
     n.vsum[...] = jnp.zeros(n.vsum.shape, F32)
 
-    def backward_block(where):
-        rows = key_rows(where)
-        bias = score_bias(where)
-        keys_t = n.kt[:, rows] if roomy else n.kva[rows, :DH].T
-
-        def wide(p, first=0):
-            return slice(first + 2 * HEAD * p, first + 2 * HEAD * (p + 1))
-
-        def long(p):
-            return slice(2 * T * p, 2 * T * (p + 1))
-
-        for p in range(pairs):
-            n.slope[:, long(p)] = nt(n.kva[rows, wide(p)], n.qm[p])
-            n.grad_probs[:, long(p)] = nt(n.kva[rows, wide(p, DH)], n.dm[p])
-        for p in range(pairs):
-            probs = jnp.exp(n.slope[:, long(p)] + bias - n.lse[p])
-            n.probs[:, long(p)] = probs.astype(BF16)
-            n.grad_scores[:, long(p)] = (probs * (n.grad_probs[:, long(p)] - n.delta[p])).astype(BF16)
-        for p in range(pairs):
-            low = nn(n.probs[:, long(p)], n.dm[p]).astype(BF16)
-            n.kva[rows, wide(p, DH)] = low
-            n.kva[rows, wide(p)] = nn(n.grad_scores[:, long(p)], n.qm[p]).astype(BF16)
-            n.vsum[:, wide(p)] += jnp.sum(low.astype(F32), axis=0, keepdims=True)
-        for j in range(heads):
-            n.dqt[of_head(j)] += nn(keys_t[of_head(j)], n.grad_scores[:, T * j : T * (j + 1)])
-        return nt(n.kva[rows], n.wkv[...])
-
     crossing, turn_of_cross = [], [0]
 
     def put_cross(where):
@@ -762,13 +788,14 @@
         send, recv = n.c_send.at[turn_of_cross[0] % 2], n.c_recv.at[where]
         return remote(xa.at[where, pl.ds(0, F)], xa.at[where, pl.ds(F, F)], send, recv, sibling)
 
-    def key_block(where, extra=None):
-        found = backward_block(where)
+    def key_block(where, extra=None, ready=False):
+        found = backward_block(where, ready)
         if extra is not None:
             found = found + extra()
-        part[...] = found
-        xa[where, pl.ds(0, F)] = part[pl.ds(other_rows, F)].astype(BF16)
-        n.ix_sum[where] = part[pl.ds(own_rows, F)].astype(BF16)
+        found = found.astype(BF16)
+        first, second = found[:F], found[F:]
+        xa[where, pl.ds(0, F)] = jnp.where(core == 0, second, first)
+        n.ix_sum[where] = jnp.where(core == 0, first, second)
 
     def join(where):
         cross(where).wait_recv()
@@ -810,23 +837,23 @@
                 small_put(1, h + 1)
 
     def small_end():
-        found = around_small[0]
+        found = around_small[0].astype(F32)
         for where in range(1, C):
-            found = found + around_small[where]
-        n.fs[...] = found
+            found = found + around_small[where].astype(F32)
+        n.fs[:, :DH] = found[:8]
+        n.fs[:, DH:] = found[8:]
         scatter(3, n.fs, n.ys, False)
 
     chain_s = [functools.partial(small_step, h) for h in range(1, N + 1)] + [small_end]
     blocks = [N] + [side * d for d in range(N - 1, 0, -1) for side in (1, -1)] + [0]
     if N == 4:
         due = [""] * 8
-        due[0], due[1], due[3], due[4], due[5], due[7] = "mF", "De", "dOx", "U", "e", "uSx"
-        last = "basubasduaebsduabsxdsabx"
+        due[0], due[1], due[3], due[4], due[5], due[7] = "mfF", "De", "dOx", "U", "e", "u"
+        middle, last = "Sx", "basubasduaebsduabsxdsabx"
     else:
-        due = ["mFD", "e"] + ["ed"[b % 4 // 2] if b % 2 == 0 else "x" for b in range(2, 2 * N)]
+        due = ["mfFD", "e"] + ["ed"[b % 4 // 2] if b % 2 == 0 else "x" for b in range(2, 2 * N)]
         due[4] += "OU"
-        due[2 * N - 1] += "S"
-        last = "ebaxdus" * (N + 2)
+        middle, last = "S", "ebaxdus" * (N + 2)
     chains = dict(e=chain_e, d=chain_d, u=chain_u, x=chain_x, a=chain_a, b=chain_b, s=chain_s)
 
     def begin_input():
@@ -837,9 +864,11 @@
         grad_down()
         flow_d.begin()
 
-    def begin_up():
+    def begin_forward():
         nonlocal swapped_xbm
         swapped_xbm = forward_xb()
+
+    def begin_up():
         grad_up()
         flow_u.begin()
 
@@ -850,7 +879,8 @@
 
     def begin_small():
         small_swap.wait_recv()
-        around_small[pos] = n.small[0, mine] + n.small[1, mine]
+        both = (n.small[0, mine] + n.small[1, mine]).astype(BF16)
+        around_small[pos] = jnp.concatenate([both[:, :DH], both[:, DH:]])
         small_put(0, 1)
         small_put(1, 1)
 
@@ -860,7 +890,7 @@
         swapped_actm = swap(9, att.at[1, own_ff], att.at[1, own_ff], att.at[1, other_ff])
 
     swapped_xbm = lent_out = swapped_actm = small_swap = None
-    begins = dict(m=mate_hidden, F=begin_input, D=begin_down, U=begin_up, O=begin_out, S=begin_small)
+    begins = dict(m=mate_hidden, F=begin_input, D=begin_down, U=begin_up, O=begin_out, S=begin_small, f=begin_forward)
 
     def work(letters):
         for letter in letters:
@@ -870,7 +900,7 @@
                 chains[letter].pop(0)()
 
     for index, step in enumerate(blocks):
-        key_block(around(step), query_part if step == 0 else None)
+        key_block(around(step), query_part if step == 0 else None, index == 0)
         turn_of_cross[0] = index
         put_cross(around(step))
         if step == 0:
@@ -882,6 +912,8 @@
     ordered = [around(d) for d in [N] + [side * d for d in range(N - 1, 0, -1) for side in (1, -1)] + [0]]
     for where in ordered[:3]:
         lent_query(chip_at(where)).start()
+    deliver(n.out_low, n.out, 0)
+    work(middle)
     grad_attention([2, 3], lambda rows: n.xt[rows], n.kva[...])
     for k, where in enumerate(ordered):
         if k >= 3:
@@ -1112,7 +1144,7 @@
         fa=pltpu.VMEM((2, CR // 2, DH), wire),
         fb=pltpu.VMEM((2, CR // 2, DH), wire),
         small=pltpu.VMEM((2, 16, D), F32),
-        small_ring=pltpu.VMEM((C, 8, D), F32),
+        small_ring=pltpu.VMEM((C, 16, DH), BF16),
         fs=pltpu.VMEM((8, D), F32),
         load_sem=dma((18,)),
         g_send=dma((2, PIECES)),

time: 100 us -> 98.4 us (0.984)
  Pallas kernels: 99.2 us -> 97.4 us
    pallas_call x1, Pallas kernels: 97.7 us -> 95.9 us  [on_device(): pl.pallas_call(functools.partial(layer_kernel, names, S, R), out_shape=[(...]
where the time goes in v5:
time: 98.4 us; the launch traced here: 98.2 us
  Pallas kernels  97.4 us (99%)
    pallas_call x1, Pallas kernels, on_device(): pl.pallas_call(functools.partial(layer_kernel, names, S, R), out_shape=[(...  95.9 us

profile of v5, /device:TPU:0, one launch (start us, length us, event | category | flops | bytes accessed | tf_op | source)
XLA Modules:
  0.0 98.2 jit_solution(6145827960206196326)
XLA Ops:
  0.7 95.9 %layer.1 = (bf16[128,768]{1,0:T(8,128)(2,1)S(1)}, f32[128,768]{1,0:T(8,128)S(1)}, bf16[1,2,96,384]{3,2,1,0:T(8,128)(2,1)S(1)}, bf16[2,2,96,384]{3,2,1,0:T(8,128)...) custom-call(bf16[128,768]{1,0:T(8,128)(2,1)} %bitcast.4, ...), custom_call_target="tpu_custom_call" | custom-call | tf_op jit(solution)/shard_map/layer/pallas_call | solution.py:1177
  96.6 1.5 %finish.1 = (bf16[128,768]{1,0:T(8,128)(2,1)}, f32[128,768]{1,0:T(8,128)}, f32[48,768]{1,0:T(8,128)}, f32[48]{0:T(128)}, f32[48,768]{1,0:T(8,128)}, /*index=5*/f...) custom-call(bf16[128,768]{1,0:T(8,128)(2,1)S(1)} %get-tuple-element., ...), custom_call_target="tpu_custom_call" | custom-call | tf_op jit(solution)/shard_map/finish/pallas_call | solution.py:1193

commit v6 on v5

--- a/solution.py
+++ b/solution.py
@@ -113,6 +113,8 @@
     other_rows = pl.multiple_of((1 - core) * F, F)
     half_d = pl.multiple_of(core * DH, 128)
     half_f = pl.multiple_of(core * FH, 128)
+    other_f = pl.multiple_of((1 - core) * FH, 128)
+    own_slot = 1 if roomy else 0
     loads = []
     for source, target in (
         (n.x, xa.at[pos, pl.ds(own_rows, F)]),
@@ -130,12 +132,15 @@
         (n.shift2, n.thin7),
         (n.bias_u, n.thin_u),
         (n.wo_hbm, n.wo),
-        (n.wu_hbm.at[:, pl.ds(half_f, FH)], n.wu),
-        (n.wd_hbm.at[pl.ds(half_f, FH)], n.wd),
+        (n.wu_hbm.at[:, pl.ds(other_f, FH)], n.wu.at[0]),
+        (n.wd_hbm.at[pl.ds(other_f, FH)], n.wd.at[0]),
         (n.cot_hbm, n.cot),
+        (n.wu_hbm.at[:, pl.ds(half_f, FH)], n.wu.at[own_slot]),
+        (n.wd_hbm.at[pl.ds(half_f, FH)], n.wd.at[own_slot]),
     ):
         loads.append(pltpu.make_async_copy(source, target, n.load_sem.at[len(loads)]))
-        loads[-1].start()
+        if roomy or len(loads) <= 18:
+            loads[-1].start()
 
     pl.semaphore_wait(barrier, len(partners))
 
@@ -378,56 +383,67 @@
     n.x1[...] = normed
     xb = n.xb
     xb[pl.ds(own_rows, F)] = normed.astype(BF16)
-    swapped = swap(1, xb.at[pl.ds(own_rows, F)], xb.at[pl.ds(own_rows, F)], xb.at[pl.ds(other_rows, F)])
+    swapped_xb = swap(1, xb.at[pl.ds(own_rows, F)], xb.at[pl.ds(own_rows, F)], xb.at[pl.ds(other_rows, F)])
     xbm = n.xbm
     lent_xb = lend(0, xb.at[pl.ds(own_rows, F)], xbm.at[pl.ds(own_rows, F)], mate, xbm.at[pl.ds(own_rows, F)])
-    loads[15].wait()
-
     act, slope = n.act, n.slope
     acto, att = n.acto, n.att
     du = act
 
-    def up_rows(rows):
+    def up_half(i):
+        half = 1 - core if i == 0 else core
+        rows = slice(F * i, F * (i + 1))
         for t in range(FH // D):
             cols = slice(D * t, D * (t + 1))
-            bias = n.vec[pl.ds(UP_BIAS + core * (FH // D) + t, 1)]
-            value, tangent = gelu_parts(nn(xb[rows], n.wu[:, cols]) + bias)
+            bias = n.vec[pl.ds(UP_BIAS + half * (FH // D) + t, 1)]
+            hidden = nn(xb[pl.ds(own_rows, F)], n.wu[own_slot * i, :, cols]) + bias
+            value, tangent = gelu_parts(hidden)
             low = value.astype(BF16)
             act[rows, cols] = low
             turned = low.T
             for c in range(D // CD):
-                for half in range(2):
-                    for side in range(2):
-                        first = CD * c + CD // 2 * half + CD // 4 * side
-                        acto[side, D // CD * t + c, half, :, rows] = turned[first : first + CD // 4]
-            slope[rows, cols] = tangent
-
-    up_rows(pl.ds(own_rows, F))
-    swapped.wait_recv()
-    up_rows(pl.ds(other_rows, F))
-    own_ff = pl.ds(core * (C // 2), C // 2)
-    other_ff = pl.ds((1 - core) * (C // 2), C // 2)
-    lent_act = lend(1, acto.at[1, :, 1 - parity], att.at[1, own_ff], mate, att.at[1, own_ff])
-    swapped_first = swap(10, acto.at[0], n.atf.at[own_ff], n.atf.at[other_ff])
-    swapped_act = swap(2, acto.at[1, :, parity], att.at[0, own_ff], att.at[0, other_ff])
+                for side in range(2):
+                    for q in range(2):
+                        first = CD * c + CD // 2 * q + CD // 4 * side
+                        acto[side, half * (C // 2) + D // CD * t + c, q] = turned[first : first + CD // 4]
+            if i == 0:
+                n.slope_out[:, cols] = tangent.astype(BF16)
+            else:
+                slope[pl.ds(own_rows, F), cols] = tangent
+
+    loads[15].wait()
+    if roomy:
+        loads[18].wait()
+    up_half(0)
+    if not roomy:
+        loads[18].start()
+        loads[18].wait()
+    up_half(1)
+    own_cols, other_cols = pl.ds(own_rows, F), pl.ds(other_rows, F)
+    lent_act = lend(1, acto.at[1, :, 1 - parity], att.at[1, :, :, own_cols], mate, att.at[1, :, :, own_cols])
+    swapped_slope = swap(3, n.slope_out, n.slope_in, n.slope_in)
+    swapped_first = swap(10, acto.at[0], n.atf.at[:, :, :, own_cols], n.atf.at[:, :, :, other_cols])
+    swapped_act = swap(2, acto.at[1, :, parity], att.at[0, :, :, own_cols], att.at[0, :, :, other_cols])
     loads[16].wait()
     loads[17].wait()
+    if roomy:
+        loads[19].wait()
     part = n.part
 
-    def part_swap(index):
-        n.part_out[index] = part[pl.ds(other_rows, F)].astype(BF16)
-        return swap(3 + 2 * index, n.part_out.at[index], n.part_in.at[index], n.part_in.at[index])
-
-    part[...] = nn(act[...], n.wd[...])
-    part_arrives = part_swap(0)
-    n.atf[own_ff] = acto[0]
-    att[0, own_ff] = acto[1, :, parity]
-    n.xbt[...] = xb[...].T
+    def part_swap():
+        n.part_out[...] = part[pl.ds(other_rows, F)].astype(BF16)
+        return swap(5, n.part_out, n.part_in, n.part_in)
+
+    fed = nn(act[:F], n.wd[0])
+    if not roomy:
+        part[:F] = fed
+        loads[19].start()
+        loads[19].wait()
+        fed = part[:F]
+    fed = fed + nn(act[F:], n.wd[own_slot])
     upstream = n.cot[...].astype(F32)
-    small[SHIFT2 : SHIFT2 + 1] = jnp.sum(upstream, axis=0, keepdims=True)
-    part_arrives.wait_recv()
     second_normal, second_scale = norm_parts(
-        n.x1[...] + part[pl.ds(own_rows, F)] + n.part_in[0].astype(F32) + vec(DOWN_BIAS)
+        n.x1[...] + fed + vec(DOWN_BIAS)
     )
     n.out_low[...] = (second_normal * vec(GAIN2) + vec(SHIFT2)).astype(BF16)
     residual = norm_back(upstream * vec(GAIN2), second_normal, second_scale)
@@ -457,8 +473,15 @@
                 (2 * chip + c, mate_row),
             )
         )
+    small[SHIFT2 : SHIFT2 + 1] = jnp.sum(upstream, axis=0, keepdims=True)
     small[GAIN2 : GAIN2 + 1] = jnp.sum(upstream * second_normal, axis=0, keepdims=True)
     small[DOWN_BIAS : DOWN_BIAS + 1] = jnp.sum(low.astype(F32), axis=0, keepdims=True)
+    n.atf[:, :, :, own_cols] = acto[0]
+    att[0, :, :, own_cols] = acto[1, :, parity]
+    swapped_xb.wait_recv()
+    n.xbt[...] = xb[...].T
+    swapped_slope.wait_recv()
+    slope[pl.ds(other_rows, F)] = n.slope_in[...].astype(F32)
     swapped.wait_recv()
 
     class Flow:
@@ -703,19 +726,19 @@
     flow_e.begin()
     for t in range(FH // D):
         cols = slice(D * t, D * (t + 1))
-        low = (nt(df[...], n.wd[cols, :]) * slope[:, cols]).astype(BF16)
+        low = (nt(df[...], n.wd[own_slot, cols, :]) * slope[:, cols]).astype(BF16)
         du[:, cols] = low
         small[pl.ds(UP_BIAS + core * (FH // D) + t, 1)] = jnp.sum(low.astype(F32), axis=0, keepdims=True)
 
     quarter = pl.multiple_of(parity * (FH // 2), FH // 2)
     other_quarter = pl.multiple_of((1 - parity) * (FH // 2), FH // 2)
     lent_du = lend(4, du.at[:, pl.ds(other_quarter, FH // 2)], n.dum, mate, n.dum)
-    part[...] = nt(du[...], n.wu[...])
-    part_arrives = part_swap(1)
+    part[...] = nt(du[...], n.wu[own_slot])
+    part_arrives = part_swap()
 
     find_probs(around(N))
     part_arrives.wait_recv()
-    grad_normed = n.dh2[...] + part[pl.ds(own_rows, F)] + n.part_in[1].astype(F32)
+    grad_normed = n.dh2[...] + part[pl.ds(own_rows, F)] + n.part_in[...].astype(F32)
     normal = n.n1[...]
     small[GAIN1 : GAIN1 + 1] = jnp.sum(grad_normed * normal, axis=0, keepdims=True)
     small[SHIFT1 : SHIFT1 + 1] = jnp.sum(grad_normed, axis=0, keepdims=True)
@@ -848,7 +871,7 @@
     blocks = [N] + [side * d for d in range(N - 1, 0, -1) for side in (1, -1)] + [0]
     if N == 4:
         due = [""] * 8
-        due[0], due[1], due[3], due[4], due[5], due[7] = "mfF", "De", "dOx", "U", "e", "u"
+        due[0], due[1], due[3], due[4], due[5], due[7] = "mfF", "De", "dx", "UO", "e", "u"
         middle, last = "Sx", "basubasduaebsduabsxdsabx"
     else:
         due = ["mfFD", "e"] + ["ed"[b % 4 // 2] if b % 2 == 0 else "x" for b in range(2, 2 * N)]
@@ -887,7 +910,9 @@
     def mate_hidden():
         nonlocal swapped_actm
         lent_act.wait_recv()
-        swapped_actm = swap(9, att.at[1, own_ff], att.at[1, own_ff], att.at[1, other_ff])
+        swapped_actm = swap(
+            9, att.at[1, :, :, own_cols], att.at[1, :, :, own_cols], att.at[1, :, :, other_cols]
+        )
 
     swapped_xbm = lent_out = swapped_actm = small_swap = None
     begins = dict(m=mate_hidden, F=begin_input, D=begin_down, U=begin_up, O=begin_out, S=begin_small, f=begin_forward)
@@ -1070,13 +1095,14 @@
         yb=((R // 2, 2, 2, CR // 2, DH), wire),
         ys=((R, 2, 8, D), F32),
     )
+    roomy = C <= 8
     dma = pltpu.SemaphoreType.DMA
     scratch = dict(
         wq=pltpu.VMEM((D, DH), BF16),
         wkv=pltpu.VMEM((D, D), BF16),
         wo=pltpu.VMEM((D, D), BF16),
-        wu=pltpu.VMEM((D, FH), BF16),
-        wd=pltpu.VMEM((FH, D), BF16),
+        wu=pltpu.VMEM((2 if roomy else 1, D, FH), BF16),
+        wd=pltpu.VMEM((2 if roomy else 1, FH, D), BF16),
         xa=pltpu.VMEM((C, T, D), BF16),
         xt=pltpu.VMEM((D, keys), BF16),
         kva=pltpu.VMEM((keys, D), BF16),
@@ -1115,17 +1141,19 @@
         df=pltpu.VMEM((T, D), BF16),
         da=pltpu.VMEM((T, D), BF16),
         act=pltpu.VMEM((T, FH), BF16),
-        acto=pltpu.VMEM((2, C // 2, 2, CD // 4, T), BF16),
+        acto=pltpu.VMEM((2, C, 2, CD // 4, F), BF16),
         atf=pltpu.VMEM((C, 2, CD // 4, T), BF16),
         att=pltpu.VMEM((2, C, CD // 4, T), BF16),
+        slope_out=pltpu.VMEM((F, FH), BF16),
+        slope_in=pltpu.VMEM((F, FH), BF16),
         xbm=pltpu.VMEM((T, D), BF16),
         xmt=pltpu.VMEM((D, T), BF16),
         dfm=pltpu.VMEM((T, DH), BF16),
         dum=pltpu.VMEM((T, FH // 2), BF16),
         slope=pltpu.VMEM((T, FH), F32),
         part=pltpu.VMEM((T, D), F32),
-        part_in=pltpu.VMEM((2, F, D), BF16),
-        part_out=pltpu.VMEM((2, F, D), BF16),
+        part_in=pltpu.VMEM((F, D), BF16),
+        part_out=pltpu.VMEM((F, D), BF16),
         gd_sum=pltpu.VMEM((C, CD // 4, DH), BF16),
         gd_in=pltpu.VMEM((2, N, CD // 4, DH), BF16),
         ge_sum=pltpu.VMEM((C, 2, CD // 4, DH), BF16),
@@ -1146,7 +1174,7 @@
         small=pltpu.VMEM((2, 16, D), F32),
         small_ring=pltpu.VMEM((C, 16, DH), BF16),
         fs=pltpu.VMEM((8, D), F32),
-        load_sem=dma((18,)),
+        load_sem=dma((20,)),
         g_send=dma((2, PIECES)),
         g_recv=dma((2, N, PIECES)),
         s_send=dma((2,)),
@@ -1170,10 +1198,9 @@
         h_send=dma((3, R)),
         f_recv=dma((6, R, 2)),
     )
-    if C <= 8:
+    if roomy:
         scratch.update(kt=pltpu.VMEM((DH, keys), BF16))
     names = [*operands, *results, *scratch]
-    roomy = C <= 8
     found = pl.pallas_call(
         functools.partial(layer_kernel, names, S, R),
         out_shape=[(pltpu.VMEM if roomy else jax.ShapeDtypeStruct)(shape, kind) for shape, kind in results.values()],

time: 98.4 us -> 97.1 us (0.987)
  Pallas kernels: 97.4 us -> 96 us
    pallas_call x1, Pallas kernels: 95.9 us -> 94.5 us  [on_device(): pl.pallas_call(functools.partial(layer_kernel, names, S, R), out_shape=[(...]
where the time goes in v6:
time: 97.1 us; the launch traced here: 96.8 us
  Pallas kernels  96 us (99%)
    pallas_call x1, Pallas kernels, on_device(): pl.pallas_call(functools.partial(layer_kernel, names, S, R), out_shape=[(...  94.5 us

profile of v6, /device:TPU:0, one launch (start us, length us, event | category | flops | bytes accessed | tf_op | source)
XLA Modules:
  0.0 96.8 jit_solution(3916026789183924117)
XLA Ops:
  0.7 94.5 %layer.1 = (bf16[128,768]{1,0:T(8,128)(2,1)S(1)}, f32[128,768]{1,0:T(8,128)S(1)}, bf16[1,2,96,384]{3,2,1,0:T(8,128)(2,1)S(1)}, bf16[2,2,96,384]{3,2,1,0:T(8,128)...) custom-call(bf16[128,768]{1,0:T(8,128)(2,1)} %bitcast.4, ...), custom_call_target="tpu_custom_call" | custom-call | tf_op jit(solution)/shard_map/layer/pallas_call | solution.py:1204
  95.2 1.5 %finish.1 = (bf16[128,768]{1,0:T(8,128)(2,1)}, f32[128,768]{1,0:T(8,128)}, f32[48,768]{1,0:T(8,128)}, f32[48]{0:T(128)}, f32[48,768]{1,0:T(8,128)}, /*index=5*/f...) custom-call(bf16[128,768]{1,0:T(8,128)(2,1)S(1)} %get-tuple-element., ...), custom_call_target="tpu_custom_call" | custom-call | tf_op jit(solution)/shard_map/finish/pallas_call | solution.py:1220

commit v7 on v6

--- a/solution.py
+++ b/solution.py
@@ -871,7 +871,7 @@
     blocks = [N] + [side * d for d in range(N - 1, 0, -1) for side in (1, -1)] + [0]
     if N == 4:
         due = [""] * 8
-        due[0], due[1], due[3], due[4], due[5], due[7] = "mfF", "De", "dx", "UO", "e", "u"
+        due[0], due[1], due[3], due[4], due[5], due[7] = "mfF", "De", "xd", "UO", "e", "u"
         middle, last = "Sx", "basubasduaebsduabsxdsabx"
     else:
         due = ["mfFD", "e"] + ["ed"[b % 4 // 2] if b % 2 == 0 else "x" for b in range(2, 2 * N)]

time: 97.1 us -> 97.8 us (level)
  no operation moved by 1% of the time
where the time goes in v7:
time: 97.8 us; the launch traced here: 97.6 us
  Pallas kernels  96.8 us (99%)
    pallas_call x1, Pallas kernels, on_device(): pl.pallas_call(functools.partial(layer_kernel, names, S, R), out_shape=[(...  95.3 us

profile of v7, /device:TPU:0, one launch (start us, length us, event | category | flops | bytes accessed | tf_op | source)
XLA Modules:
  0.0 97.6 jit_solution(15309231090269203231)
XLA Ops:
  0.7 95.3 %layer.1 = (bf16[128,768]{1,0:T(8,128)(2,1)S(1)}, f32[128,768]{1,0:T(8,128)S(1)}, bf16[1,2,96,384]{3,2,1,0:T(8,128)(2,1)S(1)}, bf16[2,2,96,384]{3,2,1,0:T(8,128)...) custom-call(bf16[128,768]{1,0:T(8,128)(2,1)} %bitcast.4, ...), custom_call_target="tpu_custom_call" | custom-call | tf_op jit(solution)/shard_map/layer/pallas_call | solution.py:1204
  96.0 1.5 %finish.1 = (bf16[128,768]{1,0:T(8,128)(2,1)}, f32[128,768]{1,0:T(8,128)}, f32[48,768]{1,0:T(8,128)}, f32[48]{0:T(128)}, f32[48,768]{1,0:T(8,128)}, /*index=5*/f...) custom-call(bf16[128,768]{1,0:T(8,128)(2,1)S(1)} %get-tuple-element., ...), custom_call_target="tpu_custom_call" | custom-call | tf_op jit(solution)/shard_map/finish/pallas_call | solution.py:1220
